TPU v7x, 32 devices: a whole 2x2x4 slice. The times are simulated.
32 devices in a mesh: section: 4 (over y, x), dp: 8 (over z, core).
Axes of the slice: x: 2, y: 2, z: 4, core: 2. Of those that a mesh axis runs over, the one named last changes fastest.
Arguments:
- hidden_in: bfloat16 [128, 32, 768], P(('section', 'dp')), may hold values from -6 to 6
- lengths: int32 [128], P(('section', 'dp')), may hold values from 8 to 32, as said below
- labels: int32 [128], P(('section', 'dp')), may hold values from 0 to 31, as said below
- chosen: int32 [128, 32, 32], P(('section', 'dp')), may hold values from 0 to 4095, as said below
- slab_main: bfloat16 [4, 768, 3072], P('section'), may hold values from -1 to 1, as said below
- slab_side: bfloat16 [4, 768, 3072], P('section'), may hold values from -1 to 1, as said below
- section_gains: float32 [4, 768], P('section'), may hold values from 0.5 to 1.5
- rel_bias: float32 [32, 12], replicated, may hold values from -3 to 3
- final_gain: float32 [768], replicated, may hold values from 0.5 to 1.5
- out_proj: bfloat16 [768, 128], replicated, may hold values from -0.01953125 to 0.01953125
- doc_vectors: bfloat16 [4096, 128], P('dp'), may hold values from -3 to 3
Outputs:
- out_vectors: bfloat16 [128, 32, 128], P(('section', 'dp'))
- query_loss: float32 [128], P(('section', 'dp'))
- input_grad: float32 [128, 32, 768], P(('section', 'dp'))
- grad_main: float32 [4, 768, 3072], P('section', 'dp')
- grad_side: float32 [4, 768, 3072], P('section', 'dp')
- grad_gains: float32 [4, 768], P('section', 'dp')
- grad_bias: float32 [32, 12], replicated
- grad_final_gain: float32 [768], replicated
- grad_proj: float32 [768, 128], replicated
Inputs may be any that keep to these rules, and one draw needn't show every extreme that they name: `lengths`: a query's slots at positions of at least its length are padding; its keys there are masked and its tokens there do not enter its loss. Number of the positive document of each query, among 32 documents of 128 tokens; document t holds rows t * 128 to t * 128 + 127 of doc_vectors, and index o of dp holds documents o * 4 to o * 4 + 3. Within one block of 4 queries the labels are distinct, and at most 1 of them lie on one index of dp, exactly 1 on some. `chosen`: rows of doc_vectors retrieved for each query token; every one lies in a document named by labels in the same block of 4 queries. `slab_main`: weights of order 768 ** -0.5 or smaller. `slab_side`: weights of order 768 ** -0.5 or smaller.
All inputs are finite; a program needn't handle non-finite values.
Results may differ from a plain program's by a relative error of at most 0.025.
Values may be sent and summed in bfloat16 or wider, within the bound.
A program may use at most 704 MiB of HBM per device.

v0:
```python
import jax
import jax.numpy as jnp
import numpy as np
from jax import lax
from jax.sharding import PartitionSpec as P

H = 12
DH = 64
DOC_LEN = 128


EPS_NORM = 1e-06
MASK_FILL = -1000000000.0
HIGHEST = lax.Precision.HIGHEST


def from_behind(value, axis, steps):
    count = lax.axis_size(axis)
    initial, last = (max(0, -steps), min(count, count - steps))
    return lax.ppermute(value, axis, [(source, source + steps) for source in range(initial, last)])


def spread(block, axis, owner):
    block = jnp.where(lax.axis_index(axis) == owner, block, jnp.zeros_like(block))
    return lax.psum(block, axis)


def as_sent(value):
    return jax.tree.map(lambda a: a.astype(jnp.bfloat16) if a.dtype == jnp.float32 else a, value)


def bucket_onehot(query_len):
    places = np.arange(query_len)
    relative = places[None, :] - places[:, None]
    distance = np.abs(relative)
    signed_part = np.where(relative > 0, 16, 0)
    far_bucket = 8 + np.floor(np.log(np.maximum(distance, 1) / 8.0) / np.log(16.0) * 8.0).astype(
        np.int64
    )
    far_bucket = np.minimum(far_bucket, 15)
    buckets = signed_part + np.where(distance < 8, distance, far_bucket)
    return (buckets[:, :, None] == np.arange(32)[None, None, :]).astype(np.float32)


def rms_scale(values, gain_vec):
    return (
        values * lax.rsqrt(jnp.mean(values * values, axis=-1, keepdims=True) + EPS_NORM) * gain_vec
    )


def unit_rows(projected):
    return projected * lax.rsqrt(jnp.sum(projected * projected, axis=-1, keepdims=True) + EPS_NORM)


def gated_units(gate_vals, up_vals):
    return jax.nn.gelu(gate_vals, approximate=True) * up_vals


def contract_rows(left_mat, right_mat):
    return lax.dot_general(
        left_mat, right_mat, (((0,), (0,)), ((), ())), preferred_element_type=jnp.float32
    )


def contract_cols(left_mat, right_mat):
    return lax.dot_general(
        left_mat, right_mat, (((1,), (1,)), ((), ())), preferred_element_type=jnp.float32
    )


def loss_from_scores(similarity, hit_table, lens_now):
    query_len = similarity.shape[1]
    imputed = jnp.mean(similarity, axis=-1)
    token_mass = jnp.exp(imputed)[..., None] + jnp.einsum(
        "blk,blkc->blc", jnp.exp(similarity), hit_table, precision=HIGHEST
    )
    token_scores = jnp.log(token_mass)
    live_slots = (jnp.arange(query_len)[None, :] < lens_now[:, None]).astype(jnp.float32)
    doc_scores = jnp.sum(live_slots[:, :, None] * token_scores, axis=1) / lens_now[:, None].astype(
        jnp.float32
    )
    maximum_score = jnp.max(doc_scores, axis=-1, keepdims=True)
    log_total = maximum_score[:, 0] + jnp.log(jnp.sum(jnp.exp(doc_scores - maximum_score), axis=-1))
    return log_total - jnp.diagonal(doc_scores)


def per_device(
    hidden_in,
    lengths,
    labels,
    chosen,
    slab_main,
    slab_side,
    section_gains,
    rel_bias,
    final_gain,
    out_proj,
    doc_vectors,
):
    sections = lax.axis_size("section")
    section_now = lax.axis_index("section")
    is_attention = section_now % 2 == 0
    is_first = section_now == 0
    is_last = section_now == sections - 1
    batch_size, query_len, model_width = hidden_in.shape
    row_count = batch_size * query_len
    retrieved = chosen.shape[2]
    vector_width = out_proj.shape[1]
    head_width = H * DH
    weight_main = slab_main[0]
    weight_side = slab_side[0]
    section_gain = section_gains[0]
    slab_width = weight_main.shape[1]
    all_hidden, all_lengths = (
        lax.all_gather(hidden_in, "section", axis=0, tiled=True),
        lax.all_gather(lengths, "section", axis=0, tiled=True),
    )
    weight_lent = from_behind(weight_side, "section", 1)
    onehot = jnp.asarray(bucket_onehot(query_len))
    small_bias = jnp.einsum("ijc,ch->hij", onehot, rel_bias, precision=HIGHEST)
    position_bias = jnp.tile(small_bias, (1, batch_size, batch_size))
    places = jnp.arange(row_count)
    owner_query = places // query_len
    within_query = places % query_len
    same_query = owner_query[:, None] == owner_query[None, :]

    def key_mask(lens_now):
        live_keys = within_query < jnp.repeat(lens_now, query_len)
        return same_query & live_keys[None, :]

    flat_chosen = chosen.reshape(row_count * retrieved)
    shard_rows = lax.all_gather(doc_vectors, "dp", axis=0, tiled=True)
    inside = (flat_chosen >= 0) & (flat_chosen < shard_rows.shape[0])
    picked = jnp.take(shard_rows, jnp.clip(flat_chosen, 0, shard_rows.shape[0] - 1), axis=0)
    doc_rows = jnp.where(
        inside[:, None], picked, jnp.zeros((row_count * retrieved, vector_width), jnp.bfloat16)
    )
    zero_slab = jnp.zeros((model_width, slab_width), jnp.float32)
    zero_width = jnp.zeros((model_width,), jnp.float32)
    zero_table = jnp.zeros(rel_bias.shape, jnp.float32)
    zero_proj = jnp.zeros((model_width, vector_width), jnp.float32)
    zero_states = jnp.zeros((row_count, model_width), jnp.float32)
    zero_units = jnp.zeros((row_count, vector_width), jnp.bfloat16)

    def attention_core(states, lens_now):
        normed_low = rms_scale(states, section_gain).astype(jnp.bfloat16)
        projected = jnp.dot(
            normed_low, weight_main[:, : 3 * head_width], preferred_element_type=jnp.float32
        ).astype(jnp.bfloat16)
        query_part = projected[:, :head_width].reshape(row_count, H, DH)
        key_part = projected[:, head_width : 2 * head_width].reshape(row_count, H, DH)
        value_part = projected[:, 2 * head_width :].reshape(row_count, H, DH)
        raw_scores = jnp.einsum(
            "ihd,jhd->hij", query_part, key_part, preferred_element_type=jnp.float32
        )
        scores = jnp.where(key_mask(lens_now)[None], raw_scores + position_bias, MASK_FILL)
        maximum_score = jnp.max(scores, axis=-1, keepdims=True)
        exp_scores = jnp.exp(scores - maximum_score)
        soft_weights = exp_scores / jnp.sum(exp_scores, axis=-1, keepdims=True)
        soft_low = soft_weights.astype(jnp.bfloat16)
        context = (
            jnp.einsum("hij,jhd->ihd", soft_low, value_part, preferred_element_type=jnp.float32)
            .reshape(row_count, head_width)
            .astype(jnp.bfloat16)
        )
        outputs = states + contract_cols(context, weight_main[:, 3 * head_width :])
        return (
            outputs,
            (normed_low, query_part, key_part, value_part, soft_weights, soft_low, context),
        )

    def ffn_core(states):
        normed_low = rms_scale(states, section_gain).astype(jnp.bfloat16)
        gate_vals = jnp.dot(normed_low, weight_main, preferred_element_type=jnp.float32)
        up_vals = jnp.dot(normed_low, weight_lent, preferred_element_type=jnp.float32)
        hidden_low = gated_units(gate_vals, up_vals).astype(jnp.bfloat16)
        outputs = states + contract_cols(hidden_low, weight_side)
        return (outputs, (normed_low, gate_vals, up_vals, hidden_low))

    def final_core(states):
        normed_final = rms_scale(states, final_gain).astype(jnp.bfloat16)
        projected = jnp.dot(normed_final, out_proj, preferred_element_type=jnp.float32)
        return (unit_rows(projected).astype(jnp.bfloat16), (normed_final, projected))

    def spare_forward(states, lens_now):
        return (zero_states, zero_units)

    def attention_forward(states, lens_now):
        return (attention_core(states, lens_now)[0], zero_units)

    def ffn_forward(states, lens_now):
        return (ffn_core(states)[0], zero_units)

    def last_forward(states, lens_now):
        outputs = ffn_core(states)[0]
        return (outputs, final_core(outputs)[0])

    kept_inputs = jnp.zeros((sections, row_count, model_width), jnp.bfloat16)
    finals = jnp.zeros((sections, row_count, vector_width), jnp.bfloat16)
    incoming = jnp.zeros((row_count, model_width), jnp.bfloat16)
    tick_count = 2 * sections - 1
    for tick_index in range(tick_count):
        micro_index = tick_index - section_now
        is_valid = (micro_index >= 0) & (micro_index < sections)
        slot_index = jnp.clip(micro_index, 0, sections - 1)
        first_micro = min(tick_index, sections - 1)
        first_rows = all_hidden[first_micro * batch_size : (first_micro + 1) * batch_size].reshape(
            row_count, model_width
        )
        section_input = jnp.where(is_first, first_rows, incoming)
        lens_now = lax.dynamic_slice_in_dim(all_lengths, slot_index * batch_size, batch_size, 0)
        previous = lax.dynamic_index_in_dim(kept_inputs, slot_index, 0, keepdims=False)
        kept_inputs = lax.dynamic_update_index_in_dim(
            kept_inputs, jnp.where(is_valid, section_input, previous), slot_index, 0
        )
        branch = jnp.where(
            is_valid, jnp.where(is_attention, 1, jnp.where(is_last, 3, 2)), 0
        ).astype(jnp.int32)
        outputs, unit_values = lax.switch(
            branch,
            [spare_forward, attention_forward, ffn_forward, last_forward],
            section_input.astype(jnp.float32),
            lens_now,
        )
        previous_units = lax.dynamic_index_in_dim(finals, slot_index, 0, keepdims=False)
        finals = lax.dynamic_update_index_in_dim(
            finals, jnp.where(is_valid & is_last, unit_values, previous_units), slot_index, 0
        )
        if tick_index + 1 < tick_count:
            incoming = from_behind(outputs.astype(jnp.bfloat16), "section", 1)
    every_final = spread(finals, "section", sections - 1)
    my_units = lax.dynamic_index_in_dim(every_final, section_now, 0, keepdims=False)
    row_vectors = doc_rows.reshape(row_count, retrieved, vector_width)
    similarity = jnp.einsum("ikc,ic->ik", row_vectors, my_units, preferred_element_type=jnp.float32)
    hit_table = ((chosen // DOC_LEN)[..., None] == labels[None, None, None, :]).astype(jnp.float32)

    def block_loss(similarity_block):
        return loss_from_scores(similarity_block, hit_table, lengths)

    losses, loss_pull = jax.vjp(block_loss, similarity.reshape(batch_size, query_len, retrieved))
    similarity_grad = loss_pull(jnp.ones_like(losses))[0].reshape(row_count, retrieved)
    unit_grad_local = jnp.einsum(
        "ik,ikc->ic", similarity_grad, row_vectors.astype(jnp.float32), precision=HIGHEST
    )
    unit_grads = lax.all_gather(
        unit_grad_local.astype(jnp.bfloat16), "section", axis=0, tiled=True
    ).astype(unit_grad_local.dtype)

    def ffn_grads(states, saved_parts, grad_out):
        normed_low, gate_vals, up_vals, hidden_low = saved_parts
        grad_low = grad_out.astype(jnp.bfloat16)
        d_side = contract_rows(grad_low, hidden_low)
        d_hidden = jnp.dot(grad_low, weight_side, preferred_element_type=jnp.float32)
        d_gate, d_up = jax.vjp(gated_units, gate_vals, up_vals)[1](d_hidden)
        gate_low = d_gate.astype(jnp.bfloat16)
        up_low = d_up.astype(jnp.bfloat16)
        d_main = contract_rows(normed_low, gate_low)
        d_lent = contract_rows(normed_low, up_low)
        d_normed = contract_cols(gate_low, weight_main) + contract_cols(up_low, weight_lent)
        d_states, d_gain = jax.vjp(rms_scale, states, section_gain)[1](d_normed)
        return (grad_out + d_states, d_main, d_side, d_lent, d_gain, zero_table)

    def spare_backward(states, lens_now, grad_in, unit_grad):
        return (
            zero_states,
            zero_slab,
            zero_slab,
            zero_slab,
            zero_width,
            zero_table,
            zero_width,
            zero_proj,
        )

    def attention_backward(states, lens_now, grad_in, unit_grad):
        outputs, saved_parts = attention_core(states, lens_now)
        normed_low, query_part, key_part, value_part, soft_weights, soft_low, context = saved_parts
        grad_low = grad_in.astype(jnp.bfloat16)
        d_out_weight = contract_rows(grad_low, context)
        d_context = (
            jnp.dot(grad_low, weight_main[:, 3 * head_width :], preferred_element_type=jnp.float32)
            .astype(jnp.bfloat16)
            .reshape(row_count, H, DH)
        )
        d_soft = jnp.einsum(
            "ihd,jhd->hij", d_context, value_part, preferred_element_type=jnp.float32
        )
        d_value = jnp.einsum(
            "hij,ihd->jhd", soft_low, d_context, preferred_element_type=jnp.float32
        )
        d_scores = soft_weights * (d_soft - jnp.sum(soft_weights * d_soft, axis=-1, keepdims=True))
        folded = jnp.sum(
            d_scores.reshape(H, batch_size, query_len, batch_size, query_len), axis=(1, 3)
        )
        d_table = jnp.einsum("hij,ijc->ch", folded, onehot, precision=HIGHEST)
        d_scores_low = d_scores.astype(jnp.bfloat16)
        d_query = jnp.einsum(
            "hij,jhd->ihd", d_scores_low, key_part, preferred_element_type=jnp.float32
        )
        d_key = jnp.einsum(
            "hij,ihd->jhd", d_scores_low, query_part, preferred_element_type=jnp.float32
        )
        d_projected = jnp.concatenate(
            [
                d_query.reshape(row_count, head_width),
                d_key.reshape(row_count, head_width),
                d_value.reshape(row_count, head_width),
            ],
            axis=1,
        ).astype(jnp.bfloat16)
        d_in_weight = contract_rows(normed_low, d_projected)
        d_normed = contract_cols(d_projected, weight_main[:, : 3 * head_width])
        d_states, d_gain = jax.vjp(rms_scale, states, section_gain)[1](d_normed)
        d_main = jnp.concatenate([d_in_weight, d_out_weight], axis=1)
        return (
            grad_in + d_states,
            d_main,
            zero_slab,
            zero_slab,
            d_gain,
            d_table,
            zero_width,
            zero_proj,
        )

    def ffn_backward(states, lens_now, grad_in, unit_grad):
        outputs, saved_parts = ffn_core(states)
        return ffn_grads(states, saved_parts, grad_in) + (zero_width, zero_proj)

    def last_backward(states, lens_now, grad_in, unit_grad):
        outputs, saved_parts = ffn_core(states)
        unit_values, final_saved = final_core(outputs)
        normed_final, projected = final_saved
        d_projected = jax.vjp(unit_rows, projected)[1](unit_grad)[0].astype(jnp.bfloat16)
        d_proj = contract_rows(normed_final, d_projected)
        d_normed = contract_cols(d_projected, out_proj)
        d_outputs, d_fgain = jax.vjp(rms_scale, outputs, final_gain)[1](d_normed)
        return ffn_grads(states, saved_parts, d_outputs) + (d_fgain, d_proj)

    running_grads = (zero_slab, zero_slab, zero_slab, zero_width, zero_table, zero_width, zero_proj)
    input_grads = jnp.zeros((sections, row_count, model_width), jnp.float32)
    grad_incoming = zero_states
    for tick_index in range(tick_count):
        micro_index = tick_index - (sections - 1 - section_now)
        is_valid = (micro_index >= 0) & (micro_index < sections)
        slot_index = jnp.clip(micro_index, 0, sections - 1)
        section_input = lax.dynamic_index_in_dim(kept_inputs, slot_index, 0, keepdims=False).astype(
            jnp.float32
        )
        lens_now = lax.dynamic_slice_in_dim(all_lengths, slot_index * batch_size, batch_size, 0)
        unit_grad = lax.dynamic_slice_in_dim(unit_grads, slot_index * row_count, row_count, 0)
        branch = jnp.where(
            is_valid, jnp.where(is_attention, 1, jnp.where(is_last, 3, 2)), 0
        ).astype(jnp.int32)
        results = lax.switch(
            branch,
            [spare_backward, attention_backward, ffn_backward, last_backward],
            section_input,
            lens_now,
            grad_incoming,
            unit_grad,
        )
        running_grads = tuple(
            (running + addend for running, addend in zip(running_grads, results[1:]))
        )
        previous = lax.dynamic_index_in_dim(input_grads, slot_index, 0, keepdims=False)
        input_grads = lax.dynamic_update_index_in_dim(
            input_grads, jnp.where(is_valid & is_first, results[0], previous), slot_index, 0
        )
        if tick_index + 1 < tick_count:
            grad_incoming = from_behind(as_sent(results[0]), "section", -1)
    accum_main, accum_side, accum_lent, accum_gain, accum_table, accum_fgain, accum_proj = (
        running_grads
    )
    lent_full = jax.tree.map(
        lambda part, own: part.astype(own.dtype),
        from_behind(as_sent(accum_lent), "section", -1),
        accum_lent,
    )
    main_part, side_total, gain_part = (
        lax.psum_scatter(accum_main, "dp", scatter_dimension=0, tiled=True),
        lax.psum_scatter(
            jnp.where(is_attention, lent_full, accum_side), "dp", scatter_dimension=0, tiled=True
        ),
        lax.psum_scatter(accum_gain, "dp", scatter_dimension=0, tiled=True),
    )
    table_sum, fgain_sum, proj_sum = lax.psum(
        (accum_table, accum_fgain, accum_proj), ("section", "dp")
    )
    exchanged = lax.all_to_all(
        input_grads.astype(jnp.bfloat16), "section", split_axis=0, concat_axis=0, tiled=True
    ).astype(input_grads.dtype)
    return (
        my_units.reshape(batch_size, query_len, vector_width),
        losses,
        exchanged[0].reshape(batch_size, query_len, model_width),
        main_part[None],
        side_total[None],
        gain_part[None],
        table_sum,
        fgain_sum,
        proj_sum,
    )


def solution(mesh):
    in_specs = (
        P(("section", "dp"), None, None),
        P(("section", "dp")),
        P(("section", "dp")),
        P(("section", "dp"), None, None),
        P("section", None, None),
        P("section", None, None),
        P("section", None),
        P(),
        P(),
        P(),
        P("dp", None),
    )
    out_specs = (
        P(("section", "dp"), None, None),
        P(("section", "dp")),
        P(("section", "dp"), None, None),
        P("section", "dp", None),
        P("section", "dp", None),
        P("section", "dp"),
        P(),
        P(),
        P(),
    )
    return jax.shard_map(
        per_device, mesh=mesh, in_specs=in_specs, out_specs=out_specs, check_vma=False
    )
```

profile of v0, /device:TPU:16, one launch (start us, length us, event | category | flops | bytes accessed | tf_op | source)
XLA Modules:
  0.0 1167.7 jit_solution(3128955425197521259)
XLA Ops:
  17.1 106.2 %all_gather.12 = bf16[16,32,768]{2,1,0:T(8,128)(2,1)S(1)} all-gather(bf16[4,32,768]{2,1,0:T(8,128)(2,1)} %param.68), channel_id=1, replica_groups=mesh['section'=4,'dp'=8] {'section'}, dimensions={0}, use_global_device_ids=true | all-gather | bytes 983040 | tf_op jit(solution)/shard_map/all_gather | solution.py:115
  143.1 15.8 %gather_fusion = bf16[4096,128]{1,0:T(8,128)(2,1)} fusion(bf16[4096,128]{1,0:T(8,128)(2,1)} %all-gather.2.cloned.1.call-done, s32[4096]{0:T(1024)S(1)} %broadcast_clamp_fusion.1), kind=kCustom, calls=%fused_computation | custom fusion | bytes 2113536 | tf_op jit(solution)/shard_map/jit(_take)/gather | solution.py:134
  158.9 20.3 %conditional.14 = (f32[128,768]{1,0:T(8,128)}, bf16[128,128]{1,0:T(8,128)(2,1)S(1)}) conditional(s32[]{:T(128)} %clamp.55, () %tuple.308, (f32[128,768]{1,0:T(8,128)S(1)}, f32[1,768]{1,0:T(1,128)S(1)}, bf16[768,3072]{1,0:T(8,128)(2,1)}, s32[]{:T(128)}, s32[16]{0:T(128)S(1)}, /*index=5*/s32[128]{0:T(128)S(1)}, ...), branch_computations={%region_0.1_spmd, %region_1.5_spmd, %region_5.7_spmd, %region_7.11... | conditional | flops 1842479360 | bytes 19715604 | solution.py:219
  185.5 11.0 conditional.15
  207.3 18.6 %conditional.16 = (f32[128,768]{1,0:T(8,128)}, bf16[128,128]{1,0:T(8,128)(2,1)S(1)}) conditional(s32[]{:T(128)} %clamp.57, () %tuple.316, (f32[128,768]{1,0:T(8,128)S(1)}, f32[1,768]{1,0:T(1,128)S(1)}, bf16[768,3072]{1,0:T(8,128)(2,1)}, s32[]{:T(128)}, s32[16]{0:T(128)}, /*index=5*/s32[128]{0:T(128)}, ...), branch_computations={%region_22.23_spmd, %region_23.27_spmd, %region_27.29_spmd, %regio... | conditional | flops 1842479360 | bytes 19715604 | solution.py:219
  232.4 10.3 conditional.17
  243.7 7.6 collective-permute-start.4
  255.5 7.9 conditional.18
  264.4 9.1 collective-permute-start.5
  279.4 8.6 collective-permute-start.6
  299.4 61.1 %all-reduce.6.cloned.1.call-done = bf16[4,128,128]{2,1,0:T(8,128)(2,1)} async-done(((bf16[4,128,128]{2,1,0:T(8,128)(2,1)}), bf16[4,128,128]{2,1,0:T(8,128)(2,1)}) %all-reduce.6.cloned.1.call-update) | async-done | bytes 131088 | tf_op jit(solution)/shard_map/psum | solution.py:25
  373.5 8.6 all_gather.15
  382.1 40.7 %conditional.21 = (bf16[128,768]{1,0:T(8,128)(2,1)}, f32[768,3072]{1,0:T(8,128)}, f32[768,3072]{1,0:T(8,128)}, f32[768,3072]{1,0:T(8,128)}, f32[768]{0:T(1024)S(...) conditional(s32[]{:T(128)} %clamp.62, () %tuple.336, ...), branch_computations={%region_82.83_spmd, %region_83.91_spmd, %region_91.95_spmd, %regio... | conditional | flops 5528862720 | bytes 128993616 | solution.py:355
  430.7 33.0 %conditional.22 = (bf16[128,768]{1,0:T(8,128)(2,1)}, f32[768,3072]{1,0:T(8,128)}, f32[768,3072]{1,0:T(8,128)}, f32[768,3072]{1,0:T(8,128)}, f32[768]{0:T(1024)S(...) conditional(s32[]{:T(128)} %clamp.63, () %tuple.340, ...), branch_computations={%region_104.105_spmd, %region_105.113_spmd, %region_113.117_spmd, ... | conditional | flops 5528862720 | bytes 128993616 | solution.py:355
  471.5 33.1 %conditional.23 = (bf16[128,768]{1,0:T(8,128)(2,1)}, f32[768,3072]{1,0:T(8,128)}, f32[768,3072]{1,0:T(8,128)}, f32[768,3072]{1,0:T(8,128)}, f32[768]{0:T(1024)S(...) conditional(s32[]{:T(128)} %clamp.64, () %tuple.344, ...), branch_computations={%region_126.127_spmd, %region_127.135_spmd, %region_135.139_spmd, ... | conditional | flops 5528862720 | bytes 128993616 | solution.py:355
  506.0 75.2 %collective-permute-done.9 = bf16[128,768]{1,0:T(8,128)(2,1)S(1)} collective-permute-done((bf16[128,768]{1,0:T(8,128)(2,1)}, bf16[128,768]{1,0:T(8,128)(2,1)S(1)}, u32[]{:S(2)}, u32[]{:S(2)}) %collective-permute-start.9) | collective-permute-done | bytes 196640 | tf_op jit(solution)/shard_map/ppermute | solution.py:20
  581.2 70.8 %conditional.24 = (bf16[128,768]{1,0:T(8,128)(2,1)}, f32[768,3072]{1,0:T(8,128)}, f32[768,3072]{1,0:T(8,128)}, f32[768,3072]{1,0:T(8,128)}, f32[768]{0:T(1024)S(...) conditional(s32[]{:T(128)} %clamp.65, () %tuple.348, ...), branch_computations={%region_148.149_spmd, %region_149.157_spmd, %region_157.161_spmd, ... | conditional | flops 5528862720 | bytes 128993616 | solution.py:355
  608.3 8.7 pad_maximum_fusion.12
  653.4 6.6 collective-permute-done.10
  660.0 70.8 %conditional.25 = (bf16[128,768]{1,0:T(8,128)(2,1)}, f32[768,3072]{1,0:T(8,128)}, f32[768,3072]{1,0:T(8,128)}, f32[768,3072]{1,0:T(8,128)}, f32[768]{0:T(1024)S(...) conditional(s32[]{:T(128)} %clamp.66, () %tuple.352, ...), branch_computations={%region_170.171_spmd, %region_171.179_spmd, %region_179.183_spmd, ... | conditional | flops 5528862720 | bytes 128993616 | solution.py:355
  687.1 8.8 pad_maximum_fusion.16
  738.7 70.7 %conditional.26 = (bf16[128,768]{1,0:T(8,128)(2,1)}, f32[768,3072]{1,0:T(8,128)}, f32[768,3072]{1,0:T(8,128)}, f32[768,3072]{1,0:T(8,128)}, f32[768]{0:T(1024)S(...) conditional(s32[]{:T(128)} %clamp.67, () %tuple.356, ...), branch_computations={%region_192.193_spmd, %region_193.201_spmd, %region_201.205_spmd, ... | conditional | flops 5528862720 | bytes 128993616 | solution.py:355
  765.8 8.7 pad_maximum_fusion.20
  817.3 63.5 %conditional.27 = (bf16[128,768]{1,0:T(8,128)(2,1)}, f32[768,3072]{1,0:T(8,128)}, f32[768,3072]{1,0:T(8,128)}, f32[768,3072]{1,0:T(8,128)}, f32[768]{0:T(1024)S(...) conditional(s32[]{:T(128)} %clamp.68, () %tuple.360, ...), branch_computations={%region_214.215_spmd, %region_215.223_spmd, %region_223.227_spmd, ... | conditional | flops 5528862720 | bytes 119032144 | solution.py:355
  839.9 8.7 pad_maximum_fusion.24
  883.4 26.9 %add_add_fusion.35 = f32[768,3072]{1,0:T(8,128)} fusion(f32[768,3072]{1,0:T(8,128)} %get-tuple-element.1889, f32[768,3072]{1,0:T(8,128)} %get-tuple-element.1888, f32[768,3072]{1,0:T(8,128)} %get-tuple-element.1887, f32[768,3072]{1,0:T(8,128)} %get-tuple-element.1886, f32[768,3072]{1,0:T(8,128)} %get-tuple-element.1885, ...), kind=kLoop, calls=%fused_computation.1252 | loop fusion | flops 14155776 | bytes 75497472 | tf_op jit(solution)/shard_map/add | solution.py:364
  910.4 23.4 %add_convert_fusion = bf16[768,3072]{1,0:T(8,128)(2,1)S(1)} fusion(f32[768,3072]{1,0:T(8,128)} %get-tuple-element.1896, f32[768,3072]{1,0:T(8,128)} %get-tuple-element.1895, f32[768,3072]{1,0:T(8,128)} %get-tuple-element.1894, f32[768,3072]{1,0:T(8,128)} %get-tuple-element.1893, f32[768,3072]{1,0:T(8,128)} %get-tuple-element.1892, ...), kind=kLoop, calls=%fused_computation.1251 | loop fusion | flops 16515072 | bytes 70778880 | tf_op jit(solution)/shard_map/convert_element_type | solution.py:29
  935.1 95.5 %collective-permute-done.13 = bf16[768,3072]{1,0:T(8,128)(2,1)} collective-permute-done((bf16[768,3072]{1,0:T(8,128)(2,1)S(1)}, bf16[768,3072]{1,0:T(8,128)(2,1)}, u32[]{:S(2)}, u32[]{:S(2)}) %collective-permute-start.13) | collective-permute-done | bytes 4718624 | tf_op jit(solution)/shard_map/ppermute | solution.py:20
  1030.6 28.3 %add_select_fusion = f32[768,3072]{1,0:T(8,128)} fusion(f32[768,3072]{1,0:T(8,128)} %get-tuple-element.1903, f32[768,3072]{1,0:T(8,128)} %get-tuple-element.1902, f32[768,3072]{1,0:T(8,128)} %get-tuple-element.1901, f32[768,3072]{1,0:T(8,128)} %get-tuple-element.1900, f32[768,3072]{1,0:T(8,128)} %get-tuple-element.1899, ...), kind=kLoop, calls=%fused_computation.1250 | loop fusion | flops 18874368 | bytes 80216064 | tf_op jit(solution)/shard_map/jit(_where)/select_n | solution.py:383
  1081.6 42.8 %all-reduce.2 = (f32[32,12]{0,1:T(8,128)}, f32[768]{0:T(1024)}) all-reduce(f32[32,12]{0,1:T(8,128)S(1)} %add_add_fusion.37, f32[768]{0:T(1024)S(1)} %add_add_fusion.38), channel_id=1, replica_groups=mesh['section'=4,'dp'=8] {'section','dp'}, use_global_device_ids=true, to_apply=%region_239.240 | all-reduce | flops 1152 | bytes 9216 | tf_op jit(solution)/shard_map/psum | solution.py:387
  1124.5 12.5 %all-reduce.1 = f32[768]{0:T(1024)S(1)} all-reduce(f32[768]{0:T(1024)S(1)} %add_add_fusion.39), channel_id=4, replica_groups=mesh['section'=4,'dp'=8] {'dp'}, use_global_device_ids=true, to_apply=%region_238.239.clone | all-reduce | flops 768 | bytes 6144
  1144.5 13.9 %reduce-scatter.5.cloned.1.call-done = f32[96,3072]{1,0:T(8,128)} async-done(((f32[768,3072]{1,0:T(8,128)}), f32[96,3072]{1,0:T(8,128)}) %reduce-scatter.5.cloned.1.call-update) | async-done | bytes 1179664 | tf_op jit(solution)/shard_map/reduce_scatter | solution.py:382
  (649 shorter events, 417.0 us)
Async XLA Ops:
  8.0 120.1 %copy-start = (f32[32,12]{0,1:T(8,128)S(1)}, f32[32,12]{0,1:T(8,128)}, u32[]{:S(2)}) copy-start(f32[32,12]{0,1:T(8,128)} %param.75) | copy-start | bytes 4612
  8.0 135.1 %all-gather.2.cloned.1.call-start = ((), (), s32[]{:S(2)}) async-start(), calls=%async_computation.4 | async-start | bytes 1179648 | tf_op jit(solution)/shard_map/all_gather | solution.py:132
  8.1 150.8 %collective-permute-start = (bf16[768,3072]{1,0:T(8,128)(2,1)}, bf16[768,3072]{1,0:T(8,128)(2,1)}, u32[]{:S(2)}, u32[]{:S(2)}) collective-permute-start(bf16[768,3072]{1,0:T(8,128)(2,1)} %bitcast.933), channel_id=1, source_target_pairs={{0,8},{8,16},{16,24},{1,9},{9,17},{17,25},{2,10},{10,18},{18,26},{... | collective-permute-start | bytes 14155784 | tf_op jit(solution)/shard_map/ppermute | solution.py:20
  13.7 346.8 %all-reduce.6.cloned.1.call-start = ((), (), s32[]{:S(2)}) async-start(), calls=%async_computation.3 | async-start | bytes 262144 | tf_op jit(solution)/shard_map/psum | solution.py:25
  142.4 222.6 %copy-start.128 = (f32[4,32]{1,0:T(4,128)}, f32[4,32]{1,0:T(4,128)S(1)}, u32[]{:S(2)}) copy-start(f32[4,32]{1,0:T(4,128)S(1)} %fusion.697) | copy-start | bytes 1540
  180.2 4.5 collective-permute-start.1
  197.5 9.0 collective-permute-start.2
  226.9 4.7 collective-permute-start.3
  243.7 11.0 collective-permute-start.4
  264.4 12.5 %collective-permute-start.5 = (bf16[128,768]{1,0:T(8,128)(2,1)S(1)}, bf16[128,768]{1,0:T(8,128)(2,1)S(1)}, u32[]{:S(2)}, u32[]{:S(2)}) collective-permute-start(bf16[128,768]{1,0:T(8,128)(2,1)S(1)} %convert_element_type.995), channel_id=1, source_target_pairs={{0,8},{8,16},{16,24},{1,9},{9,17},{17,25},{2,10},{10,18},{18,26},{... | collective-permute-start | bytes 589832 | tf_op jit(solution)/shard_map/ppermute | solution.py:20
  279.4 11.8 %collective-permute-start.6 = (bf16[128,768]{1,0:T(8,128)(2,1)S(1)}, bf16[128,768]{1,0:T(8,128)(2,1)S(1)}, u32[]{:S(2)}, u32[]{:S(2)}) collective-permute-start(bf16[128,768]{1,0:T(8,128)(2,1)S(1)} %convert_element_type.997), channel_id=1, source_target_pairs={{0,8},{8,16},{16,24},{1,9},{9,17},{17,25},{2,10},{10,18},{18,26},{... | collective-permute-start | bytes 589832 | tf_op jit(solution)/shard_map/ppermute | solution.py:20
  295.9 848.6 %all-reduce.8.cloned.1.call-start = ((), (), s32[]{:S(2)}) async-start(), calls=%async_computation.7 | async-start | bytes 786432 | tf_op jit(solution)/shard_map/psum | solution.py:387
  296.7 64.6 %copy-start.115 = (pred[4,32,32]{2,1,0:T(8,128)(4,1)S(1)}, pred[4,32,32]{2,1,0:T(8,128)(4,1)}, u32[]{:S(2)}) copy-start(pred[4,32,32]{2,1,0:T(8,128)(4,1)} %compare_and_fusion.1) | copy-start | bytes 12292
  422.8 7.8 collective-permute-start.7
  463.7 7.8 collective-permute-start.8
  471.5 109.7 %copy-start.6 = (f32[128,768]{1,0:T(8,128)S(1)}, f32[128,768]{1,0:T(8,128)}, u32[]{:S(2)}) copy-start(f32[128,768]{1,0:T(8,128)} %get-tuple-element.2698) | copy-start | bytes 1179652
  504.7 76.5 %copy-start.70 = (f32[768,128]{1,0:T(8,128)}, f32[768,128]{1,0:T(8,128)S(1)}, u32[]{:S(2)}) copy-start(f32[768,128]{1,0:T(8,128)S(1)} %get-tuple-element.1927) | copy-start | bytes 1179652
  504.7 76.5 %copy-start.120 = (f32[32,12]{0,1:T(8,128)}, f32[32,12]{0,1:T(8,128)S(1)}, u32[]{:S(2)}) copy-start(f32[32,12]{0,1:T(8,128)S(1)} %get-tuple-element.2398) | copy-start | bytes 4612
  504.7 76.5 %copy-start.138 = (f32[768]{0:T(1024)}, f32[768]{0:T(1024)S(1)}, u32[]{:S(2)}) copy-start(f32[768]{0:T(1024)S(1)} %get-tuple-element.1906) | copy-start | bytes 9220
  504.7 76.5 %copy-start.140 = (f32[768]{0:T(1024)}, f32[768]{0:T(1024)S(1)}, u32[]{:S(2)}) copy-start(f32[768]{0:T(1024)S(1)} %get-tuple-element.1920) | copy-start | bytes 9220
  504.7 76.5 %collective-permute-start.9 = (bf16[128,768]{1,0:T(8,128)(2,1)}, bf16[128,768]{1,0:T(8,128)(2,1)S(1)}, u32[]{:S(2)}, u32[]{:S(2)}) collective-permute-start(bf16[128,768]{1,0:T(8,128)(2,1)} %get-tuple-element.1878), channel_id=1, source_target_pairs={{8,0},{16,8},{24,16},{9,1},{17,9},{25,17},{10,2},{18,10},{26,18},{... | collective-permute-start | bytes 589832 | tf_op jit(solution)/shard_map/ppermute | solution.py:20
  581.2 78.8 %copy-start.5 = (f32[128,768]{1,0:T(8,128)S(1)}, f32[128,768]{1,0:T(8,128)}, u32[]{:S(2)}) copy-start(f32[128,768]{1,0:T(8,128)} %get-tuple-element.2697) | copy-start | bytes 1179652
  652.1 7.9 collective-permute-start.10
  660.0 78.7 %copy-start.4 = (f32[128,768]{1,0:T(8,128)S(1)}, f32[128,768]{1,0:T(8,128)}, u32[]{:S(2)}) copy-start(f32[128,768]{1,0:T(8,128)} %get-tuple-element.2696) | copy-start | bytes 1179652
  730.9 7.8 collective-permute-start.11
  738.7 78.6 %copy-start.3 = (f32[128,768]{1,0:T(8,128)S(1)}, f32[128,768]{1,0:T(8,128)}, u32[]{:S(2)}) copy-start(f32[128,768]{1,0:T(8,128)} %get-tuple-element.2695) | copy-start | bytes 1179652
  809.5 7.8 collective-permute-start.12
  883.3 261.2 %reduce-scatter.3.cloned.1.call-start = ((), (), s32[]{:S(2)}) async-start(), calls=%async_computation.5 | async-start | bytes 10616832 | tf_op jit(solution)/shard_map/reduce_scatter | solution.py:381
  910.3 248.0 %reduce-scatter.5.cloned.1.call-start = ((), (), s32[]{:S(2)}) async-start(), calls=%async_computation.6 | async-start | bytes 10616832 | tf_op jit(solution)/shard_map/reduce_scatter | solution.py:382
  933.8 96.8 %collective-permute-start.13 = (bf16[768,3072]{1,0:T(8,128)(2,1)S(1)}, bf16[768,3072]{1,0:T(8,128)(2,1)}, u32[]{:S(2)}, u32[]{:S(2)}) collective-permute-start(bf16[768,3072]{1,0:T(8,128)(2,1)S(1)} %add_convert_fusion), channel_id=1, source_target_pairs={{8,0},{16,8},{24,16},{9,1},{17,9},{25,17},{10,2},{18,10},{26,18},{... | collective-permute-start | bytes 14155784 | tf_op jit(solution)/shard_map/ppermute | solution.py:20
  1076.3 83.9 %copy-start.1 = (f32[32,12]{0,1:T(8,128)S(1)}, f32[32,12]{0,1:T(8,128)}, u32[]{:S(2)}) copy-start(f32[32,12]{0,1:T(8,128)} %param.75) | copy-start | bytes 4612
  1078.0 59.6 %all-to-all-start = ((bf16[4,128,768]{2,1,0:T(8,128)(2,1)}), bf16[4,128,768]{2,1,0:T(8,128)(2,1)S(1)}, u32[]{:S(2)}, u32[]{:S(2)}) async-start(bf16[4,128,768]{2,1,0:T(8,128)(2,1)} %bitcast_dynamic-update-slice_fusion), calls=%async_computation | async-start | bytes 1572864 | tf_op jit(solution)/shard_map/all_to_all | solution.py:390
  (108 other events, 1043.4 us)
Sparse Core Ops, SparseCore 0:
  13.8 20.8 all-gather.1
  910.5 96.4 reduce-scatter.2
  1059.0 99.3 reduce-scatter.4
Sparse Core Ops, SparseCore 1:
  296.0 64.4 all-reduce.5
  883.4 261.0 all-reduce.7
where the time goes:
time: 1180 us; the launch traced here: 1170 us
  waiting for transfers between devices  288 us (24%)
  other arithmetic  187 us (16%)
  blocking collectives  176 us (15%)
  local copies, waits for them, and re-layouts  172 us (15%)
  loops' own time  160 us (14%)
  matrix products  115 us (10%)
  starting transfers between devices  51.9 us (4%)
  between operations  18.5 us (2%)
    ppermute x14, waiting for transfers between devices, from_behind(): lax.ppermute(value, axis, [(source, source + steps) for source in range(i...  207 us
    another operation x7, loops' own time, per_device(): lax.switch(branch, [spare_backward, attention_backward, ffn_backward, las...  132 us
    all_gather x1, blocking collectives, per_device(): lax.all_gather(hidden_in, 'section', axis=0, tiled=True)  106 us
    broadcast_in_dim x17, local copies, waits for them, and re-layouts, per_device(): zero_slab = jnp.zeros((model_width, slab_width), jnp.float32)  81.3 us
    psum x1, waiting for transfers between devices, spread(): return lax.psum(block, axis)  61.1 us
    ppermute x14, starting transfers between devices, from_behind(): lax.ppermute(value, axis, [(source, source + steps) for source in range(i...  48.2 us
    psum x1, blocking collectives, per_device(): lax.psum((accum_table, accum_fgain, accum_proj), ('section', 'dp'))  42.8 us
    concatenate x4, other arithmetic, attention_backward(): d_main = jnp.concatenate([d_in_weight, d_out_weight], axis=1)  35 us
  transfers between devices with their start and end apart: 20, of which 12 were waited for; matrix products, arithmetic and copies ran while one was open for 13% of the time, Pallas kernels for 0%

commit v1 on v0

v1 whole, which is shorter than its diff:
```python
import functools
import math

import jax
import jax.numpy as jnp
import numpy as np
from jax import lax
from jax.experimental import pallas as pl
from jax.experimental.pallas import tpu as pltpu
from jax.sharding import PartitionSpec as P

H = 12
DH = 64
DOC_LEN = 128
EPS_NORM = 1e-06
MASK_FILL = -1000000000.0
HIGHEST = lax.Precision.HIGHEST
MESH = pl.DeviceIdType.MESH
F32 = jnp.float32
BF16 = jnp.bfloat16
VMEM = pltpu.VMEM
GELU_C = math.sqrt(2.0 / math.pi)
GELU_A = 0.044715
FF_STEP = 512
LEND_STEP = 128


def bucket_table(query_len):
    places = np.arange(query_len)
    relative = places[None, :] - places[:, None]
    distance = np.abs(relative)
    signed_part = np.where(relative > 0, 16, 0)
    far_bucket = 8 + np.floor(np.log(np.maximum(distance, 1) / 8.0) / np.log(16.0) * 8.0).astype(
        np.int64
    )
    far_bucket = np.minimum(far_bucket, 15)
    return (signed_part + np.where(distance < 8, distance, far_bucket)).astype(np.int32)


def nn(a, b):
    return jnp.dot(a, b, preferred_element_type=F32)


def nt(a, b):
    return lax.dot_general(a, b, (((1,), (1,)), ((), ())), preferred_element_type=F32)


def tn(a, b):
    return lax.dot_general(a, b, (((0,), (0,)), ((), ())), preferred_element_type=F32)


def rms_inverse(values):
    return lax.rsqrt(jnp.mean(values * values, axis=-1, keepdims=True) + EPS_NORM)


def rms_back(scaled, inverse, gain, grad):
    inner = grad * gain
    grad_values = inverse * (inner - scaled * jnp.mean(inner * scaled, axis=-1, keepdims=True))
    return grad_values, jnp.sum(grad * scaled, axis=0, keepdims=True)


def relay_kernel(
    sections,
    dp_size,
    batch_size,
    retrieved,
    hid_ref,
    meta_ref,
    idx_ref,
    lab_ref,
    main_ref,
    side_ref,
    gain_ref,
    bias_ref,
    bucket_ref,
    fgain_ref,
    proj_ref,
    docs_ref,
    units_ref,
    loss_ref,
    dx_ref,
    l1_ref,
    r1_ref,
    l2_ref,
    l3_ref,
    r3_ref,
    dgain_ref,
    dbias_ref,
    dfgain_ref,
    dproj_ref,
    lent,
    xin,
    xout,
    dyin,
    meta_rx,
    idx_rx,
    lab_rx,
    own_docs,
    table,
    counts,
    act_b,
    n_t,
    qkv,
    probs,
    bias_sc,
    fin_rx,
    unit_tx,
    unit_rx,
    loss_tx,
    loss_rx,
    state_ss,
    state_rs,
    grad_ss,
    grad_rs,
    meta_ss,
    meta_rs,
    idx_ss,
    idx_rs,
    lab_ss,
    lab_rs,
    tab_ss,
    tab_rs,
    lend_ss,
    lend_rs,
    fin_ss,
    fin_rs,
    unit_ss,
    unit_rs,
    loss_ss,
    loss_rs,
    up_ss,
    up_rs,
    nt_ss,
    nt_rs,
):
    s = lax.axis_index("section")
    d = lax.axis_index("dp")
    rows, width = hid_ref.shape
    ff = main_ref.shape[1]
    head_width = H * DH
    doc_rows = docs_ref.shape[0]
    query_len = rows // batch_size
    last = sections - 1
    group = d - lax.rem(d, 4)
    place = lax.rem(d, 4)
    core_peer = group + place + 1 - 2 * lax.rem(place, 2)
    far_place = lax.rem(place + 2, 4)
    far_peer = group + far_place
    is_attention = lax.rem(s, 2) == 0

    def copy(src, dst, send_sem, recv_sem, section, dp):
        return pltpu.make_async_remote_copy(
            src_ref=src,
            dst_ref=dst,
            send_sem=send_sem,
            recv_sem=recv_sem,
            device_id=(section, dp),
            device_id_type=MESH,
        )

    def block(m):
        return pl.ds(pl.multiple_of(m * rows, rows), rows)

    barrier = pltpu.get_barrier_semaphore()
    for step in range(1, sections):
        pl.semaphore_signal(
            barrier, inc=1, device_id=(lax.rem(s + step, sections), d), device_id_type=MESH
        )

    def greet(step, carry):
        pl.semaphore_signal(
            barrier, inc=1, device_id=(s, lax.rem(d + step, dp_size)), device_id_type=MESH
        )
        return carry

    lax.fori_loop(1, dp_size, greet, 0)
    pl.semaphore_wait(barrier, sections - 1 + dp_size - 1)

    def lend_columns(quarter, part):
        start = quarter * (ff // 4) + part * LEND_STEP
        return pl.ds(pl.multiple_of(start, LEND_STEP), LEND_STEP)

    parts = ff // 4 // LEND_STEP

    def lend_copy(part):
        columns = lend_columns(place, part)
        return copy(
            side_ref.at[:, columns],
            lent.at[:, columns],
            lend_ss.at[0, part],
            lend_rs.at[0, part],
            lax.rem(s + 1, sections),
            d,
        )

    def lend_forward(kind, quarter, part, peer):
        columns = lend_columns(quarter, part)
        return copy(
            lent.at[:, columns],
            lent.at[:, columns],
            lend_ss.at[kind, part],
            lend_rs.at[kind, part],
            s,
            peer,
        )

    def state_copy(m):
        return copy(
            xout.at[m], xin.at[m], state_ss.at[m], state_rs.at[m], lax.rem(s + 1, sections), d
        )

    def grad_copy(m):
        return copy(
            xout.at[m],
            dyin.at[m],
            grad_ss.at[m],
            grad_rs.at[m],
            lax.rem(s + sections - 1, sections),
            d,
        )

    def up_copy(m):
        return copy(
            act_b.at[block(m), :],
            r3_ref.at[block(m), :],
            up_ss.at[m],
            up_rs.at[m],
            lax.rem(s + sections - 1, sections),
            d,
        )

    def normed_copy(m):
        return copy(
            n_t.at[:, block(m)],
            l3_ref.at[:, block(m)],
            nt_ss.at[m],
            nt_rs.at[m],
            lax.rem(s + sections - 1, sections),
            d,
        )

    def meta_copy(to, slot):
        return copy(meta_ref, meta_rx.at[slot], meta_ss.at[to], meta_rs.at[slot], to, d)

    def idx_copy(slot):
        return copy(idx_ref, idx_rx.at[slot], idx_ss, idx_rs.at[slot], last, d)

    def lab_copy(slot):
        return copy(lab_ref, lab_rx.at[slot], lab_ss, lab_rs.at[slot], last, d)

    def hid_copy(slot):
        return copy(hid_ref, xin.at[slot], state_ss.at[sections], state_rs.at[slot], 0, d)

    def unit_copy(m, to):
        return copy(unit_tx.at[m], unit_rx, unit_ss.at[m], unit_rs, to, d)

    def loss_copy(m, to):
        return copy(loss_tx.at[m], loss_rx, loss_ss.at[m], loss_rs, to, d)

    def fin_copy(m, to):
        return copy(xout.at[m], fin_rx, fin_ss.at[m], fin_rs, to, d)

    def table_rows(owner):
        return pl.ds(pl.multiple_of(owner * doc_rows, doc_rows), doc_rows)

    def table_copy(to):
        return copy(docs_ref, table.at[table_rows(d), :], tab_ss.at[to], tab_rs.at[d], s, to)

    @pl.when(s != 0)
    def _():
        hid_copy(s).start()

    @pl.when(s == 0)
    def _():
        xin[0] = hid_ref[...]

    for to in range(sections):

        @pl.when(s != to)
        def _():
            meta_copy(to, s).start()

    meta_rx[s] = meta_ref[...]

    @pl.when(s != last)
    def _():
        idx_copy(s).start()
        lab_copy(s).start()

    @pl.when(is_attention)
    def _():
        for part in range(parts):
            lend_copy(part).start()

    dgain_ref[...] = jnp.zeros_like(dgain_ref)
    dfgain_ref[...] = jnp.zeros_like(dfgain_ref)
    dproj_ref[...] = jnp.zeros_like(dproj_ref)
    dbias_ref[...] = jnp.zeros_like(dbias_ref)

    gain = gain_ref[...]

    def wait_meta(m):
        @pl.when(m != s)
        def _():
            meta_copy(0, m).wait_recv()

    def load_state(m):
        states = xin[m].astype(F32)
        inverse = rms_inverse(states)
        return states, inverse, states * inverse

    lane = lax.broadcasted_iota(jnp.int32, (1, 128), 1)
    low_half = lane < DH

    def half_of(value, upper):
        keep = jnp.logical_not(low_half) if upper else low_half
        return jnp.where(keep, value.astype(F32), 0.0).astype(BF16)

    def attention_setup():
        buckets = bucket_ref[...]
        for h in range(H):
            total = jnp.zeros(buckets.shape, F32)
            for b in range(32):
                total = jnp.where(buckets == b, bias_ref[b, h], total)
            bias_sc[h] = total

    def attention_forward(m):
        states, inverse, scaled = load_state(m)
        normed = scaled * gain
        l1_ref[:, block(m)] = normed.T.astype(BF16)
        normed_low = normed.astype(BF16)
        for start in range(0, 3 * head_width, head_width):
            qkv[block(m), start : start + head_width] = nn(
                normed_low, main_ref[:, start : start + head_width]
            ).astype(BF16)
        live = meta_rx[m, 0:1, :] > 0.5
        row_query = lax.broadcasted_iota(jnp.int32, (rows, rows), 0) // query_len
        column_query = lax.broadcasted_iota(jnp.int32, (rows, rows), 1) // query_len
        keep = jnp.logical_and(row_query == column_query, live)
        for pair in range(H // 2):
            at = pair * 128
            query = qkv[block(m), at : at + 128]
            keys = qkv[block(m), head_width + at : head_width + at + 128]
            values = qkv[block(m), 2 * head_width + at : 2 * head_width + at + 128]
            contexts = []
            for upper in (0, 1):
                h = 2 * pair + upper
                raw = nt(half_of(query, upper), keys)
                biased = raw.reshape(batch_size, query_len, rows) + bias_sc[h][None]
                scores = jnp.where(keep, biased.reshape(rows, rows), MASK_FILL)
                top = jnp.max(scores, axis=-1, keepdims=True)
                grown = jnp.exp(scores - top)
                soft = grown / jnp.sum(grown, axis=-1, keepdims=True)
                probs[m, h] = soft
                contexts.append(nn(soft.astype(BF16), values))
            r1_ref[block(m), 3 * head_width + at : 3 * head_width + at + 128] = jnp.where(
                low_half, contexts[0], contexts[1]
            ).astype(BF16)
        context = r1_ref[block(m), 3 * head_width :]
        return states + nt(context, main_ref[:, 3 * head_width :])

    def attention_backward(m):
        states, inverse, scaled = load_state(m)
        grad_low = dyin[m]
        grad = grad_low.astype(F32)
        l2_ref[:, block(m)] = grad.T.astype(BF16)
        grad_context = nn(grad_low, main_ref[:, 3 * head_width :]).astype(BF16)
        for pair in range(H // 2):
            at = pair * 128
            query = qkv[block(m), at : at + 128]
            keys = qkv[block(m), head_width + at : head_width + at + 128]
            values = qkv[block(m), 2 * head_width + at : 2 * head_width + at + 128]
            grad_pair = grad_context[:, at : at + 128]
            found = []
            for upper in (0, 1):
                h = 2 * pair + upper
                soft = probs[m, h]
                grad_soft = nt(half_of(grad_pair, upper), values)
                moved = soft * grad_soft
                grad_scores = moved - soft * jnp.sum(moved, axis=-1, keepdims=True)
                dbias_ref[h] += jnp.sum(
                    grad_scores.reshape(batch_size, query_len, rows), axis=0
                )
                scores_low = grad_scores.astype(BF16)
                found.append(
                    (
                        nn(scores_low, keys),
                        tn(scores_low, query),
                        tn(soft.astype(BF16), grad_pair),
                    )
                )
            for third in range(3):
                start = third * head_width + at
                r1_ref[block(m), start : start + 128] = jnp.where(
                    low_half, found[0][third], found[1][third]
                ).astype(BF16)
        grad_normed = nt(r1_ref[block(m), : 3 * head_width], main_ref[:, : 3 * head_width])
        grad_states, grad_gain = rms_back(scaled, inverse, gain, grad_normed)
        dgain_ref[...] += grad_gain
        return grad + grad_states

    def ffn_forward(m):
        states, inverse, scaled = load_state(m)
        normed = scaled * gain
        turned = normed.T.astype(BF16)
        l1_ref[:, block(m)] = turned
        l2_ref[:, block(m)] = turned
        n_t[:, block(m)] = turned
        normed_copy(m).start()
        normed_low = normed.astype(BF16)
        outputs = states
        for start in range(0, ff, FF_STEP):
            columns = slice(start, start + FF_STEP)
            gate = nn(normed_low, main_ref[:, columns])
            up = nn(normed_low, lent[:, columns])
            square = gate * gate
            bent = jnp.tanh(GELU_C * gate * (1.0 + GELU_A * square))
            half = 0.5 * (1.0 + bent)
            smooth = gate * half
            slope = half + 0.5 * gate * (1.0 - bent * bent) * (
                GELU_C * (1.0 + 3.0 * GELU_A * square)
            )
            hidden = (smooth * up).astype(BF16)
            r3_ref[block(m), columns] = hidden
            r1_ref[block(m), columns] = (slope * up).astype(BF16)
            act_b[block(m), columns] = smooth.astype(BF16)
            outputs = outputs + nt(hidden, side_ref[:, columns])
        return outputs

    def ffn_backward(m, grad):
        states, inverse, scaled = load_state(m)
        grad_low = grad.astype(BF16)
        l3_ref[:, block(m)] = grad.T.astype(BF16)
        grad_normed = jnp.zeros((rows, width), F32)
        for start in range(0, ff, FF_STEP):
            columns = slice(start, start + FF_STEP)
            grad_hidden = nn(grad_low, side_ref[:, columns])
            grad_gate = (grad_hidden * r1_ref[block(m), columns].astype(F32)).astype(BF16)
            grad_up = (grad_hidden * act_b[block(m), columns].astype(F32)).astype(BF16)
            r1_ref[block(m), columns] = grad_gate
            act_b[block(m), columns] = grad_up
            grad_normed = (
                grad_normed
                + nt(grad_gate, main_ref[:, columns])
                + nt(grad_up, lent[:, columns])
            )
        up_copy(m).start()
        grad_states, grad_gain = rms_back(scaled, inverse, gain, grad_normed)
        dgain_ref[...] += grad_gain
        return grad + grad_states

    def count_hits(m):
        for c in range(batch_size):
            base = lab_rx[m, c : c + 1, :] * DOC_LEN
            numbers = lax.broadcasted_iota(jnp.int32, (DOC_LEN, rows), 0) + base
            total = jnp.zeros((DOC_LEN, rows), F32)
            for k in range(retrieved):
                total = total + jnp.where(idx_rx[m, k : k + 1, :] == numbers, 1.0, 0.0)
            counts[m, c * DOC_LEN : (c + 1) * DOC_LEN, :] = total

    def pick_docs(m):
        for c in range(batch_size):
            label = lab_rx[m, c : c + 1, :]

            def pick(t, picked):
                here = table[pl.ds(pl.multiple_of(t * DOC_LEN, DOC_LEN), DOC_LEN), :].astype(F32)
                return jnp.where(label == t, here, picked)

            picked = lax.fori_loop(
                0, table.shape[0] // DOC_LEN, pick, jnp.zeros((DOC_LEN, table.shape[1]), F32)
            )
            own_docs[m, c * DOC_LEN : (c + 1) * DOC_LEN, :] = picked.astype(BF16)

    def loss_and_grad(m, unit):
        docs = own_docs[m]
        sims = nt(docs, unit)
        count = counts[m]
        imputed = jnp.sum(count * sims, axis=0, keepdims=True) / retrieved
        grown = count * jnp.exp(sims)
        imputed_mass = jnp.exp(imputed)
        mass = imputed_mass + jnp.concatenate(
            [
                jnp.sum(grown[c * DOC_LEN : (c + 1) * DOC_LEN], axis=0, keepdims=True)
                for c in range(batch_size)
            ],
            axis=0,
        )
        weighted = jnp.log(mass) * meta_rx[m, 1:2, :]
        token_query = lax.broadcasted_iota(jnp.int32, (1, rows), 1) // query_len
        candidate = lax.broadcasted_iota(jnp.int32, (batch_size, 1), 0)
        losses = jnp.zeros((1, rows), F32)
        grad_tokens = jnp.zeros((batch_size, rows), F32)
        for q in range(batch_size):
            own = token_query == q
            score = jnp.sum(jnp.where(own, weighted, 0.0), axis=1, keepdims=True)
            top = jnp.max(score, axis=0, keepdims=True)
            risen = jnp.exp(score - top)
            total = jnp.sum(risen, axis=0, keepdims=True)
            chosen_one = (candidate == q).astype(F32)
            loss = top + jnp.log(total) - jnp.sum(score * chosen_one, axis=0, keepdims=True)
            losses = losses + jnp.where(lane == q, loss, 0.0)
            grad_tokens = grad_tokens + jnp.where(own, risen / total - chosen_one, 0.0)
        grad_mass = grad_tokens * meta_rx[m, 1:2, :] / mass
        shared = jnp.sum(grad_mass, axis=0, keepdims=True) * imputed_mass / retrieved
        grad_sims = count * shared + jnp.concatenate(
            [
                grown[c * DOC_LEN : (c + 1) * DOC_LEN] * grad_mass[c : c + 1]
                for c in range(batch_size)
            ],
            axis=0,
        )
        high = grad_sims.astype(BF16)
        rest = (grad_sims - high.astype(F32)).astype(BF16)
        return losses, tn(high, docs) + tn(rest, docs)

    def finish(m, states):
        inverse = rms_inverse(states)
        scaled = states * inverse
        normed = (scaled * fgain_ref[...]).astype(BF16)
        projected = nn(normed, proj_ref[...])
        length = lax.rsqrt(jnp.sum(projected * projected, axis=-1, keepdims=True) + EPS_NORM)
        exact = projected * length
        unit = exact.astype(BF16)
        losses, grad_unit = loss_and_grad(m, unit)
        unit_tx[m] = unit
        loss_tx[m] = jnp.broadcast_to(losses, loss_tx.shape[1:])

        @pl.when(m != last)
        def _():
            unit_copy(m, m).start()
            loss_copy(m, m).start()

        @pl.when(m == last)
        def _():
            units_ref[...] = unit_tx[last]
            loss_ref[...] = loss_tx[last]

        grad_projected = (
            length * (grad_unit - exact * jnp.sum(grad_unit * exact, axis=-1, keepdims=True))
        ).astype(BF16)
        dproj_ref[...] += tn(normed, grad_projected)
        grad_normed = nt(grad_projected, proj_ref[...])
        grad_states, grad_gain = rms_back(scaled, inverse, fgain_ref[...], grad_normed)
        dfgain_ref[...] += grad_gain
        return grad_states

    def loop(body):
        def step(m, carry):
            body(m)
            return carry

        lax.fori_loop(0, sections, step, 0)

    def wait_state(m):
        @pl.when(jnp.logical_or(s != 0, m != 0))
        def _():
            state_copy(m).wait_recv()

    @pl.when(is_attention)
    def _():
        attention_setup()

        def forward(m):
            wait_meta(m)
            wait_state(m)
            xout[m] = attention_forward(m).astype(BF16)
            state_copy(m).start()

        loop(forward)
        loop(lambda m: state_copy(m).wait_send())

        def backward(m):
            grad_copy(m).wait_recv()
            result = attention_backward(m)
            xout[m] = result.astype(BF16)

            @pl.when(s != 0)
            def _():
                grad_copy(m).start()

            @pl.when(jnp.logical_and(s == 0, m != 0))
            def _():
                fin_copy(m, m).start()

            @pl.when(jnp.logical_and(s == 0, m == 0))
            def _():
                dx_ref[...] = xout[0].astype(F32)

        loop(backward)

        @pl.when(s != 0)
        def _():
            loop(lambda m: grad_copy(m).wait_send())

        @pl.when(s == 0)
        def _():
            for m in range(1, sections):
                fin_copy(m, m).wait_send()

        for part in range(parts):
            lend_copy(part).wait_send()
        loop(lambda m: normed_copy(m).wait_recv())
        loop(lambda m: up_copy(m).wait_recv())

    @pl.when(jnp.logical_not(is_attention))
    def _():
        for part in range(parts):
            lend_copy(part).wait_recv()
            lend_forward(1, place, part, core_peer).start()
            lend_forward(2, place, part, far_peer).start()

        @pl.when(s == last)
        def _():
            idx_rx[last] = idx_ref[...]
            lab_rx[last] = lab_ref[...]
            table[table_rows(d), :] = docs_ref[...]

            def send_table(step, carry):
                table_copy(lax.rem(d + step, dp_size)).start()
                return carry

            lax.fori_loop(1, dp_size, send_table, 0)

            def prepare(m):
                @pl.when(m != last)
                def _():
                    idx_copy(m).wait_recv()
                    lab_copy(m).wait_recv()

                count_hits(m)

            loop(prepare)

        for part in range(parts):
            lend_forward(2, far_place, part, far_peer).wait_recv()
            lend_forward(3, far_place, part, core_peer).start()
        for part in range(parts):
            lend_forward(1, place, part, core_peer).wait_recv()
            lend_forward(3, far_place, part, core_peer).wait_recv()

        @pl.when(s == last)
        def _():
            def take_table(step, carry):
                owner = lax.rem(d + step, dp_size)
                copy(
                    docs_ref,
                    table.at[table_rows(owner), :],
                    tab_ss.at[owner],
                    tab_rs.at[owner],
                    s,
                    owner,
                ).wait_recv()
                return carry

            lax.fori_loop(1, dp_size, take_table, 0)
            loop(pick_docs)
            loop(wait_meta)

            def both(m):
                wait_state(m)
                states = ffn_forward(m)
                grad = finish(m, states)
                xout[m] = ffn_backward(m, grad).astype(BF16)
                grad_copy(m).start()

            loop(both)
            loop(lambda m: grad_copy(m).wait_send())
            for m in range(sections - 1):
                unit_copy(m, m).wait_send()
                loss_copy(m, m).wait_send()

            def drain_table(step, carry):
                table_copy(lax.rem(d + step, dp_size)).wait_send()
                return carry

            lax.fori_loop(1, dp_size, drain_table, 0)

        @pl.when(s != last)
        def _():
            def forward(m):
                wait_state(m)
                xout[m] = ffn_forward(m).astype(BF16)
                state_copy(m).start()

            loop(forward)
            loop(lambda m: state_copy(m).wait_send())

            def backward(m):
                grad_copy(m).wait_recv()
                xout[m] = ffn_backward(m, dyin[m].astype(F32)).astype(BF16)
                grad_copy(m).start()

            loop(backward)
            loop(lambda m: grad_copy(m).wait_send())
            loop(wait_meta)

        loop(lambda m: normed_copy(m).wait_send())
        loop(lambda m: up_copy(m).wait_send())
        for part in range(parts):
            lend_forward(1, place, part, core_peer).wait_send()
            lend_forward(2, place, part, far_peer).wait_send()
            lend_forward(3, far_place, part, core_peer).wait_send()

    for to in range(sections):

        @pl.when(s != to)
        def _():
            meta_copy(to, s).wait_send()

    @pl.when(s != 0)
    def _():
        hid_copy(s).wait_send()
        fin_copy(0, s).wait_recv()
        dx_ref[...] = fin_rx[...].astype(F32)

    @pl.when(s != last)
    def _():
        idx_copy(s).wait_send()
        lab_copy(s).wait_send()
        unit_copy(0, s).wait_recv()
        loss_copy(0, s).wait_recv()
        units_ref[...] = unit_rx[...]
        loss_ref[...] = loss_rx[...]


def relay(
    sections, dp_size, batch_size, retrieved, hid, meta, idx, lab, main, side, gain, bias, buckets,
    fgain, proj, docs
):
    rows, width = hid.shape
    ff = main.shape[1]
    total = sections * rows
    vector = proj.shape[1]
    query_len = rows // batch_size
    parts = ff // 4 // LEND_STEP
    dma = pltpu.SemaphoreType.DMA
    in_vmem = pl.BlockSpec(memory_space=VMEM)
    shape = jax.ShapeDtypeStruct
    out_shape = (
        shape((rows, vector), BF16),
        shape((8, rows), F32),
        shape((rows, width), F32),
        shape((width, total), BF16),
        shape((total, ff), BF16),
        shape((width, total), BF16),
        shape((width, total), BF16),
        shape((total, ff), BF16),
        shape((1, width), F32),
        shape((H, query_len, rows), F32),
        shape((1, width), F32),
        shape((width, vector), F32),
    )
    scratch = [
        VMEM((width, ff), BF16),
        VMEM((sections, rows, width), BF16),
        VMEM((sections, rows, width), BF16),
        VMEM((sections, rows, width), BF16),
        VMEM((sections, 8, rows), F32),
        VMEM((sections, retrieved, rows), jnp.int32),
        VMEM((sections, 8, 128), jnp.int32),
        VMEM((sections, batch_size * DOC_LEN, vector), BF16),
        VMEM((dp_size * docs.shape[0], vector), BF16),
        VMEM((sections, batch_size * DOC_LEN, rows), F32),
        VMEM((total, ff), BF16),
        VMEM((width, total), BF16),
        VMEM((total, 3 * H * DH), BF16),
        VMEM((sections, H, rows, rows), F32),
        VMEM((H, query_len, rows), F32),
        VMEM((rows, width), BF16),
        VMEM((sections, rows, vector), BF16),
        VMEM((rows, vector), BF16),
        VMEM((sections, 8, rows), F32),
        VMEM((8, rows), F32),
        dma((sections + 1,)),
        dma((sections,)),
        dma((sections,)),
        dma((sections,)),
        dma((sections,)),
        dma((sections,)),
        dma,
        dma((sections,)),
        dma,
        dma((sections,)),
        dma((dp_size,)),
        dma((dp_size,)),
        dma((4, parts)),
        dma((4, parts)),
        dma((sections,)),
        dma,
        dma((sections,)),
        dma,
        dma((sections,)),
        dma,
        dma((sections,)),
        dma((sections,)),
        dma((sections,)),
        dma((sections,)),
    ]
    in_specs = [in_vmem] * 12
    in_specs[7] = pl.BlockSpec(memory_space=pltpu.SMEM)
    return pl.pallas_call(
        functools.partial(relay_kernel, sections, dp_size, batch_size, retrieved),
        out_shape=out_shape,
        in_specs=in_specs,
        out_specs=(in_vmem,) * len(out_shape),
        scratch_shapes=scratch,
        compiler_params=pltpu.CompilerParams(
            collective_id=0, has_side_effects=True, vmem_limit_bytes=62 * 2**20
        ),
        name="relay",
    )(hid, meta, idx, lab, main, side, gain, bias, buckets, fgain, proj, docs)


def per_device(
    hidden_in,
    lengths,
    labels,
    chosen,
    slab_main,
    slab_side,
    section_gains,
    rel_bias,
    final_gain,
    out_proj,
    doc_vectors,
):
    sections = lax.axis_size("section")
    dp_size = lax.axis_size("dp")
    is_attention = lax.axis_index("section") % 2 == 0
    batch_size, query_len, width = hidden_in.shape
    rows = batch_size * query_len
    retrieved = chosen.shape[2]
    head_width = H * DH

    live = (jnp.arange(query_len)[None, :] < lengths[:, None]).astype(F32)
    per_slot = live / lengths[:, None].astype(F32)
    meta = jnp.concatenate(
        [live.reshape(1, rows), per_slot.reshape(1, rows), jnp.zeros((6, rows), F32)], axis=0
    )
    idx = chosen.reshape(rows, retrieved).T
    lab = jnp.broadcast_to(jnp.pad(labels, (0, 8 - batch_size))[:, None], (8, 128))
    buckets = jnp.asarray(np.tile(bucket_table(query_len), (1, batch_size)))
    (units, loss, input_grad, l1, r1, l2, l3, r3, gain_grad, bias_grad, fgain_grad, proj_grad) = relay(
        sections,
        dp_size,
        batch_size,
        retrieved,
        hidden_in.reshape(rows, width),
        meta,
        idx,
        lab,
        slab_main[0],
        slab_side[0],
        section_gains,
        rel_bias,
        buckets,
        final_gain.reshape(1, width),
        out_proj,
        doc_vectors,
    )
    main_grad = jnp.concatenate(
        [nn(l1, r1[:, : 3 * head_width]), nn(l2, r1[:, 3 * head_width :])], axis=1
    )
    side_grad = nn(l3, r3)
    main_part = lax.psum_scatter(main_grad, "dp", scatter_dimension=0, tiled=True)
    side_part = lax.psum_scatter(side_grad, "dp", scatter_dimension=0, tiled=True)
    gain_part = lax.psum_scatter(gain_grad[0], "dp", scatter_dimension=0, tiled=True)
    onehot = jnp.asarray(
        (bucket_table(query_len)[:, :, None] == np.arange(32)[None, None, :]).astype(np.float32)
    )
    folded = jnp.sum(bias_grad.reshape(H, query_len, batch_size, query_len), axis=2)
    table_grad = jnp.einsum("hij,ijc->ch", folded, onehot, precision=HIGHEST)
    table_sum, fgain_sum, proj_sum = lax.psum(
        (table_grad, fgain_grad[0], proj_grad), ("section", "dp")
    )
    return (
        units.reshape(batch_size, query_len, -1),
        loss[0, :batch_size],
        input_grad.reshape(batch_size, query_len, width),
        main_part[None],
        side_part[None],
        gain_part[None],
        table_sum,
        fgain_sum,
        proj_sum,
    )


def solution(mesh):
    both = ("section", "dp")
    in_specs = (
        P(both, None, None),
        P(both),
        P(both),
        P(both, None, None),
        P("section", None, None),
        P("section", None, None),
        P("section", None),
        P(),
        P(),
        P(),
        P("dp", None),
    )
    out_specs = (
        P(both, None, None),
        P(both),
        P(both, None, None),
        P("section", "dp", None),
        P("section", "dp", None),
        P("section", "dp"),
        P(),
        P(),
        P(),
    )
    return jax.shard_map(
        per_device, mesh=mesh, in_specs=in_specs, out_specs=out_specs, check_vma=False
    )
```

time: 1180 us -> 489 us (0.41)
  Pallas kernels: 0 us -> 221 us
  other arithmetic: 187 us -> 10.7 us
  loops' own time: 160 us -> 0 us
  local copies, waits for them, and re-layouts: 172 us -> 14.5 us
  waiting for transfers between devices: 288 us -> 153 us
  blocking collectives: 176 us -> 57.5 us
  matrix products: 115 us -> 14 us
  starting transfers between devices: 51.9 us -> 0.13 us
    pallas_call x0 -> x1, Pallas kernels: none -> 221 us  [relay(): pl.pallas_call(functools.partial(relay_kernel, sections, dp_size, batch_s...]
    ppermute x14 -> x0, waiting for transfers between devices: 207 us -> none  [from_behind(): lax.ppermute(value, axis, [(source, source + steps) for source in range(i...]
    another operation x14 -> x0, loops' own time: 160 us -> none  [the longest x7 132 us: per_device(): lax.switch(branch, [spare_backward, attention_backward, ffn_backward, las...]
    all_gather x2 -> x0, blocking collectives: 115 us -> none  [the longest x1 106 us: per_device(): lax.all_gather(hidden_in, 'section', axis=0, tiled=True)]
    dot_general x66 -> x4, matrix products: 115 us -> 14 us  [the longest x3 13.4 us: nn(): return jnp.dot(a, b, preferred_element_type=F32)]
    broadcast_in_dim x60 -> x2, local copies, waits for them, and re-layouts: 87.8 us -> 0.66 us  [the longest x1 0.66 us: per_device(): jnp.broadcast_to(jnp.pad(labels, (0, 8 - batch_size))[:, None], (8, 128))]
    psum x2 -> x1, waiting for transfers between devices: 67.2 us -> 153 us  [per_device(): lax.psum((table_grad, fgain_grad[0], proj_grad), ('section', 'dp'))]
    ppermute x14 -> x0, starting transfers between devices: 48.2 us -> none  [from_behind(): lax.ppermute(value, axis, [(source, source + steps) for source in range(i...]
  transfers between devices with their start and end apart: 20 -> 3, of which waited for: 12 -> 1; matrix products, arithmetic and copies ran while one was open for 13% -> 5% of each run, Pallas kernels for 0% -> 0%
where the time goes in v1:
time: 489 us; the launch traced here: 486 us
  Pallas kernels  221 us (45%)
  waiting for transfers between devices  153 us (31%)
  blocking collectives  57.5 us (12%)
  between operations  16.3 us (3%)
  local copies, waits for them, and re-layouts  14.5 us (3%)
  matrix products  14 us (3%)
  other arithmetic  10.7 us (2%)
    pallas_call x1, Pallas kernels, relay(): pl.pallas_call(functools.partial(relay_kernel, sections, dp_size, batch_s...  221 us
    psum x1, waiting for transfers between devices, per_device(): lax.psum((table_grad, fgain_grad[0], proj_grad), ('section', 'dp'))  153 us
    psum x1, blocking collectives, per_device(): lax.psum((table_grad, fgain_grad[0], proj_grad), ('section', 'dp'))  45.2 us
    dot_general x3, matrix products, nn(): return jnp.dot(a, b, preferred_element_type=F32)  13.4 us
    unnamed x1, blocking collectives  12.3 us
  transfers between devices with their start and end apart: 3, of which 1 were waited for; matrix products, arithmetic and copies ran while one was open for 5% of the time, Pallas kernels for 0%

profile of v1, /device:TPU:16, one launch (start us, length us, event | category | flops | bytes accessed | tf_op | source)
XLA Modules:
  0.0 486.2 jit_solution(3126796169024668959)
XLA Ops:
  8.1 0.7 convert_element_type.23
  8.7 0.7 fusion.5
  9.5 0.1 div.18
  9.6 0.1 reshape.99
  9.7 1.3 reshape.95.fgain_ref
  10.9 1.5 copy.30
  12.5 1.4 copy.26.bias_ref
  13.8 0.7 pad.4
  14.5 0.1 pad.9.clone
  14.6 0.7 maximum_maximum_fusion.meta_ref
  15.3 0.7 broadcast_in_dim.22.lab_ref
  15.9 220.5 %relay.1 = (bf16[128,128]{1,0:T(8,128)(2,1)}, f32[8,128]{1,0:T(8,128)}, f32[128,768]{1,0:T(8,128)}, bf16[768,512]{1,0:T(8,128)(2,1)}, bf16[512,3072]{1,0:T(8,128...) custom-call(bf16[128,768]{1,0:T(8,128)(2,1)} %bitcast.24, ...), custom_call_target="tpu_custom_call" | custom-call | tf_op jit(solution)/shard_map/relay/pallas_call | solution.py:801
  236.5 2.3 fusion.2
  238.8 0.2 copy-done
  239.1 4.9 %fusion = f32[768,2304]{1,0:T(8,128)} fusion(bf16[768,512]{1,0:T(8,128)(2,1)S(1)} %copy-done.1, bf16[512,3072]{1,0:T(8,128)(2,1)S(1)} %copy-done), kind=kOutput, calls=%fused_computation.1 | convolution fusion | flops 1811939328 | bytes 10223616 | tf_op jit(solution)/shard_map/dot_general | solution.py:41
  244.0 8.1 %pad_maximum_fusion = f32[768,3072]{1,0:T(8,128)} fusion(f32[768,768]{1,0:T(8,128)S(1)} %fusion.2, f32[768,2304]{1,0:T(8,128)} %fusion), kind=kLoop, calls=%fused_computation | loop fusion | flops 2359296 | bytes 18874368 | tf_op jit(solution)/shard_map/concatenate | solution.py:861
  252.1 1.8 copy-done.8
  254.0 6.2 %fusion.6 = f32[768,3072]{1,0:T(8,128)} fusion(bf16[768,512]{1,0:T(8,128)(2,1)} %get-tuple-element.27, bf16[512,3072]{1,0:T(8,128)(2,1)S(1)} %copy-done.8), kind=kOutput, calls=%fused_computation.12 | convolution fusion | flops 2415919104 | bytes 13369344 | tf_op jit(solution)/shard_map/dot_general | solution.py:41
  260.3 0.6 copy-done.7
  260.9 0.2 copy-done.4
  261.1 0.3 reshape.98
  261.5 0.5 reduce_sum.9
  262.0 0.6 dynamic-slice
  263.2 0.6 convolution_bitcast_fusion
  263.8 45.2 %all-reduce.2 = (f32[32,12]{0,1:T(8,128)}, f32[768]{0:T(1024)}) all-reduce(f32[32,12]{0,1:T(8,128)S(1)} %convolution_bitcast_fusion, f32[768]{0:T(1024)S(1)} %reduce.1), channel_id=1, replica_groups=mesh['section'=4,'dp'=8] {'section','dp'}, use_global_device_ids=true, to_apply=%region_4.5 | all-reduce | flops 1152 | bytes 9216 | tf_op jit(solution)/shard_map/psum | solution.py:873
  309.0 12.3 %all-reduce.1 = f32[768]{0:T(1024)S(1)} all-reduce(f32[768]{0:T(1024)S(1)} %reduce), channel_id=4, replica_groups=mesh['section'=4,'dp'=8] {'dp'}, use_global_device_ids=true, to_apply=%region_2.3.clone | all-reduce | flops 768 | bytes 6144
  321.3 0.6 dynamic-slice_bitcast_fusion
  321.9 1.2 slice_bitcast_fusion
  323.1 152.6 %all-reduce.5.cloned.1.call-done = f32[768,128]{1,0:T(8,128)} async-done(((f32[768,128]{1,0:T(8,128)}), f32[768,128]{1,0:T(8,128)}) %all-reduce.5.cloned.1.call-update) | async-done | bytes 393232 | tf_op jit(solution)/shard_map/psum | solution.py:873
  475.7 0.6 copy.37
  476.3 0.7 copy.38
  477.0 1.8 copy.39
  (29 shorter events, 0.3 us)
Async XLA Ops:
  8.0 467.7 %all-reduce.5.cloned.1.call-start = ((), (), s32[]{:S(2)}) async-start(), calls=%async_computation.4 | async-start | bytes 786432 | tf_op jit(solution)/shard_map/psum | solution.py:873
  236.4 2.4 copy-start.1
  236.5 239.2 %reduce-scatter.3.cloned.1.call-start = ((), (), s32[]{:S(2)}) async-start(), calls=%async_computation.2 | async-start | bytes 10616832 | tf_op jit(solution)/shard_map/reduce_scatter | solution.py:865
  236.5 2.6 copy-start
  252.1 1.9 copy-start.8
  252.1 223.6 %reduce-scatter.5.cloned.1.call-start = ((), (), s32[]{:S(2)}) async-start(), calls=%async_computation.3 | async-start | bytes 10616832 | tf_op jit(solution)/shard_map/reduce_scatter | solution.py:866
  260.2 0.7 copy-start.7
  260.2 0.7 copy-start.6
  260.2 0.9 copy-start.4
  260.2 1.8 copy-start.9
  260.2 3.0 copy-start.2
  260.2 215.5 %copy-start.5 = (bf16[128,128]{1,0:T(8,128)(2,1)S(1)}, bf16[128,128]{1,0:T(8,128)(2,1)}, u32[]{:S(2)}) copy-start(bf16[128,128]{1,0:T(8,128)(2,1)} %get-tuple-element.21) | copy-start | bytes 98308
  260.2 216.1 %copy-start.3 = (f32[128,768]{1,0:T(8,128)S(1)}, f32[128,768]{1,0:T(8,128)}, u32[]{:S(2)}) copy-start(f32[128,768]{1,0:T(8,128)} %get-tuple-element.23) | copy-start | bytes 1179652
Sparse Core Ops, SparseCore 0:
  236.6 239.0 all-reduce.4
Sparse Core Ops, SparseCore 1:
  252.2 103.1 reduce-scatter.2
  358.1 98.2 reduce-scatter.4

commit v2 on v1

v2 whole, which is shorter than its diff:
```python
import functools
import math
import types

import jax
import jax.numpy as jnp
import numpy as np
from jax import lax
from jax.experimental import pallas as pl
from jax.experimental.pallas import tpu as pltpu
from jax.sharding import PartitionSpec as P

H = 12
DH = 64
DOC_LEN = 128
EPS_NORM = 1e-06
MASK_FILL = -1000000000.0
HIGHEST = lax.Precision.HIGHEST
MESH = pl.DeviceIdType.MESH
F32 = jnp.float32
BF16 = jnp.bfloat16
VMEM = pltpu.VMEM
GELU_C = math.sqrt(2.0 / math.pi)
GELU_A = 0.044715
FF_STEP = 512
LEND_STEP = 128


def bucket_table(query_len):
    places = np.arange(query_len)
    relative = places[None, :] - places[:, None]
    distance = np.abs(relative)
    signed_part = np.where(relative > 0, 16, 0)
    far_bucket = 8 + np.floor(np.log(np.maximum(distance, 1) / 8.0) / np.log(16.0) * 8.0).astype(
        np.int64
    )
    far_bucket = np.minimum(far_bucket, 15)
    return (signed_part + np.where(distance < 8, distance, far_bucket)).astype(np.int32)


def nn(a, b):
    return jnp.dot(a, b, preferred_element_type=F32)


def nt(a, b):
    return lax.dot_general(a, b, (((1,), (1,)), ((), ())), preferred_element_type=F32)


def tn(a, b):
    return lax.dot_general(a, b, (((0,), (0,)), ((), ())), preferred_element_type=F32)


def rms_inverse(values):
    return lax.rsqrt(jnp.mean(values * values, axis=-1, keepdims=True) + EPS_NORM)


def rms_back(scaled, inverse, gain, grad):
    inner = grad * gain
    grad_values = inverse * (inner - scaled * jnp.mean(inner * scaled, axis=-1, keepdims=True))
    return grad_values, jnp.sum(grad * scaled, axis=0, keepdims=True)


def sum_order(line):
    orders = []
    for place in range(line):
        others = [j for j in range(line) if j != place]
        others.sort(key=lambda j: (-abs(j - place), min(j, line - 1 - j)))
        orders.append(others + [place])
    return orders


class Sizes:
    def __init__(self, sections, dp_size, batch_size, query_len, retrieved, width, ff, vector, doc_rows):
        self.sections = sections
        self.dp_size = dp_size
        self.batch_size = batch_size
        self.query_len = query_len
        self.retrieved = retrieved
        self.width = width
        self.ff = ff
        self.vector = vector
        self.doc_rows = doc_rows
        self.rows = batch_size * query_len
        self.total = sections * self.rows
        self.parts = ff // 4 // LEND_STEP
        self.share = width // dp_size
        self.summed = self.share % 16 == 0 and dp_size % 2 == 0
        self.line = dp_size // 2
        self.step_columns = H * DH
        self.per_slab = ff // self.step_columns
        self.units = 2 * self.per_slab
        self.steps = self.line * self.units


def relay_kernel(z, names, *refs):
    r = types.SimpleNamespace(**dict(zip(names, refs, strict=True)))
    s = lax.axis_index("section")
    d = lax.axis_index("dp")
    sections, dp_size, rows, width, ff = z.sections, z.dp_size, z.rows, z.width, z.ff
    batch_size, query_len, parts = z.batch_size, z.query_len, z.parts
    head_width = H * DH
    last = sections - 1
    after = lax.rem(s + 1, sections)
    before = lax.rem(s + sections - 1, sections)
    group = d - lax.rem(d, 4)
    place = lax.rem(d, 4)
    core_peer = group + place + 1 - 2 * lax.rem(place, 2)
    far_place = lax.rem(place + 2, 4)
    far_peer = group + far_place
    is_attention = lax.rem(s, 2) == 0
    is_ffn = jnp.logical_not(is_attention)

    def copy(src, dst, send_sem, recv_sem, section, dp):
        return pltpu.make_async_remote_copy(
            src_ref=src,
            dst_ref=dst,
            send_sem=send_sem,
            recv_sem=recv_sem,
            device_id=(section, dp),
            device_id_type=MESH,
        )

    def block(m):
        return pl.ds(pl.multiple_of(m * rows, rows), rows)

    def peers(body):
        def step(k, carry):
            body(lax.rem(d + k, dp_size))
            return carry

        lax.fori_loop(1, dp_size, step, 0)

    def other_sections(body):
        for k in range(1, sections):
            body(lax.rem(s + k, sections))

    def main_load():
        return pltpu.make_async_copy(r.main_hbm.at[0], r.main, r.load_sem.at[0])

    def side_load():
        return pltpu.make_async_copy(r.side_hbm.at[0], r.side, r.load_sem.at[1])

    main_load().start()

    @pl.when(is_ffn)
    def _():
        side_load().start()

    barrier = pltpu.get_barrier_semaphore()
    other_sections(
        lambda to: pl.semaphore_signal(barrier, inc=1, device_id=(to, d), device_id_type=MESH)
    )
    peers(lambda to: pl.semaphore_signal(barrier, inc=1, device_id=(s, to), device_id_type=MESH))

    lane = lax.broadcasted_iota(jnp.int32, (1, rows), 1)
    token_query = lane // query_len
    token_slot = lax.rem(lane, query_len)
    length = jnp.zeros((1, rows), jnp.int32)
    for q in range(batch_size):
        length = jnp.where(token_query == q, r.lengths[q], length)
    live = jnp.where(token_slot < length, 1.0, 0.0)
    r.meta[...] = jnp.zeros_like(r.meta)
    r.meta[0:1, :] = live
    r.meta[1:2, :] = live / length.astype(F32)
    r.idx[:8, :] = jnp.zeros((8, rows), jnp.int32)
    for c in range(batch_size):
        r.idx[c : c + 1, :] = jnp.full((1, rows), r.labels[c], jnp.int32)
    r.idx[8:, :] = r.chosen[...].T

    pl.semaphore_wait(barrier, sections - 1 + dp_size - 1)

    def lend_columns(quarter, part):
        start = quarter * (ff // 4) + part * LEND_STEP
        return pl.ds(pl.multiple_of(start, LEND_STEP), LEND_STEP)

    def lend_copy(part):
        columns = lend_columns(place, part)
        return copy(
            r.side_hbm.at[0, :, columns],
            r.lent.at[:, columns],
            r.lend_ss.at[0, part],
            r.lend_rs.at[0, part],
            after,
            d,
        )

    def lend_forward(kind, quarter, part, peer):
        columns = lend_columns(quarter, part)
        return copy(
            r.lent.at[:, columns],
            r.lent.at[:, columns],
            r.lend_ss.at[kind, part],
            r.lend_rs.at[kind, part],
            s,
            peer,
        )

    def state_copy(m):
        return copy(r.xout.at[m], r.xin.at[m], r.state_ss.at[m], r.state_rs.at[m], after, d)

    def grad_copy(m):
        return copy(r.gout.at[m], r.gin.at[m], r.grad_ss.at[m], r.grad_rs.at[m], before, d)

    def meta_copy(to, slot):
        return copy(r.meta, r.meta_rx.at[slot], r.meta_ss.at[to], r.meta_rs.at[slot], to, d)

    def idx_copy(slot):
        return copy(r.idx, r.idx_rx.at[slot], r.idx_ss, r.idx_rs.at[slot], last, d)

    def hid_copy(slot):
        return copy(r.hid, r.xin.at[slot], r.state_ss.at[sections], r.state_rs.at[slot], 0, d)

    def unit_copy(m, to):
        return copy(r.unit_tx.at[m], r.unit_rx, r.unit_ss.at[m], r.unit_rs, to, d)

    def loss_copy(m, to):
        return copy(r.loss_tx.at[m], r.loss_rx, r.loss_ss.at[m], r.loss_rs, to, d)

    def fin_copy(m, to):
        return copy(r.gout.at[m], r.fin_rx, r.fin_ss.at[m], r.fin_rs, to, d)

    def table_rows(owner):
        return pl.ds(pl.multiple_of(owner * z.doc_rows, z.doc_rows), z.doc_rows)

    def table_copy(to, owner):
        return copy(
            r.docs, r.table.at[table_rows(owner), :], r.tab_ss.at[to], r.tab_rs.at[owner], s, to
        )

    @pl.when(s != 0)
    def _():
        hid_copy(s).start()

    @pl.when(s == 0)
    def _():
        r.xin[0] = r.hid[...]

    other_sections(lambda to: meta_copy(to, s).start())
    r.meta_rx[s] = r.meta[...]

    @pl.when(s != last)
    def _():
        idx_copy(s).start()

    @pl.when(is_attention)
    def _():
        for part in range(parts):
            lend_copy(part).start()

    r.small[...] = jnp.zeros_like(r.small)
    r.tab_grad[...] = jnp.zeros_like(r.tab_grad)
    r.dproj[...] = jnp.zeros_like(r.dproj)
    r.dbias[...] = jnp.zeros_like(r.dbias)
    at_gain = slice(0, width)
    at_fgain = slice(width, 2 * width)
    gain = r.gain[...]
    fgain = r.fgain[...].reshape(1, width)

    def wait_meta(m):
        @pl.when(m != s)
        def _():
            meta_copy(0, m).wait_recv()

    def load_state(m):
        states = r.xin[m].astype(F32)
        inverse = rms_inverse(states)
        return states, inverse, states * inverse

    low_half = lax.broadcasted_iota(jnp.int32, (1, 128), 1) < DH

    def half_of(value, upper):
        keep = jnp.logical_not(low_half) if upper else low_half
        return jnp.where(keep, value.astype(F32), 0.0).astype(BF16)

    def attention_setup():
        buckets = r.buckets[...]
        for h in range(H):
            total = jnp.zeros(buckets.shape, F32)
            for b in range(32):
                total = jnp.where(buckets == b, r.bias[b : b + 1, h : h + 1], total)
            r.bias_sc[h] = total

    def attention_table():
        buckets = r.buckets[...]
        head_lane = lax.broadcasted_iota(jnp.int32, (32, 128), 1)

        def head(h, carry):
            grad = r.dbias[h]
            by_bucket = jnp.concatenate(
                [
                    jnp.sum(jnp.where(buckets == b, grad, 0.0), axis=0, keepdims=True)
                    for b in range(32)
                ],
                axis=0,
            )
            column = jnp.sum(by_bucket, axis=1, keepdims=True)
            r.tab_grad[...] += jnp.where(head_lane == h, column, 0.0)
            return carry

        lax.fori_loop(0, H, head, 0)

    def attention_forward(m):
        states, inverse, scaled = load_state(m)
        normed = scaled * gain
        r.left[0, :, block(m)] = normed.T.astype(BF16)
        normed_low = normed.astype(BF16)
        for start in range(0, 3 * head_width, head_width):
            r.qkv[block(m), start : start + head_width] = nn(
                normed_low, r.main[:, start : start + head_width]
            ).astype(BF16)
        live = r.meta_rx[m, 0:1, :] > 0.5
        row_query = lax.broadcasted_iota(jnp.int32, (rows, rows), 0) // query_len
        column_query = lax.broadcasted_iota(jnp.int32, (rows, rows), 1) // query_len
        keep = jnp.logical_and(row_query == column_query, live)
        for pair in range(H // 2):
            at = pair * 128
            query = r.qkv[block(m), at : at + 128]
            keys = r.qkv[block(m), head_width + at : head_width + at + 128]
            values = r.qkv[block(m), 2 * head_width + at : 2 * head_width + at + 128]
            contexts = []
            for upper in (0, 1):
                h = 2 * pair + upper
                raw = nt(half_of(query, upper), keys)
                biased = raw.reshape(batch_size, query_len, rows) + r.bias_sc[h][None]
                scores = jnp.where(keep, biased.reshape(rows, rows), MASK_FILL)
                top = jnp.max(scores, axis=-1, keepdims=True)
                grown = jnp.exp(scores - top)
                soft = grown / jnp.sum(grown, axis=-1, keepdims=True)
                r.probs[m, h] = soft
                contexts.append(nn(soft.astype(BF16), values))
            r.right[0, block(m), 3 * head_width + at : 3 * head_width + at + 128] = jnp.where(
                low_half, contexts[0], contexts[1]
            ).astype(BF16)
        context = r.right[0, block(m), 3 * head_width :]
        return states + nt(context, r.main[:, 3 * head_width :])

    def attention_backward(m):
        states, inverse, scaled = load_state(m)
        grad_low = r.gin[m]
        grad = grad_low.astype(F32)
        r.left[1, :, block(m)] = grad.T.astype(BF16)
        grad_context = nn(grad_low, r.main[:, 3 * head_width :]).astype(BF16)
        for pair in range(H // 2):
            at = pair * 128
            query = r.qkv[block(m), at : at + 128]
            keys = r.qkv[block(m), head_width + at : head_width + at + 128]
            values = r.qkv[block(m), 2 * head_width + at : 2 * head_width + at + 128]
            grad_pair = grad_context[:, at : at + 128]
            found = []
            for upper in (0, 1):
                h = 2 * pair + upper
                soft = r.probs[m, h]
                grad_soft = nt(half_of(grad_pair, upper), values)
                moved = soft * grad_soft
                grad_scores = moved - soft * jnp.sum(moved, axis=-1, keepdims=True)
                r.dbias[h] += jnp.sum(grad_scores.reshape(batch_size, query_len, rows), axis=0)
                scores_low = grad_scores.astype(BF16)
                found.append(
                    (
                        nn(scores_low, keys),
                        tn(scores_low, query),
                        tn(soft.astype(BF16), grad_pair),
                    )
                )
            for third in range(3):
                start = third * head_width + at
                r.right[0, block(m), start : start + 128] = jnp.where(
                    low_half, found[0][third], found[1][third]
                ).astype(BF16)
        grad_normed = nt(r.right[0, block(m), : 3 * head_width], r.main[:, : 3 * head_width])
        grad_states, grad_gain = rms_back(scaled, inverse, gain, grad_normed)
        r.small[:, at_gain] += grad_gain
        return grad + grad_states

    def ffn_forward(m):
        states, inverse, scaled = load_state(m)
        normed = scaled * gain
        r.left[0, :, block(m)] = normed.T.astype(BF16)
        normed_low = normed.astype(BF16)
        outputs = states
        for start in range(0, ff, FF_STEP):
            columns = slice(start, start + FF_STEP)
            gate = nn(normed_low, r.main[:, columns])
            up = nn(normed_low, r.lent[:, columns])
            square = gate * gate
            bent = jnp.tanh(GELU_C * gate * (1.0 + GELU_A * square))
            half = 0.5 * (1.0 + bent)
            smooth = gate * half
            slope = half + 0.5 * gate * (1.0 - bent * bent) * (
                GELU_C * (1.0 + 3.0 * GELU_A * square)
            )
            hidden = (smooth * up).astype(BF16)
            r.right[1, block(m), columns] = hidden
            r.right[0, block(m), columns] = (slope * up).astype(BF16)
            r.right[2, block(m), columns] = smooth.astype(BF16)
            outputs = outputs + nt(hidden, r.side[:, columns])
        return outputs

    def ffn_backward(m, grad):
        states, inverse, scaled = load_state(m)
        grad_low = grad.astype(BF16)
        r.left[1, :, block(m)] = grad.T.astype(BF16)
        grad_normed = jnp.zeros((rows, width), F32)
        for start in range(0, ff, FF_STEP):
            columns = slice(start, start + FF_STEP)
            grad_hidden = nn(grad_low, r.side[:, columns])
            grad_gate = (grad_hidden * r.right[0, block(m), columns].astype(F32)).astype(BF16)
            grad_up = (grad_hidden * r.right[2, block(m), columns].astype(F32)).astype(BF16)
            r.right[0, block(m), columns] = grad_gate
            r.right[2, block(m), columns] = grad_up
            grad_normed = (
                grad_normed
                + nt(grad_gate, r.main[:, columns])
                + nt(grad_up, r.lent[:, columns])
            )
        grad_states, grad_gain = rms_back(scaled, inverse, gain, grad_normed)
        r.small[:, at_gain] += grad_gain
        return grad + grad_states

    def count_hits(m):
        for c in range(batch_size):
            base = r.idx_rx[m, c : c + 1, :] * DOC_LEN
            numbers = lax.broadcasted_iota(jnp.int32, (DOC_LEN, rows), 0) + base
            total = jnp.zeros((DOC_LEN, rows), F32)
            for k in range(z.retrieved):
                total = total + jnp.where(r.idx_rx[m, 8 + k : 9 + k, :] == numbers, 1.0, 0.0)
            r.counts[m, c * DOC_LEN : (c + 1) * DOC_LEN, :] = total

    def pick_docs(m):
        for c in range(batch_size):
            label = r.idx_rx[m, c : c + 1, :]

            def pick(t, picked):
                here = r.table[pl.ds(pl.multiple_of(t * DOC_LEN, DOC_LEN), DOC_LEN), :].astype(F32)
                return jnp.where(label == t, here, picked)

            picked = lax.fori_loop(
                0, dp_size * z.doc_rows // DOC_LEN, pick, jnp.zeros((DOC_LEN, z.vector), F32)
            )
            r.own_docs[m, c * DOC_LEN : (c + 1) * DOC_LEN, :] = picked.astype(BF16)

    def loss_and_grad(m, unit):
        docs = r.own_docs[m]
        sims = nt(docs, unit)
        count = r.counts[m]
        imputed = jnp.sum(count * sims, axis=0, keepdims=True) / z.retrieved
        grown = count * jnp.exp(sims)
        imputed_mass = jnp.exp(imputed)
        mass = imputed_mass + jnp.concatenate(
            [
                jnp.sum(grown[c * DOC_LEN : (c + 1) * DOC_LEN], axis=0, keepdims=True)
                for c in range(batch_size)
            ],
            axis=0,
        )
        weighted = jnp.log(mass) * r.meta_rx[m, 1:2, :]
        candidate = lax.broadcasted_iota(jnp.int32, (batch_size, 1), 0)
        losses = jnp.zeros((1, rows), F32)
        grad_tokens = jnp.zeros((batch_size, rows), F32)
        for q in range(batch_size):
            own = token_query == q
            score = jnp.sum(jnp.where(own, weighted, 0.0), axis=1, keepdims=True)
            top = jnp.max(score, axis=0, keepdims=True)
            risen = jnp.exp(score - top)
            total = jnp.sum(risen, axis=0, keepdims=True)
            chosen_one = (candidate == q).astype(F32)
            loss = top + jnp.log(total) - jnp.sum(score * chosen_one, axis=0, keepdims=True)
            losses = losses + jnp.where(lane == q, loss, 0.0)
            grad_tokens = grad_tokens + jnp.where(own, risen / total - chosen_one, 0.0)
        grad_mass = grad_tokens * r.meta_rx[m, 1:2, :] / mass
        shared = jnp.sum(grad_mass, axis=0, keepdims=True) * imputed_mass / z.retrieved
        grad_sims = count * shared + jnp.concatenate(
            [
                grown[c * DOC_LEN : (c + 1) * DOC_LEN] * grad_mass[c : c + 1]
                for c in range(batch_size)
            ],
            axis=0,
        )
        high = grad_sims.astype(BF16)
        rest = (grad_sims - high.astype(F32)).astype(BF16)
        return losses, tn(high, docs) + tn(rest, docs)

    def finish_states(m, states):
        inverse = rms_inverse(states)
        scaled = states * inverse
        normed = (scaled * fgain).astype(BF16)
        projected = nn(normed, r.proj[...])
        size = lax.rsqrt(jnp.sum(projected * projected, axis=-1, keepdims=True) + EPS_NORM)
        exact = projected * size
        unit = exact.astype(BF16)
        losses, grad_unit = loss_and_grad(m, unit)
        r.unit_tx[m] = unit
        r.loss_tx[m] = jnp.broadcast_to(losses, (8, rows))

        @pl.when(m != last)
        def _():
            unit_copy(m, m).start()
            loss_copy(m, m).start()

        grad_projected = (
            size * (grad_unit - exact * jnp.sum(grad_unit * exact, axis=-1, keepdims=True))
        ).astype(BF16)
        r.dproj[...] += tn(normed, grad_projected)
        grad_normed = nt(grad_projected, r.proj[...])
        grad_states, grad_gain = rms_back(scaled, inverse, fgain, grad_normed)
        r.small[:, at_fgain] += grad_gain
        return grad_states

    def loop(body):
        def step(m, carry):
            body(m)
            return carry

        lax.fori_loop(0, sections, step, 0)

    def wait_state(m):
        @pl.when(jnp.logical_or(s != 0, m != 0))
        def _():
            state_copy(m).wait_recv()

    @pl.when(is_attention)
    def _():
        attention_setup()
        main_load().wait()

        def forward(m):
            wait_meta(m)
            wait_state(m)
            r.xout[m] = attention_forward(m).astype(BF16)
            state_copy(m).start()

        loop(forward)

        def backward(m):
            grad_copy(m).wait_recv()
            r.gout[m] = attention_backward(m).astype(BF16)

            @pl.when(s != 0)
            def _():
                grad_copy(m).start()

            @pl.when(jnp.logical_and(s == 0, m != 0))
            def _():
                fin_copy(m, m).start()

        loop(backward)
        attention_table()

    @pl.when(is_ffn)
    def _():
        for part in range(parts):
            lend_copy(part).wait_recv()
            lend_forward(1, place, part, core_peer).start()
            lend_forward(2, place, part, far_peer).start()

        @pl.when(s == last)
        def _():
            r.idx_rx[last] = r.idx[...]
            r.table[table_rows(d), :] = r.docs[...]
            peers(lambda to: table_copy(to, d).start())

            def prepare(m):
                @pl.when(m != last)
                def _():
                    idx_copy(m).wait_recv()

                count_hits(m)

            loop(prepare)

        for part in range(parts):
            lend_forward(2, far_place, part, far_peer).wait_recv()
            lend_forward(3, far_place, part, core_peer).start()
        for part in range(parts):
            lend_forward(1, place, part, core_peer).wait_recv()
            lend_forward(3, far_place, part, core_peer).wait_recv()
        main_load().wait()
        side_load().wait()

        @pl.when(s == last)
        def _():
            peers(lambda owner: table_copy(owner, owner).wait_recv())
            loop(pick_docs)
            loop(wait_meta)

            def both(m):
                wait_state(m)
                states = ffn_forward(m)
                grad = finish_states(m, states)
                r.gout[m] = ffn_backward(m, grad).astype(BF16)
                grad_copy(m).start()

            loop(both)

        @pl.when(s != last)
        def _():
            def forward(m):
                wait_state(m)
                r.xout[m] = ffn_forward(m).astype(BF16)
                state_copy(m).start()

            loop(forward)

            def backward(m):
                grad_copy(m).wait_recv()
                r.gout[m] = ffn_backward(m, r.gin[m].astype(F32)).astype(BF16)
                grad_copy(m).start()

            loop(backward)
            loop(wait_meta)

        for part in range(parts):
            lend_forward(1, place, part, core_peer).wait_send()
            lend_forward(2, place, part, far_peer).wait_send()
            lend_forward(3, far_place, part, core_peer).wait_send()

    if z.summed:
        sum_gradients(z, r, s, d, copy, peers, other_sections, is_attention)

    other_sections(lambda to: meta_copy(to, s).wait_send())

    @pl.when(s != 0)
    def _():
        hid_copy(s).wait_send()
        fin_copy(0, s).wait_recv()
        r.dx[...] = r.fin_rx[...].astype(F32).reshape(batch_size, query_len, width)
        loop(lambda m: grad_copy(m).wait_send())

    @pl.when(s == 0)
    def _():
        r.dx[...] = r.gout[0].astype(F32).reshape(batch_size, query_len, width)
        for m in range(1, sections):
            fin_copy(m, m).wait_send()

    @pl.when(is_attention)
    def _():
        for part in range(parts):
            lend_copy(part).wait_send()

    def write_own(unit, losses):
        r.units[...] = unit.reshape(batch_size, query_len, z.vector)
        r.loss[...] = losses

    @pl.when(s != last)
    def _():
        idx_copy(s).wait_send()
        loop(lambda m: state_copy(m).wait_send())
        unit_copy(0, s).wait_recv()
        loss_copy(0, s).wait_recv()
        write_own(r.unit_rx[...], r.loss_rx[...])

    @pl.when(s == last)
    def _():
        peers(lambda to: table_copy(to, d).wait_send())
        for m in range(sections - 1):
            unit_copy(m, m).wait_send()
            loss_copy(m, m).wait_send()
        write_own(r.unit_tx[last], r.loss_tx[last])


def sum_gradients(z, r, s, d, copy, peers, other_sections, is_attention):
    sections, dp_size, width, ff, share, line = z.sections, z.dp_size, z.width, z.ff, z.share, z.line
    step_columns, per_slab, units, steps = z.step_columns, z.per_slab, z.units, z.steps
    place = d // 2
    core = lax.rem(d, 2)
    peer = d + 1 - 2 * core
    last = sections - 1
    before = lax.rem(s + sections - 1, sections)
    is_ffn = jnp.logical_not(is_attention)
    orders = sum_order(line)

    def piece_rows(owner):
        return pl.ds(pl.multiple_of(owner * share, share), share)

    def small_copies(to, slot):
        return (
            copy(r.small, r.small_rx.at[slot], r.small_ss.at[0, to], r.small_rs.at[0, slot], s, to),
            copy(r.tab_grad, r.tab_rx.at[slot], r.small_ss.at[1, to], r.small_rs.at[1, slot], s, to),
        )

    def proj_copy(to, slot):
        return copy(
            r.dproj.at[piece_rows(to), :],
            r.proj_rx.at[slot],
            r.proj_ss.at[to],
            r.proj_rs.at[slot],
            s,
            to,
        )

    def column_copies(to, slot):
        return (
            copy(
                r.small_tx, r.small_cx.at[slot], r.column_ss.at[0, to], r.column_rs.at[0, slot], to, d
            ),
            copy(r.tab_tx, r.tab_cx.at[slot], r.column_ss.at[1, to], r.column_rs.at[1, slot], to, d),
        )

    def piece_copy(to):
        rows = piece_rows(d)
        return copy(
            r.proj_out.at[rows, :], r.proj_out.at[rows, :], r.piece_ss.at[to], r.piece_rs, to, d
        )

    def spread_copy(to, owner):
        rows = piece_rows(owner)
        return copy(
            r.proj_out.at[rows, :],
            r.proj_out.at[rows, :],
            r.spread_ss.at[to],
            r.spread_rs.at[owner],
            s,
            to,
        )

    def each(copies, action):
        for one in copies:
            getattr(one, action)()

    def total_of(ref, count):
        total = ref[0]
        for k in range(1, count):
            total = total + ref[k]
        return total

    def small_first():
        peers(lambda to: each(small_copies(to, d), "start"))
        r.small_rx[d] = r.small[...]
        r.tab_rx[d] = r.tab_grad[...]

        @pl.when(s == last)
        def _():
            peers(lambda to: proj_copy(to, d).start())
            r.proj_rx[d] = r.dproj[piece_rows(d), :]

    def small_second():
        peers(lambda owner: each(small_copies(owner, owner), "wait_recv"))
        r.small_tx[...] = total_of(r.small_rx, dp_size)
        r.tab_tx[...] = total_of(r.tab_rx, dp_size)
        r.small_cx[s] = r.small_tx[...]
        r.tab_cx[s] = r.tab_tx[...]
        other_sections(lambda to: each(column_copies(to, s), "start"))

        @pl.when(s == last)
        def _():
            peers(lambda owner: proj_copy(owner, owner).wait_recv())
            r.proj_out[piece_rows(d), :] = total_of(r.proj_rx, dp_size)
            for to in range(sections - 1):
                piece_copy(to).start()
            peers(lambda to: spread_copy(to, d).start())

    def small_third():
        other_sections(lambda to: each(column_copies(to, to), "wait_recv"))
        r.fgain_out[...] = total_of(r.small_cx, sections)[:, width:]
        r.table_out[...] = total_of(r.tab_cx, sections)[:, :H]
        r.gain_out[...] = pltpu.roll(
            jnp.broadcast_to(r.small_tx[:, :width], (8, width)), width - d * share, 1
        )[0:1, :share]

        @pl.when(s != last)
        def _():
            piece_copy(0).wait_recv()
            peers(lambda to: spread_copy(to, d).start())

    def small_last():
        peers(lambda owner: spread_copy(owner, owner).wait_recv())
        peers(lambda to: spread_copy(to, d).wait_send())
        peers(lambda to: each(small_copies(to, d), "wait_send"))
        other_sections(lambda to: each(column_copies(to, s), "wait_send"))

        @pl.when(s == last)
        def _():
            peers(lambda to: proj_copy(to, d).wait_send())
            for to in range(sections - 1):
                piece_copy(to).wait_send()

    def target(i):
        found = jnp.int32(0)
        for k in range(line):
            found = jnp.where(place == k, orders[k][i], found)
        return found

    targets = [target(i) for i in range(line)]

    def parts_of(t):
        i, u = t // units, lax.rem(t, units)
        j = targets[0]
        for k in range(1, line):
            j = jnp.where(i == k, targets[k], j)
        slab, column = lax.rem(u, 2), u // 2
        columns = pl.ds(pl.multiple_of(column * step_columns, step_columns), step_columns)
        return j, u, slab, column, columns

    def core_copy(t):
        return copy(
            r.core_tx.at[lax.rem(t, 4)], r.core_rx.at[t], r.core_ss.at[t], r.core_rs.at[t], s, peer
        )

    def up_core_copy(k):
        return copy(
            r.up_core_tx.at[lax.rem(k, 4)], r.up_rx.at[k], r.up_core_ss.at[k], r.up_rs.at[k], s, peer
        )

    def up_copy(k):
        return copy(
            r.up_tx.at[lax.rem(k, 4)], r.up_rx.at[k], r.up_ss.at[k], r.up_rs.at[k], before, d
        )

    def line_view(t):
        row = pl.ds(pl.multiple_of(lax.rem(t, dp_size) * share, share), share)
        column = pl.ds(pl.multiple_of(t // dp_size * step_columns, step_columns), step_columns)
        return r.lent.at[row, column]

    def line_copy(t, way, j, u, to):
        slot = j - 1 + way
        return copy(
            line_view(t),
            r.line_rx.at[way, slot, u],
            r.line_ss.at[t],
            r.line_rs.at[way, slot, u],
            s,
            to * 2 + core,
        )

    def theirs(j):
        return pl.ds(pl.multiple_of((j * 2 + 1 - core) * share, share), share)

    def ours(j):
        return pl.ds(pl.multiple_of((j * 2 + core) * share, share), share)

    def begin(t):
        j, u, slab, column, columns = parts_of(t)
        k = t // 2
        mixed = jnp.logical_and(is_attention, column == per_slab - 1)
        which = jnp.where(jnp.logical_or(slab == 1, mixed), 1, 0)

        @pl.when(jnp.logical_or(is_ffn, slab == 0))
        def _():
            right = r.right[slab, :, columns]

            @pl.when(t >= 4)
            def _():
                core_copy(t - 4).wait_send()

            r.core_tx[lax.rem(t, 4)] = nn(r.left[which, theirs(j), :], right).astype(BF16)
            core_copy(t).start()
            r.mine[lax.rem(t, 2)] = nn(r.left[which, ours(j), :], right)

        @pl.when(jnp.logical_and(is_ffn, slab == 1))
        def _():
            right = r.right[2, :, columns]

            @pl.when(k >= 4)
            def _():
                up_core_copy(k - 4).wait_send()

            r.up_core_tx[lax.rem(k, 4)] = nn(r.left[0, theirs(j), :], right).astype(BF16)
            up_core_copy(k).start()
            r.up_mine[...] = nn(r.left[0, ours(j), :], right)

    def finish(t):
        j, u, slab, column, columns = parts_of(t)
        k = t // 2
        total = r.mine.at[lax.rem(t, 2)]

        @pl.when(jnp.logical_or(is_ffn, slab == 0))
        def _():
            core_copy(t).wait_recv()
            total[...] += r.core_rx[t].astype(F32)

        @pl.when(jnp.logical_and(is_attention, slab == 1))
        def _():
            up_copy(k).wait_recv()
            total[...] = r.up_rx[k].astype(F32)

        @pl.when(jnp.logical_and(is_ffn, slab == 1))
        def _():
            up_core_copy(k).wait_recv()

            @pl.when(k >= 4)
            def _():
                up_copy(k - 4).wait_send()

            r.up_tx[lax.rem(k, 4)] = (r.up_mine[...] + r.up_rx[k].astype(F32)).astype(BF16)
            up_copy(k).start()

        way = jnp.where(j < place, 1, 0)

        @pl.when(jnp.logical_and(place > 0, j >= place))
        def _():
            line_copy(t, 0, j, u, place).wait_recv()
            total[...] += r.line_rx[0, j - 1, u].astype(F32)

        @pl.when(jnp.logical_and(place < line - 1, j <= place))
        def _():
            line_copy(t, 1, j, u, place).wait_recv()
            total[...] += r.line_rx[1, j, u].astype(F32)

        @pl.when(jnp.logical_and(j == place, slab == 0))
        def _():
            r.main_out[0, :, columns] = total[...]

        @pl.when(jnp.logical_and(j == place, slab == 1))
        def _():
            r.side_out[0, :, columns] = total[...]

        @pl.when(j != place)
        def _():
            line_view(t)[...] = total[...].astype(BF16)
            line_copy(t, way, j, u, place + 1 - 2 * way).start()

    small_first()
    begin(jnp.int32(0))

    def step(t, carry):
        @pl.when(t < steps)
        def _():
            begin(t)

        finish(t - 1)

        @pl.when(t == units)
        def _():
            small_second()

        @pl.when(t == steps - units)
        def _():
            small_third()

        return carry

    lax.fori_loop(1, steps + 1, step, 0)
    small_last()

    def drain(t, carry):
        line_copy(t, 0, 1, 0, place).wait_send()
        return carry

    lax.fori_loop(0, steps - units, drain, 0)

    def drain_core(t, carry):
        slab = lax.rem(t, 2)

        @pl.when(jnp.logical_or(is_ffn, slab == 0))
        def _():
            core_copy(t).wait_send()

        return carry

    lax.fori_loop(steps - 4, steps, drain_core, 0)

    @pl.when(is_ffn)
    def _():
        for k in range(steps // 2 - 4, steps // 2):
            up_core_copy(k).wait_send()
            up_copy(k).wait_send()


def relay(z, hid, lengths, labels, chosen, main, side, gain, bias, buckets, fgain, proj, docs):
    dma = pltpu.SemaphoreType.DMA
    shape = jax.ShapeDtypeStruct
    sections, rows, width, ff, dp_size = z.sections, z.rows, z.width, z.ff, z.dp_size
    share, steps, units = z.share, z.steps, z.units
    piece = (share, z.step_columns)
    vmem = pl.BlockSpec(memory_space=VMEM)
    smem = pl.BlockSpec(memory_space=pltpu.SMEM)
    anywhere = pl.BlockSpec(memory_space=pl.ANY)
    inputs = dict(
        hid=(hid, vmem),
        lengths=(lengths, smem),
        labels=(labels, smem),
        chosen=(chosen, vmem),
        main_hbm=(main, anywhere),
        side_hbm=(side, anywhere),
        gain=(gain, vmem),
        bias=(bias, vmem),
        buckets=(buckets, vmem),
        fgain=(fgain, vmem),
        proj=(proj, vmem),
        docs=(docs, vmem),
    )
    outputs = dict(
        units=shape((z.batch_size, z.query_len, z.vector), BF16),
        loss=shape((8, rows), F32),
        dx=shape((z.batch_size, z.query_len, width), F32),
    )
    scratch = dict(
        main=VMEM((width, ff), BF16),
        side=VMEM((width, ff), BF16),
        lent=VMEM((width, ff), BF16),
        xin=VMEM((sections, rows, width), BF16),
        xout=VMEM((sections, rows, width), BF16),
        gin=VMEM((sections, rows, width), BF16),
        gout=VMEM((sections, rows, width), BF16),
        meta=VMEM((8, rows), F32),
        meta_rx=VMEM((sections, 8, rows), F32),
        idx=VMEM((8 + z.retrieved, rows), jnp.int32),
        idx_rx=VMEM((sections, 8 + z.retrieved, rows), jnp.int32),
        own_docs=VMEM((sections, z.batch_size * DOC_LEN, z.vector), BF16),
        table=VMEM((dp_size * z.doc_rows, z.vector), BF16),
        counts=VMEM((sections, z.batch_size * DOC_LEN, rows), F32),
        qkv=VMEM((z.total, 3 * H * DH), BF16),
        probs=VMEM((sections, H, rows, rows), F32),
        bias_sc=VMEM((H, z.query_len, rows), F32),
        dbias=VMEM((H, z.query_len, rows), F32),
        fin_rx=VMEM((rows, width), BF16),
        unit_tx=VMEM((sections, rows, z.vector), BF16),
        unit_rx=VMEM((rows, z.vector), BF16),
        loss_tx=VMEM((sections, 8, rows), F32),
        loss_rx=VMEM((8, rows), F32),
        load_sem=dma((2,)),
        state_ss=dma((sections + 1,)),
        state_rs=dma((sections,)),
        grad_ss=dma((sections,)),
        grad_rs=dma((sections,)),
        meta_ss=dma((sections,)),
        meta_rs=dma((sections,)),
        idx_ss=dma,
        idx_rs=dma((sections,)),
        tab_ss=dma((dp_size,)),
        tab_rs=dma((dp_size,)),
        lend_ss=dma((4, z.parts)),
        lend_rs=dma((4, z.parts)),
        fin_ss=dma((sections,)),
        fin_rs=dma,
        unit_ss=dma((sections,)),
        unit_rs=dma,
        loss_ss=dma((sections,)),
        loss_rs=dma,
    )
    factors = dict(left=((2, width, z.total), BF16), right=((3, z.total, ff), BF16))
    partials = dict(
        small=((1, 2 * width), F32), tab_grad=((32, 128), F32), dproj=((width, z.vector), F32)
    )
    if z.summed:
        outputs |= dict(
            main_out=shape((1, share, ff), F32),
            side_out=shape((1, share, ff), F32),
            gain_out=shape((1, share), F32),
            table_out=shape((32, H), F32),
            fgain_out=shape((1, width), F32),
            proj_out=shape((width, z.vector), F32),
        )
        scratch |= {name: VMEM(*kind) for name, kind in (factors | partials).items()}
        scratch |= dict(
            mine=VMEM((2,) + piece, F32),
            up_mine=VMEM(piece, F32),
            core_tx=VMEM((4,) + piece, BF16),
            core_rx=VMEM((steps,) + piece, BF16),
            up_core_tx=VMEM((4,) + piece, BF16),
            up_tx=VMEM((4,) + piece, BF16),
            up_rx=VMEM((steps // 2,) + piece, BF16),
            line_rx=VMEM((2, z.line - 1, units) + piece, BF16),
            small_rx=VMEM((dp_size, 1, 2 * width), F32),
            small_tx=VMEM((1, 2 * width), F32),
            small_cx=VMEM((sections, 1, 2 * width), F32),
            tab_rx=VMEM((dp_size, 32, 128), F32),
            tab_tx=VMEM((32, 128), F32),
            tab_cx=VMEM((sections, 32, 128), F32),
            proj_rx=VMEM((dp_size, share, z.vector), F32),
            core_ss=dma((steps,)),
            core_rs=dma((steps,)),
            up_core_ss=dma((steps // 2,)),
            up_ss=dma((steps // 2,)),
            up_rs=dma((steps // 2,)),
            line_ss=dma((steps,)),
            line_rs=dma((2, z.line - 1, units)),
            small_ss=dma((2, dp_size)),
            small_rs=dma((2, dp_size)),
            column_ss=dma((2, sections)),
            column_rs=dma((2, sections)),
            proj_ss=dma((dp_size,)),
            proj_rs=dma((dp_size,)),
            piece_ss=dma((sections,)),
            piece_rs=dma,
            spread_ss=dma((dp_size,)),
            spread_rs=dma((dp_size,)),
        )
    else:
        outputs |= {name: shape(*kind) for name, kind in (factors | partials).items()}
    results = pl.pallas_call(
        functools.partial(relay_kernel, z, (*inputs, *outputs, *scratch)),
        out_shape=tuple(outputs.values()),
        in_specs=[spec for _, spec in inputs.values()],
        out_specs=(vmem,) * len(outputs),
        scratch_shapes=list(scratch.values()),
        compiler_params=pltpu.CompilerParams(
            collective_id=0, has_side_effects=True, vmem_limit_bytes=62 * 2**20
        ),
        name="relay",
    )(*[value for value, _ in inputs.values()])
    return types.SimpleNamespace(**dict(zip(outputs, results, strict=True)))


def sums_outside(z, out):
    head_width = H * DH
    section = lax.axis_index("section")
    is_attention = section % 2 == 0
    left, right = out.left, out.right
    second = jnp.where(is_attention, left[1], left[0])
    main_grad = jnp.concatenate(
        [nn(left[0], right[0, :, : 3 * head_width]), nn(second, right[0, :, 3 * head_width :])],
        axis=1,
    )
    up_grad = lax.ppermute(
        nn(left[0], right[2]).astype(BF16),
        "section",
        [(k, k - 1) for k in range(1, z.sections)],
    )
    side_grad = jnp.where(is_attention, up_grad.astype(F32), nn(left[1], right[1]))
    scatter = functools.partial(
        lax.psum_scatter, axis_name="dp", scatter_dimension=0, tiled=True
    )
    table, fgain, proj = lax.psum(
        (out.tab_grad[:, :H], out.small[0, z.width :], out.dproj), ("section", "dp")
    )
    return (
        scatter(main_grad)[None],
        scatter(side_grad)[None],
        scatter(out.small[0, : z.width])[None],
        table,
        fgain,
        proj,
    )


def per_device(
    hidden_in,
    lengths,
    labels,
    chosen,
    slab_main,
    slab_side,
    section_gains,
    rel_bias,
    final_gain,
    out_proj,
    doc_vectors,
):
    batch_size, query_len, width = hidden_in.shape
    rows = batch_size * query_len
    retrieved = chosen.shape[2]
    z = Sizes(
        lax.axis_size("section"),
        lax.axis_size("dp"),
        batch_size,
        query_len,
        retrieved,
        width,
        slab_main.shape[2],
        out_proj.shape[1],
        doc_vectors.shape[0],
    )
    buckets = jnp.asarray(np.tile(bucket_table(query_len), (1, batch_size)))
    out = relay(
        z,
        hidden_in.reshape(rows, width),
        lengths,
        labels,
        chosen.reshape(rows, retrieved),
        slab_main,
        slab_side,
        section_gains,
        rel_bias,
        buckets,
        final_gain,
        out_proj,
        doc_vectors,
    )
    if z.summed:
        sums = (
            out.main_out,
            out.side_out,
            out.gain_out,
            out.table_out,
            out.fgain_out[0],
            out.proj_out,
        )
    else:
        sums = sums_outside(z, out)
    return (out.units, out.loss[0, :batch_size], out.dx) + sums


def solution(mesh):
    both = ("section", "dp")
    in_specs = (
        P(both, None, None),
        P(both),
        P(both),
        P(both, None, None),
        P("section", None, None),
        P("section", None, None),
        P("section", None),
        P(),
        P(),
        P(),
        P("dp", None),
    )
    out_specs = (
        P(both, None, None),
        P(both),
        P(both, None, None),
        P("section", "dp", None),
        P("section", "dp", None),
        P("section", "dp"),
        P(),
        P(),
        P(),
    )
    return jax.shard_map(
        per_device, mesh=mesh, in_specs=in_specs, out_specs=out_specs, check_vma=False
    )
```

time: 489 us -> 236 us (0.48)
  waiting for transfers between devices: 153 us -> 0 us
  blocking collectives: 57.5 us -> 0 us
  between operations: 16.3 us -> 0.66 us
  matrix products: 14 us -> 0 us
  other arithmetic: 10.7 us -> 1.28 us
    psum x1 -> x0, waiting for transfers between devices: 153 us -> none  [per_device(): lax.psum((table_grad, fgain_grad[0], proj_grad), ('section', 'dp'))]
    psum x1 -> x0, blocking collectives: 45.2 us -> none  [per_device(): lax.psum((table_grad, fgain_grad[0], proj_grad), ('section', 'dp'))]
    dot_general x4 -> x0, matrix products: 14 us -> none  [the longest x3 13.4 us: nn(): return jnp.dot(a, b, preferred_element_type=F32)]
    unnamed x1 -> x0, blocking collectives: 12.3 us -> none
    concatenate x2 -> x0, other arithmetic: 8.77 us -> none  [the longest x1 8.11 us: per_device(): jnp.concatenate([nn(l1, r1[:, :3 * head_width]), nn(l2, r1[:, 3 * head_wi...]
    unnamed x25 -> x14, local copies, waits for them, and re-layouts: 7.99 us -> 10.7 us
  transfers between devices with their start and end apart: 3 -> 0, of which waited for: 1 -> 0; matrix products, arithmetic and copies ran while one was open for 5% -> 0% of each run, Pallas kernels for 0% -> 0%
where the time goes in v2:
time: 236 us; the launch traced here: 235 us
  Pallas kernels  221 us (94%)
  local copies, waits for them, and re-layouts  11.8 us (5%)
    pallas_call x1, Pallas kernels, relay(): pl.pallas_call(functools.partial(relay_kernel, z, (*inputs, *outputs, *sc...  221 us
    unnamed x14, local copies, waits for them, and re-layouts  10.7 us

profile of v2, /device:TPU:16, one launch (start us, length us, event | category | flops | bytes accessed | tf_op | source)
XLA Modules:
  0.0 234.7 jit_solution(6253793175409437473)
XLA Ops:
  0.6 1.4 copy.21.refs_7_
  2.0 220.9 %relay.1 = (bf16[4,32,128]{2,1,0:T(8,128)(2,1)}, f32[8,128]{1,0:T(8,128)}, f32[4,32,768]{2,1,0:T(8,128)}, f32[1,96,3072]{2,1,0:T(8,128)}, f32[1,96,3072]{2,1,0:T...) custom-call(bf16[128,768]{1,0:T(8,128)(2,1)} %bitcast.4, s32[4]{0:T(128)} %refs_1_.1, ...), custom_call_target="tpu_custom_call" | custom-call | tf_op jit(solution)/shard_map/relay/pallas_call | solution.py:1081
  222.9 1.2 slice_bitcast_fusion
  224.1 1.3 reduce
  225.4 1.4 copy.22
  226.8 1.4 copy.29
  228.1 1.8 copy.30
  229.9 0.0 copy-start
  229.9 2.5 %copy.31 = f32[1,96,3072]{2,1,0:T(8,128)} copy(f32[1,96,3072]{2,1,0:T(8,128)} %get-tuple-element.48) | data formatting | bytes 2359296
  232.4 0.0 copy-done
  232.4 0.0 copy-start.2
  232.4 0.0 copy-start.1
  232.4 1.0 copy.32
  233.4 0.0 copy-done.2
  233.4 0.5 copy.33
  233.9 0.0 copy-done.1
  233.9 0.7 copy.34
Async XLA Ops:
  229.9 2.5 %copy-start = (f32[1,96,3072]{2,1,0:T(8,128)S(1)}, f32[1,96,3072]{2,1,0:T(8,128)}, u32[]{:S(2)}) copy-start(f32[1,96,3072]{2,1,0:T(8,128)} %get-tuple-element.49) | copy-start | bytes 3538948
  232.4 1.0 copy-start.2
  232.4 1.5 copy-start.1

commit v3 on v2

--- a/solution.py
+++ b/solution.py
@@ -22,7 +22,7 @@
 VMEM = pltpu.VMEM
 GELU_C = math.sqrt(2.0 / math.pi)
 GELU_A = 0.044715
-FF_STEP = 512
+FF_STEP = 768
 LEND_STEP = 128
 
 
@@ -90,6 +90,10 @@
         self.per_slab = ff // self.step_columns
         self.units = 2 * self.per_slab
         self.steps = self.line * self.units
+        self.chunk = self.share if self.summed else H * 8
+        self.slab_chunks = ff // self.chunk
+        arriving = self.steps + 2 * (self.line - 1) * self.units
+        self.pool = max(3 * self.slab_chunks, arriving if self.summed else 0)
 
 
 def relay_kernel(z, names, *refs):
@@ -247,12 +251,23 @@
         for part in range(parts):
             lend_copy(part).start()
 
-    r.small[...] = jnp.zeros_like(r.small)
-    r.tab_grad[...] = jnp.zeros_like(r.tab_grad)
-    r.dproj[...] = jnp.zeros_like(r.dproj)
+    r.gain_grad[...] = jnp.zeros_like(r.gain_grad)
+    r.fgain_grad[...] = jnp.zeros_like(r.fgain_grad)
+
+    if not z.summed:
+
+        @pl.when(is_ffn)
+        def _():
+            r.tab_grad[...] = jnp.zeros_like(r.tab_grad)
+
+
+    if not z.summed:
+
+        @pl.when(s != last)
+        def _():
+            r.dproj[...] = jnp.zeros_like(r.dproj)
+
     r.dbias[...] = jnp.zeros_like(r.dbias)
-    at_gain = slice(0, width)
-    at_fgain = slice(width, 2 * width)
     gain = r.gain[...]
     fgain = r.fgain[...].reshape(1, width)
 
@@ -277,27 +292,44 @@
         for h in range(H):
             total = jnp.zeros(buckets.shape, F32)
             for b in range(32):
-                total = jnp.where(buckets == b, r.bias[b : b + 1, h : h + 1], total)
+                total = jnp.where(buckets == b, r.bias[h : h + 1, b : b + 1], total)
             r.bias_sc[h] = total
 
     def attention_table():
         buckets = r.buckets[...]
-        head_lane = lax.broadcasted_iota(jnp.int32, (32, 128), 1)
+        ones = jnp.ones((16, 128), BF16)
+        head_row = lax.broadcasted_iota(jnp.int32, (16, 32), 0)
 
         def head(h, carry):
             grad = r.dbias[h]
-            by_bucket = jnp.concatenate(
+            rest = jnp.concatenate(
                 [
                     jnp.sum(jnp.where(buckets == b, grad, 0.0), axis=0, keepdims=True)
                     for b in range(32)
                 ],
                 axis=0,
             )
-            column = jnp.sum(by_bucket, axis=1, keepdims=True)
-            r.tab_grad[...] += jnp.where(head_lane == h, column, 0.0)
-            return carry
-
-        lax.fori_loop(0, H, head, 0)
+            total = jnp.zeros((16, 32), F32)
+            for _ in range(3):
+                part = rest.astype(BF16)
+                total = total + nt(ones, part)
+                rest = rest - part.astype(F32)
+            return carry + jnp.where(head_row == h, total, 0.0)
+
+        r.tab_grad[...] = lax.fori_loop(0, H, head, jnp.zeros((16, 32), F32))
+
+    def turn(source, slab, start):
+        size = FF_STEP // z.chunk
+        first = slab * z.slab_chunks + start // z.chunk
+        r.pool[first : first + size] = source[:, start : start + FF_STEP].T.reshape(
+            size, z.chunk, width
+        )
+
+    def turned(slab, start, stop):
+        first = slab * z.slab_chunks
+        return r.pool[first + start // z.chunk : first + stop // z.chunk].reshape(
+            stop - start, width
+        )
 
     def attention_forward(m):
         states, inverse, scaled = load_state(m)
@@ -367,9 +399,9 @@
                 r.right[0, block(m), start : start + 128] = jnp.where(
                     low_half, found[0][third], found[1][third]
                 ).astype(BF16)
-        grad_normed = nt(r.right[0, block(m), : 3 * head_width], r.main[:, : 3 * head_width])
+        grad_normed = nn(r.right[0, block(m), : 3 * head_width], turned(0, 0, 3 * head_width))
         grad_states, grad_gain = rms_back(scaled, inverse, gain, grad_normed)
-        r.small[:, at_gain] += grad_gain
+        r.gain_grad[...] += grad_gain
         return grad + grad_states
 
     def ffn_forward(m):
@@ -393,7 +425,7 @@
             r.right[1, block(m), columns] = hidden
             r.right[0, block(m), columns] = (slope * up).astype(BF16)
             r.right[2, block(m), columns] = smooth.astype(BF16)
-            outputs = outputs + nt(hidden, r.side[:, columns])
+            outputs = outputs + nn(hidden, turned(1, start, start + FF_STEP))
         return outputs
 
     def ffn_backward(m, grad):
@@ -410,11 +442,11 @@
             r.right[2, block(m), columns] = grad_up
             grad_normed = (
                 grad_normed
-                + nt(grad_gate, r.main[:, columns])
-                + nt(grad_up, r.lent[:, columns])
+                + nn(grad_gate, turned(0, start, start + FF_STEP))
+                + nn(grad_up, turned(2, start, start + FF_STEP))
             )
         grad_states, grad_gain = rms_back(scaled, inverse, gain, grad_normed)
-        r.small[:, at_gain] += grad_gain
+        r.gain_grad[...] += grad_gain
         return grad + grad_states
 
     def count_hits(m):
@@ -424,7 +456,7 @@
             total = jnp.zeros((DOC_LEN, rows), F32)
             for k in range(z.retrieved):
                 total = total + jnp.where(r.idx_rx[m, 8 + k : 9 + k, :] == numbers, 1.0, 0.0)
-            r.counts[m, c * DOC_LEN : (c + 1) * DOC_LEN, :] = total
+            r.counts[m, c * DOC_LEN : (c + 1) * DOC_LEN, :] = total.astype(BF16)
 
     def pick_docs(m):
         for c in range(batch_size):
@@ -442,7 +474,7 @@
     def loss_and_grad(m, unit):
         docs = r.own_docs[m]
         sims = nt(docs, unit)
-        count = r.counts[m]
+        count = r.counts[m].astype(F32)
         imputed = jnp.sum(count * sims, axis=0, keepdims=True) / z.retrieved
         grown = count * jnp.exp(sims)
         imputed_mass = jnp.exp(imputed)
@@ -500,10 +532,11 @@
         grad_projected = (
             size * (grad_unit - exact * jnp.sum(grad_unit * exact, axis=-1, keepdims=True))
         ).astype(BF16)
-        r.dproj[...] += tn(normed, grad_projected)
+        r.xout[m] = normed
+        r.final_right[block(m), :] = grad_projected
         grad_normed = nt(grad_projected, r.proj[...])
         grad_states, grad_gain = rms_back(scaled, inverse, fgain, grad_normed)
-        r.small[:, at_fgain] += grad_gain
+        r.fgain_grad[...] += grad_gain
         return grad_states
 
     def loop(body):
@@ -530,6 +563,8 @@
             state_copy(m).start()
 
         loop(forward)
+        for start in range(0, ff, FF_STEP):
+            turn(r.main, 0, start)
 
         def backward(m):
             grad_copy(m).wait_recv()
@@ -544,14 +579,21 @@
                 fin_copy(m, m).start()
 
         loop(backward)
-        attention_table()
+        if not z.summed:
+            attention_table()
 
     @pl.when(is_ffn)
     def _():
+        turns = [(r.main, 0, start) for start in range(0, ff, FF_STEP)]
+        turns += [(r.side, 1, start) for start in range(0, ff, FF_STEP)]
+        main_load().wait()
+        side_load().wait()
         for part in range(parts):
             lend_copy(part).wait_recv()
             lend_forward(1, place, part, core_peer).start()
             lend_forward(2, place, part, far_peer).start()
+            for one in turns[part :: parts]:
+                turn(*one)
 
         @pl.when(s == last)
         def _():
@@ -574,13 +616,16 @@
         for part in range(parts):
             lend_forward(1, place, part, core_peer).wait_recv()
             lend_forward(3, far_place, part, core_peer).wait_recv()
-        main_load().wait()
-        side_load().wait()
+
+        def turn_lent():
+            for start in range(0, ff, FF_STEP):
+                turn(r.lent, 2, start)
 
         @pl.when(s == last)
         def _():
             peers(lambda owner: table_copy(owner, owner).wait_recv())
             loop(pick_docs)
+            turn_lent()
             loop(wait_meta)
 
             def both(m):
@@ -591,6 +636,7 @@
                 grad_copy(m).start()
 
             loop(both)
+            r.dproj[...] = tn(r.xout[...].reshape(z.total, width), r.final_right[...])
 
         @pl.when(s != last)
         def _():
@@ -600,6 +646,7 @@
                 state_copy(m).start()
 
             loop(forward)
+            turn_lent()
 
             def backward(m):
                 grad_copy(m).wait_recv()
@@ -615,7 +662,7 @@
             lend_forward(3, far_place, part, core_peer).wait_send()
 
     if z.summed:
-        sum_gradients(z, r, s, d, copy, peers, other_sections, is_attention)
+        sum_gradients(z, r, s, d, copy, peers, other_sections, is_attention, attention_table)
 
     other_sections(lambda to: meta_copy(to, s).wait_send())
 
@@ -658,7 +705,7 @@
         write_own(r.unit_tx[last], r.loss_tx[last])
 
 
-def sum_gradients(z, r, s, d, copy, peers, other_sections, is_attention):
+def sum_gradients(z, r, s, d, copy, peers, other_sections, is_attention, attention_table):
     sections, dp_size, width, ff, share, line = z.sections, z.dp_size, z.width, z.ff, z.share, z.line
     step_columns, per_slab, units, steps = z.step_columns, z.per_slab, z.units, z.steps
     place = d // 2
@@ -672,11 +719,14 @@
     def piece_rows(owner):
         return pl.ds(pl.multiple_of(owner * share, share), share)
 
-    def small_copies(to, slot):
-        return (
-            copy(r.small, r.small_rx.at[slot], r.small_ss.at[0, to], r.small_rs.at[0, slot], s, to),
-            copy(r.tab_grad, r.tab_rx.at[slot], r.small_ss.at[1, to], r.small_rs.at[1, slot], s, to),
-        )
+    def gain_copy(to, slot):
+        return copy(r.gain_grad, r.gain_rx.at[slot], r.gain_ss.at[to], r.gain_rs.at[slot], s, to)
+
+    def table_copy(to, slot):
+        return copy(r.tab_grad, r.tab_rx.at[slot], r.tabs_ss.at[to], r.tabs_rs.at[slot], s, to)
+
+    def fgain_copy(to, slot):
+        return copy(r.fgain_grad, r.fgain_rx.at[slot], r.fg_ss.at[to], r.fg_rs.at[slot], s, to)
 
     def proj_copy(to, slot):
         return copy(
@@ -688,34 +738,29 @@
             to,
         )
 
-    def column_copies(to, slot):
-        return (
-            copy(
-                r.small_tx, r.small_cx.at[slot], r.column_ss.at[0, to], r.column_rs.at[0, slot], to, d
-            ),
-            copy(r.tab_tx, r.tab_cx.at[slot], r.column_ss.at[1, to], r.column_rs.at[1, slot], to, d),
-        )
-
-    def piece_copy(to):
-        rows = piece_rows(d)
-        return copy(
-            r.proj_out.at[rows, :], r.proj_out.at[rows, :], r.piece_ss.at[to], r.piece_rs, to, d
-        )
-
     def spread_copy(to, owner):
         rows = piece_rows(owner)
         return copy(
-            r.proj_out.at[rows, :],
-            r.proj_out.at[rows, :],
+            r.proj_sum.at[rows, :],
+            r.proj_sum.at[rows, :],
             r.spread_ss.at[to],
             r.spread_rs.at[owner],
             s,
             to,
         )
 
-    def each(copies, action):
-        for one in copies:
-            getattr(one, action)()
+    def table_across(to, slot):
+        return copy(r.tab_tx, r.tab_cx.at[slot], r.across_ss.at[0, to], r.across_rs.at[slot], to, d)
+
+    def fgain_across(to):
+        return copy(
+            r.fgain_tx, r.fgain_sum, r.across_ss.at[1, to], r.across_rs.at[sections], to, d
+        )
+
+    def proj_across(to):
+        return copy(
+            r.proj_sum, r.proj_sum, r.across_ss.at[2, to], r.across_rs.at[sections + 1], to, d
+        )
 
     def total_of(ref, count):
         total = ref[0]
@@ -723,56 +768,84 @@
             total = total + ref[k]
         return total
 
+    def to_others(body):
+        for to in range(sections):
+
+            @pl.when(s != to)
+            def _():
+                body(to)
+
     def small_first():
-        peers(lambda to: each(small_copies(to, d), "start"))
-        r.small_rx[d] = r.small[...]
-        r.tab_rx[d] = r.tab_grad[...]
+        peers(lambda to: gain_copy(to, d).start())
+        r.gain_rx[d] = r.gain_grad[...]
+
+        @pl.when(is_attention)
+        def _():
+            attention_table()
+            peers(lambda to: table_copy(to, d).start())
+            r.tab_rx[d] = r.tab_grad[...]
+
+    def proj_first():
+        peers(lambda to: proj_copy(to, d).start())
+        peers(lambda to: fgain_copy(to, d).start())
+        r.proj_rx[d] = r.dproj[piece_rows(d), :]
+        r.fgain_rx[d] = r.fgain_grad[...]
+
+    def proj_second():
+        peers(lambda owner: proj_copy(owner, owner).wait_recv())
+        peers(lambda owner: fgain_copy(owner, owner).wait_recv())
+        r.proj_sum[piece_rows(d), :] = total_of(r.proj_rx, dp_size)
+        r.fgain_tx[...] = total_of(r.fgain_rx, dp_size)
+        r.fgain_sum[...] = r.fgain_tx[...]
+        peers(lambda to: spread_copy(to, d).start())
+        to_others(lambda to: fgain_across(to).start())
+
+    def proj_third():
+        peers(lambda owner: spread_copy(owner, owner).wait_recv())
+        to_others(lambda to: proj_across(to).start())
+
+    def small_second():
+        peers(lambda owner: gain_copy(owner, owner).wait_recv())
+        gain_sum = jnp.broadcast_to(total_of(r.gain_rx, dp_size), (8, width))
+        r.gain_out[...] = pltpu.roll(gain_sum, width - d * share, 1)[0:1, :share]
+
+        @pl.when(is_attention)
+        def _():
+            peers(lambda owner: table_copy(owner, owner).wait_recv())
+            r.tab_tx[...] = total_of(r.tab_rx, dp_size)
+            r.tab_cx[s // 2] = r.tab_tx[...]
+            to_others(lambda to: table_across(to, s // 2).start())
+
+    def small_last():
+        for source in range(0, sections, 2):
+
+            @pl.when(s != source)
+            def _():
+                table_across(source, source // 2).wait_recv()
+
+        r.table_out[...] = total_of(r.tab_cx, (sections + 1) // 2)[:H]
+
+        @pl.when(s != last)
+        def _():
+            fgain_across(last).wait_recv()
+            proj_across(last).wait_recv()
+
+        r.fgain_out[...] = r.fgain_sum[...].reshape(width)
+        r.proj_out[...] = r.proj_sum[...]
+        peers(lambda to: gain_copy(to, d).wait_send())
+
+        @pl.when(is_attention)
+        def _():
+            peers(lambda to: table_copy(to, d).wait_send())
+            to_others(lambda to: table_across(to, s // 2).wait_send())
 
         @pl.when(s == last)
         def _():
-            peers(lambda to: proj_copy(to, d).start())
-            r.proj_rx[d] = r.dproj[piece_rows(d), :]
-
-    def small_second():
-        peers(lambda owner: each(small_copies(owner, owner), "wait_recv"))
-        r.small_tx[...] = total_of(r.small_rx, dp_size)
-        r.tab_tx[...] = total_of(r.tab_rx, dp_size)
-        r.small_cx[s] = r.small_tx[...]
-        r.tab_cx[s] = r.tab_tx[...]
-        other_sections(lambda to: each(column_copies(to, s), "start"))
-
-        @pl.when(s == last)
-        def _():
-            peers(lambda owner: proj_copy(owner, owner).wait_recv())
-            r.proj_out[piece_rows(d), :] = total_of(r.proj_rx, dp_size)
-            for to in range(sections - 1):
-                piece_copy(to).start()
-            peers(lambda to: spread_copy(to, d).start())
-
-    def small_third():
-        other_sections(lambda to: each(column_copies(to, to), "wait_recv"))
-        r.fgain_out[...] = total_of(r.small_cx, sections)[:, width:]
-        r.table_out[...] = total_of(r.tab_cx, sections)[:, :H]
-        r.gain_out[...] = pltpu.roll(
-            jnp.broadcast_to(r.small_tx[:, :width], (8, width)), width - d * share, 1
-        )[0:1, :share]
-
-        @pl.when(s != last)
-        def _():
-            piece_copy(0).wait_recv()
-            peers(lambda to: spread_copy(to, d).start())
-
-    def small_last():
-        peers(lambda owner: spread_copy(owner, owner).wait_recv())
-        peers(lambda to: spread_copy(to, d).wait_send())
-        peers(lambda to: each(small_copies(to, d), "wait_send"))
-        other_sections(lambda to: each(column_copies(to, s), "wait_send"))
-
-        @pl.when(s == last)
-        def _():
             peers(lambda to: proj_copy(to, d).wait_send())
-            for to in range(sections - 1):
-                piece_copy(to).wait_send()
+            peers(lambda to: fgain_copy(to, d).wait_send())
+            peers(lambda to: spread_copy(to, d).wait_send())
+            to_others(lambda to: fgain_across(to).wait_send())
+            to_others(lambda to: proj_across(to).wait_send())
 
     def target(i):
         found = jnp.int32(0)
@@ -793,7 +866,7 @@
 
     def core_copy(t):
         return copy(
-            r.core_tx.at[lax.rem(t, 4)], r.core_rx.at[t], r.core_ss.at[t], r.core_rs.at[t], s, peer
+            r.core_tx.at[lax.rem(t, 4)], r.pool.at[t], r.core_ss.at[t], r.core_rs.at[t], s, peer
         )
 
     def up_core_copy(k):
@@ -811,11 +884,14 @@
         column = pl.ds(pl.multiple_of(t // dp_size * step_columns, step_columns), step_columns)
         return r.lent.at[row, column]
 
+    def line_slot(way, j, u):
+        return steps + (way * (line - 1) + j - 1 + way) * units + u
+
     def line_copy(t, way, j, u, to):
         slot = j - 1 + way
         return copy(
             line_view(t),
-            r.line_rx.at[way, slot, u],
+            r.pool.at[line_slot(way, j, u)],
             r.line_ss.at[t],
             r.line_rs.at[way, slot, u],
             s,
@@ -866,7 +942,7 @@
         @pl.when(jnp.logical_or(is_ffn, slab == 0))
         def _():
             core_copy(t).wait_recv()
-            total[...] += r.core_rx[t].astype(F32)
+            total[...] += r.pool[t].astype(F32)
 
         @pl.when(jnp.logical_and(is_attention, slab == 1))
         def _():
@@ -889,12 +965,12 @@
         @pl.when(jnp.logical_and(place > 0, j >= place))
         def _():
             line_copy(t, 0, j, u, place).wait_recv()
-            total[...] += r.line_rx[0, j - 1, u].astype(F32)
+            total[...] += r.pool[line_slot(0, j, u)].astype(F32)
 
         @pl.when(jnp.logical_and(place < line - 1, j <= place))
         def _():
             line_copy(t, 1, j, u, place).wait_recv()
-            total[...] += r.line_rx[1, j, u].astype(F32)
+            total[...] += r.pool[line_slot(1, j, u)].astype(F32)
 
         @pl.when(jnp.logical_and(j == place, slab == 0))
         def _():
@@ -909,8 +985,24 @@
             line_view(t)[...] = total[...].astype(BF16)
             line_copy(t, way, j, u, place + 1 - 2 * way).start()
 
-    small_first()
+    pl.semaphore_signal(r.core_ready, inc=1, device_id=(s, peer), device_id_type=MESH)
+
+    @pl.when(place > 0)
+    def _():
+        pl.semaphore_signal(r.line_ready, inc=1, device_id=(s, d - 2), device_id_type=MESH)
+
+    @pl.when(place < line - 1)
+    def _():
+        pl.semaphore_signal(r.line_ready, inc=1, device_id=(s, d + 2), device_id_type=MESH)
+
+    @pl.when(s == last)
+    def _():
+        proj_first()
+
+    pl.semaphore_wait(r.core_ready, 1)
     begin(jnp.int32(0))
+    neighbours = jnp.where(place > 0, 1, 0) + jnp.where(place < line - 1, 1, 0)
+    pl.semaphore_wait(r.line_ready, neighbours)
 
     def step(t, carry):
         @pl.when(t < steps)
@@ -919,13 +1011,21 @@
 
         finish(t - 1)
 
-        @pl.when(t == units)
+        @pl.when(jnp.logical_and(s == last, t == 2))
+        def _():
+            proj_second()
+
+        @pl.when(t == 4)
+        def _():
+            small_first()
+
+        @pl.when(jnp.logical_and(s == last, t == 6))
+        def _():
+            proj_third()
+
+        @pl.when(t == units + 4)
         def _():
             small_second()
-
-        @pl.when(t == steps - units)
-        def _():
-            small_third()
 
         return carry
 
@@ -998,7 +1098,9 @@
         idx_rx=VMEM((sections, 8 + z.retrieved, rows), jnp.int32),
         own_docs=VMEM((sections, z.batch_size * DOC_LEN, z.vector), BF16),
         table=VMEM((dp_size * z.doc_rows, z.vector), BF16),
-        counts=VMEM((sections, z.batch_size * DOC_LEN, rows), F32),
+        counts=VMEM((sections, z.batch_size * DOC_LEN, rows), BF16),
+        pool=VMEM((z.pool, z.chunk, width), BF16),
+        final_right=VMEM((z.total, z.vector), BF16),
         qkv=VMEM((z.total, 3 * H * DH), BF16),
         probs=VMEM((sections, H, rows, rows), F32),
         bias_sc=VMEM((H, z.query_len, rows), F32),
@@ -1030,15 +1132,18 @@
     )
     factors = dict(left=((2, width, z.total), BF16), right=((3, z.total, ff), BF16))
     partials = dict(
-        small=((1, 2 * width), F32), tab_grad=((32, 128), F32), dproj=((width, z.vector), F32)
+        gain_grad=((1, width), F32),
+        fgain_grad=((1, width), F32),
+        tab_grad=((16, 32), F32),
+        dproj=((width, z.vector), F32),
     )
     if z.summed:
         outputs |= dict(
             main_out=shape((1, share, ff), F32),
             side_out=shape((1, share, ff), F32),
             gain_out=shape((1, share), F32),
-            table_out=shape((32, H), F32),
-            fgain_out=shape((1, width), F32),
+            table_out=shape((H, 32), F32),
+            fgain_out=shape((width,), F32),
             proj_out=shape((width, z.vector), F32),
         )
         scratch |= {name: VMEM(*kind) for name, kind in (factors | partials).items()}
@@ -1046,17 +1151,17 @@
             mine=VMEM((2,) + piece, F32),
             up_mine=VMEM(piece, F32),
             core_tx=VMEM((4,) + piece, BF16),
-            core_rx=VMEM((steps,) + piece, BF16),
             up_core_tx=VMEM((4,) + piece, BF16),
             up_tx=VMEM((4,) + piece, BF16),
             up_rx=VMEM((steps // 2,) + piece, BF16),
-            line_rx=VMEM((2, z.line - 1, units) + piece, BF16),
-            small_rx=VMEM((dp_size, 1, 2 * width), F32),
-            small_tx=VMEM((1, 2 * width), F32),
-            small_cx=VMEM((sections, 1, 2 * width), F32),
-            tab_rx=VMEM((dp_size, 32, 128), F32),
-            tab_tx=VMEM((32, 128), F32),
-            tab_cx=VMEM((sections, 32, 128), F32),
+            gain_rx=VMEM((dp_size, 1, width), F32),
+            tab_rx=VMEM((dp_size, 16, 32), F32),
+            tab_tx=VMEM((16, 32), F32),
+            tab_cx=VMEM(((sections + 1) // 2, 16, 32), F32),
+            fgain_rx=VMEM((dp_size, 1, width), F32),
+            fgain_tx=VMEM((1, width), F32),
+            fgain_sum=VMEM((1, width), F32),
+            proj_sum=VMEM((width, z.vector), F32),
             proj_rx=VMEM((dp_size, share, z.vector), F32),
             core_ss=dma((steps,)),
             core_rs=dma((steps,)),
@@ -1065,14 +1170,18 @@
             up_rs=dma((steps // 2,)),
             line_ss=dma((steps,)),
             line_rs=dma((2, z.line - 1, units)),
-            small_ss=dma((2, dp_size)),
-            small_rs=dma((2, dp_size)),
-            column_ss=dma((2, sections)),
-            column_rs=dma((2, sections)),
+            core_ready=pltpu.SemaphoreType.REGULAR,
+            line_ready=pltpu.SemaphoreType.REGULAR,
+            gain_ss=dma((dp_size,)),
+            gain_rs=dma((dp_size,)),
+            tabs_ss=dma((dp_size,)),
+            tabs_rs=dma((dp_size,)),
+            fg_ss=dma((dp_size,)),
+            fg_rs=dma((dp_size,)),
+            across_ss=dma((3, sections)),
+            across_rs=dma((sections + 2,)),
             proj_ss=dma((dp_size,)),
             proj_rs=dma((dp_size,)),
-            piece_ss=dma((sections,)),
-            piece_rs=dma,
             spread_ss=dma((dp_size,)),
             spread_rs=dma((dp_size,)),
         )
@@ -1092,6 +1201,26 @@
     return types.SimpleNamespace(**dict(zip(outputs, results, strict=True)))
 
 
+def deliver_kernel(count, *refs):
+    for k in range(count):
+        refs[count + 1 + k][...] = refs[k][...]
+    losses, out = refs[count], refs[-1]
+    out[...] = losses[0:1, : out.shape[0]].reshape(out.shape)
+
+
+def deliver(values, losses, queries):
+    count = len(values)
+    vmem = pl.BlockSpec(memory_space=VMEM)
+    return pl.pallas_call(
+        functools.partial(deliver_kernel, count),
+        out_shape=tuple(jax.ShapeDtypeStruct(v.shape, v.dtype) for v in values)
+        + (jax.ShapeDtypeStruct((queries,), F32),),
+        in_specs=[vmem] * (count + 1),
+        out_specs=(vmem,) * (count + 1),
+        name="deliver",
+    )(*values, losses)
+
+
 def sums_outside(z, out):
     head_width = H * DH
     section = lax.axis_index("section")
@@ -1112,13 +1241,13 @@
         lax.psum_scatter, axis_name="dp", scatter_dimension=0, tiled=True
     )
     table, fgain, proj = lax.psum(
-        (out.tab_grad[:, :H], out.small[0, z.width :], out.dproj), ("section", "dp")
+        (out.tab_grad[:H], out.fgain_grad[0], out.dproj), ("section", "dp")
     )
     return (
         scatter(main_grad)[None],
         scatter(side_grad)[None],
-        scatter(out.small[0, : z.width])[None],
-        table,
+        scatter(out.gain_grad[0])[None],
+        table.T,
         fgain,
         proj,
     )
@@ -1161,24 +1290,19 @@
         slab_main,
         slab_side,
         section_gains,
-        rel_bias,
+        rel_bias.T,
         buckets,
         final_gain,
         out_proj,
         doc_vectors,
     )
-    if z.summed:
-        sums = (
-            out.main_out,
-            out.side_out,
-            out.gain_out,
-            out.table_out,
-            out.fgain_out[0],
-            out.proj_out,
-        )
-    else:
-        sums = sums_outside(z, out)
-    return (out.units, out.loss[0, :batch_size], out.dx) + sums
+    if not z.summed:
+        return (out.units, out.loss[0, :batch_size], out.dx) + sums_outside(z, out)
+    names = ("units", "dx", "main_out", "side_out", "gain_out", "table_out", "fgain_out", "proj_out")
+    units, dx, main, side, gain, table, fgain, proj, losses = deliver(
+        [getattr(out, n) for n in names], out.loss, batch_size
+    )
+    return units, losses, dx, main, side, gain, table.T, fgain, proj
 
 
 def solution(mesh):

time: 236 us -> 209 us (0.89)
  Pallas kernels: 221 us -> 208 us
  local copies, waits for them, and re-layouts: 11.8 us -> 0 us
    pallas_call x1, Pallas kernels: 221 us -> 205 us  [relay(): pl.pallas_call(functools.partial(relay_kernel, z, (*inputs, *outputs, *sc...]
    unnamed x14 -> x0, local copies, waits for them, and re-layouts: 10.7 us -> none
    pallas_call x0 -> x1, Pallas kernels: none -> 3.6 us  [deliver(): pl.pallas_call(functools.partial(deliver_kernel, count), out_shape=tuple(...]
where the time goes in v3:
time: 209 us
  Pallas kernels  208 us (100%)
    pallas_call x1, Pallas kernels, relay(): pl.pallas_call(functools.partial(relay_kernel, z, (*inputs, *outputs, *sc...  205 us

profile of v3, /device:TPU:16, one launch (start us, length us, event | category | flops | bytes accessed | tf_op | source)
XLA Modules:
  0.0 209.1 jit_solution(838570668360783172)
XLA Ops:
  0.6 204.8 %relay.1 = (bf16[4,32,128]{2,1,0:T(8,128)(2,1)}, f32[8,128]{1,0:T(8,128)}, f32[4,32,768]{2,1,0:T(8,128)}, f32[1,96,3072]{2,1,0:T(8,128)}, f32[1,96,3072]{2,1,0:T...) custom-call(bf16[128,768]{1,0:T(8,128)(2,1)} %bitcast.4, s32[4]{0:T(128)} %refs_1_.1, ...), custom_call_target="tpu_custom_call" | custom-call | tf_op jit(solution)/shard_map/relay/pallas_call | solution.py:1190
  205.4 3.6 %deliver.1 = (bf16[4,32,128]{2,1,0:T(8,128)(2,1)}, f32[4,32,768]{2,1,0:T(8,128)}, f32[1,96,3072]{2,1,0:T(8,128)}, f32[1,96,3072]{2,1,0:T(8,128)}, f32[1,96]{1,0:...) custom-call(bf16[4,32,128]{2,1,0:T(8,128)(2,1)} %get-tuple-element.27.refs_0_, ...), custom_call_target="tpu_custom_call" | custom-call | tf_op jit(solution)/shard_map/deliver/pallas_call | solution.py:1214

commit v4 on v3

--- a/solution.py
+++ b/solution.py
@@ -144,11 +144,35 @@
     def side_load():
         return pltpu.make_async_copy(r.side_hbm.at[0], r.side, r.load_sem.at[1])
 
+    small_loads = [
+        pltpu.make_async_copy(getattr(r, name + "_hbm"), getattr(r, name), r.small_sem.at[k])
+        for k, name in enumerate(("chosen", "bias", "buckets", "gain", "fgain", "proj"))
+    ]
+    for one in small_loads:
+        one.start()
+
+    def hid_load():
+        return pltpu.make_async_copy(r.hid_hbm, r.xin.at[0], r.load_sem.at[2])
+
+    def docs_load():
+        return pltpu.make_async_copy(r.docs_hbm, r.table.at[table_rows(d), :], r.load_sem.at[2])
+
+    def table_rows(owner):
+        return pl.ds(pl.multiple_of(owner * z.doc_rows, z.doc_rows), z.doc_rows)
+
+    @pl.when(s == 0)
+    def _():
+        hid_load().start()
+
     main_load().start()
 
     @pl.when(is_ffn)
     def _():
         side_load().start()
+
+    @pl.when(s == last)
+    def _():
+        docs_load().start()
 
     barrier = pltpu.get_barrier_semaphore()
     other_sections(
@@ -169,6 +193,8 @@
     r.idx[:8, :] = jnp.zeros((8, rows), jnp.int32)
     for c in range(batch_size):
         r.idx[c : c + 1, :] = jnp.full((1, rows), r.labels[c], jnp.int32)
+    for one in small_loads:
+        one.wait()
     r.idx[8:, :] = r.chosen[...].T
 
     pl.semaphore_wait(barrier, sections - 1 + dp_size - 1)
@@ -177,28 +203,32 @@
         start = quarter * (ff // 4) + part * LEND_STEP
         return pl.ds(pl.multiple_of(start, LEND_STEP), LEND_STEP)
 
-    def lend_copy(part):
+    def lend_copy(part, half):
         columns = lend_columns(place, part)
+        depth = slice(half * (width // 2), (half + 1) * (width // 2))
         return copy(
-            r.side_hbm.at[0, :, columns],
-            r.lent.at[:, columns],
-            r.lend_ss.at[0, part],
-            r.lend_rs.at[0, part],
+            r.side_hbm.at[0, depth, columns],
+            r.lent.at[depth, columns],
+            r.lend_ss.at[0, part, half],
+            r.lend_rs.at[0, part, half],
             after,
             d,
         )
 
-    def lend_forward(kind, quarter, part, peer):
+    def lend_forward(kind, quarter, part, half, peer):
         columns = lend_columns(quarter, part)
+        depth = slice(half * (width // 2), (half + 1) * (width // 2))
         return copy(
-            r.lent.at[:, columns],
-            r.lent.at[:, columns],
-            r.lend_ss.at[kind, part],
-            r.lend_rs.at[kind, part],
+            r.lent.at[depth, columns],
+            r.lent.at[depth, columns],
+            r.lend_ss.at[kind, part, half],
+            r.lend_rs.at[kind, part, half],
             s,
             peer,
         )
 
+    pieces = [(part, half) for part in range(parts) for half in range(2)]
+
     def state_copy(m):
         return copy(r.xout.at[m], r.xin.at[m], r.state_ss.at[m], r.state_rs.at[m], after, d)
 
@@ -212,7 +242,7 @@
         return copy(r.idx, r.idx_rx.at[slot], r.idx_ss, r.idx_rs.at[slot], last, d)
 
     def hid_copy(slot):
-        return copy(r.hid, r.xin.at[slot], r.state_ss.at[sections], r.state_rs.at[slot], 0, d)
+        return copy(r.hid_hbm, r.xin.at[slot], r.state_ss.at[sections], r.state_rs.at[slot], 0, d)
 
     def unit_copy(m, to):
         return copy(r.unit_tx.at[m], r.unit_rx, r.unit_ss.at[m], r.unit_rs, to, d)
@@ -223,21 +253,48 @@
     def fin_copy(m, to):
         return copy(r.gout.at[m], r.fin_rx, r.fin_ss.at[m], r.fin_rs, to, d)
 
-    def table_rows(owner):
-        return pl.ds(pl.multiple_of(owner * z.doc_rows, z.doc_rows), z.doc_rows)
-
     def table_copy(to, owner):
         return copy(
-            r.docs, r.table.at[table_rows(owner), :], r.tab_ss.at[to], r.tab_rs.at[owner], s, to
-        )
+            r.docs_hbm, r.table.at[table_rows(owner), :], r.tab_ss.at[to], r.tab_rs.at[owner], s, to
+        )
+
+    def table_near(owner):
+        return copy(
+            r.docs_hbm,
+            r.table.at[table_rows(owner), :],
+            r.tab_ss.at[core_peer],
+            r.tab_rs.at[owner],
+            s,
+            core_peer,
+        )
+
+    def table_forward(owner):
+        rows = table_rows(owner)
+        return copy(
+            r.table.at[rows, :], r.table.at[rows, :], r.tabf_ss.at[owner], r.tab_rs.at[owner], s, core_peer
+        )
+
+    def far_owners(body):
+        def step(k, carry):
+            body(lax.rem(d + 2 * k, dp_size))
+            return carry
+
+        lax.fori_loop(1, dp_size // 2, step, 0)
 
     @pl.when(s != 0)
     def _():
         hid_copy(s).start()
 
-    @pl.when(s == 0)
-    def _():
-        r.xin[0] = r.hid[...]
+    @pl.when(s == last)
+    def _():
+        table_near(d).start()
+        far_owners(lambda to: table_copy(to, d).start())
+
+    @pl.when(is_attention)
+    def _():
+        for part in range(parts):
+            for half in range(2):
+                lend_copy(part, half).start()
 
     other_sections(lambda to: meta_copy(to, s).start())
     r.meta_rx[s] = r.meta[...]
@@ -245,11 +302,6 @@
     @pl.when(s != last)
     def _():
         idx_copy(s).start()
-
-    @pl.when(is_attention)
-    def _():
-        for part in range(parts):
-            lend_copy(part).start()
 
     r.gain_grad[...] = jnp.zeros_like(r.gain_grad)
     r.fgain_grad[...] = jnp.zeros_like(r.fgain_grad)
@@ -559,6 +611,11 @@
         def forward(m):
             wait_meta(m)
             wait_state(m)
+
+            @pl.when(jnp.logical_and(s == 0, m == 0))
+            def _():
+                hid_load().wait()
+
             r.xout[m] = attention_forward(m).astype(BF16)
             state_copy(m).start()
 
@@ -588,18 +645,29 @@
         turns += [(r.side, 1, start) for start in range(0, ff, FF_STEP)]
         main_load().wait()
         side_load().wait()
-        for part in range(parts):
-            lend_copy(part).wait_recv()
-            lend_forward(1, place, part, core_peer).start()
-            lend_forward(2, place, part, far_peer).start()
-            for one in turns[part :: parts]:
+        def far_arrived(piece):
+            lend_forward(2, far_place, *piece, far_peer).wait_recv()
+            lend_forward(3, far_place, *piece, core_peer).start()
+
+        lag = 2
+        for k, piece in enumerate(pieces):
+            lend_copy(*piece).wait_recv()
+            lend_forward(2, place, *piece, far_peer).start()
+            lend_forward(1, place, *piece, core_peer).start()
+            if k >= lag:
+                far_arrived(pieces[k - lag])
+            for one in turns[k :: len(pieces)]:
                 turn(*one)
 
         @pl.when(s == last)
         def _():
             r.idx_rx[last] = r.idx[...]
-            r.table[table_rows(d), :] = r.docs[...]
-            peers(lambda to: table_copy(to, d).start())
+
+            def pass_on(owner):
+                table_copy(owner, owner).wait_recv()
+                table_forward(owner).start()
+
+            far_owners(pass_on)
 
             def prepare(m):
                 @pl.when(m != last)
@@ -610,12 +678,11 @@
 
             loop(prepare)
 
-        for part in range(parts):
-            lend_forward(2, far_place, part, far_peer).wait_recv()
-            lend_forward(3, far_place, part, core_peer).start()
-        for part in range(parts):
-            lend_forward(1, place, part, core_peer).wait_recv()
-            lend_forward(3, far_place, part, core_peer).wait_recv()
+        for piece in pieces[-lag:]:
+            far_arrived(piece)
+        for piece in pieces:
+            lend_forward(1, place, *piece, core_peer).wait_recv()
+            lend_forward(3, far_place, *piece, core_peer).wait_recv()
 
         def turn_lent():
             for start in range(0, ff, FF_STEP):
@@ -623,7 +690,13 @@
 
         @pl.when(s == last)
         def _():
-            peers(lambda owner: table_copy(owner, owner).wait_recv())
+            docs_load().wait()
+            table_near(core_peer).wait_recv()
+
+            def take(owner):
+                table_forward(owner + core_peer - d).wait_recv()
+
+            far_owners(take)
             loop(pick_docs)
             turn_lent()
             loop(wait_meta)
@@ -656,56 +729,87 @@
             loop(backward)
             loop(wait_meta)
 
-        for part in range(parts):
-            lend_forward(1, place, part, core_peer).wait_send()
-            lend_forward(2, place, part, far_peer).wait_send()
-            lend_forward(3, far_place, part, core_peer).wait_send()
+        for piece in pieces:
+            lend_forward(1, place, *piece, core_peer).wait_send()
+            lend_forward(2, place, *piece, far_peer).wait_send()
+            lend_forward(3, far_place, *piece, core_peer).wait_send()
+
+    def put(k, name):
+        return pltpu.make_async_copy(getattr(r, name + "_v"), getattr(r, name), r.put_sem.at[k])
+
+    homes = [put(k, name) for k, name in enumerate(("units", "loss", "dx"))]
+
+    def come_home():
+        @pl.when(s != 0)
+        def _():
+            fin_copy(0, s).wait_recv()
+            r.dx_v[...] = r.fin_rx[...].astype(F32).reshape(batch_size, query_len, width)
+
+        @pl.when(s == 0)
+        def _():
+            r.dx_v[...] = r.gout[0].astype(F32).reshape(batch_size, query_len, width)
+
+        def write_own(unit, losses):
+            r.units_v[...] = unit.reshape(batch_size, query_len, z.vector)
+            r.loss_v[...] = losses
+
+        @pl.when(s != last)
+        def _():
+            unit_copy(0, s).wait_recv()
+            loss_copy(0, s).wait_recv()
+            write_own(r.unit_rx[...], r.loss_rx[...])
+
+        @pl.when(s == last)
+        def _():
+            write_own(r.unit_tx[last], r.loss_tx[last])
+
+        for one in homes:
+            one.start()
 
     if z.summed:
-        sum_gradients(z, r, s, d, copy, peers, other_sections, is_attention, attention_table)
-
+        sum_gradients(
+            z, r, s, d, copy, peers, other_sections, is_attention, attention_table, come_home
+        )
+    else:
+        come_home()
+
+    for one in homes:
+        one.wait()
     other_sections(lambda to: meta_copy(to, s).wait_send())
 
     @pl.when(s != 0)
     def _():
         hid_copy(s).wait_send()
-        fin_copy(0, s).wait_recv()
-        r.dx[...] = r.fin_rx[...].astype(F32).reshape(batch_size, query_len, width)
         loop(lambda m: grad_copy(m).wait_send())
 
     @pl.when(s == 0)
     def _():
-        r.dx[...] = r.gout[0].astype(F32).reshape(batch_size, query_len, width)
         for m in range(1, sections):
             fin_copy(m, m).wait_send()
 
     @pl.when(is_attention)
     def _():
-        for part in range(parts):
-            lend_copy(part).wait_send()
-
-    def write_own(unit, losses):
-        r.units[...] = unit.reshape(batch_size, query_len, z.vector)
-        r.loss[...] = losses
+        for piece in pieces:
+            lend_copy(*piece).wait_send()
 
     @pl.when(s != last)
     def _():
         idx_copy(s).wait_send()
         loop(lambda m: state_copy(m).wait_send())
-        unit_copy(0, s).wait_recv()
-        loss_copy(0, s).wait_recv()
-        write_own(r.unit_rx[...], r.loss_rx[...])
 
     @pl.when(s == last)
     def _():
-        peers(lambda to: table_copy(to, d).wait_send())
+        table_near(d).wait_send()
+        far_owners(lambda to: table_copy(to, d).wait_send())
+        far_owners(lambda owner: table_forward(owner).wait_send())
         for m in range(sections - 1):
             unit_copy(m, m).wait_send()
             loss_copy(m, m).wait_send()
-        write_own(r.unit_tx[last], r.loss_tx[last])
-
-
-def sum_gradients(z, r, s, d, copy, peers, other_sections, is_attention, attention_table):
+
+
+def sum_gradients(
+    z, r, s, d, copy, peers, other_sections, is_attention, attention_table, come_home
+):
     sections, dp_size, width, ff, share, line = z.sections, z.dp_size, z.width, z.ff, z.share, z.line
     step_columns, per_slab, units, steps = z.step_columns, z.per_slab, z.units, z.steps
     place = d // 2
@@ -762,6 +866,24 @@
             r.proj_sum, r.proj_sum, r.across_ss.at[2, to], r.across_rs.at[sections + 1], to, d
         )
 
+    small_puts = [
+        pltpu.make_async_copy(source, target, r.put_sem.at[3 + k])
+        for k, (source, target) in enumerate(
+            (
+                (r.gain_out_v, r.gain_out),
+                (r.table_out_v, r.table_out),
+                (r.fgain_out_v, r.fgain_out),
+                (r.proj_sum, r.proj_out),
+            )
+        )
+    ]
+
+    def slab_put(slab, column, columns):
+        source, target = ((r.main_v, r.main_out), (r.side_v, r.side_out))[slab]
+        return pltpu.make_async_copy(
+            source.at[:, columns], target.at[0, :, columns], r.slab_sem.at[slab, column]
+        )
+
     def total_of(ref, count):
         total = ref[0]
         for k in range(1, count):
@@ -807,7 +929,7 @@
     def small_second():
         peers(lambda owner: gain_copy(owner, owner).wait_recv())
         gain_sum = jnp.broadcast_to(total_of(r.gain_rx, dp_size), (8, width))
-        r.gain_out[...] = pltpu.roll(gain_sum, width - d * share, 1)[0:1, :share]
+        r.gain_out_v[...] = pltpu.roll(gain_sum, width - d * share, 1)[0:1, :share]
 
         @pl.when(is_attention)
         def _():
@@ -823,15 +945,16 @@
             def _():
                 table_across(source, source // 2).wait_recv()
 
-        r.table_out[...] = total_of(r.tab_cx, (sections + 1) // 2)[:H]
+        r.table_out_v[...] = total_of(r.tab_cx, (sections + 1) // 2)[:H]
 
         @pl.when(s != last)
         def _():
             fgain_across(last).wait_recv()
             proj_across(last).wait_recv()
 
-        r.fgain_out[...] = r.fgain_sum[...].reshape(width)
-        r.proj_out[...] = r.proj_sum[...]
+        r.fgain_out_v[...] = r.fgain_sum[...].reshape(width)
+        for one in small_puts:
+            one.start()
         peers(lambda to: gain_copy(to, d).wait_send())
 
         @pl.when(is_attention)
@@ -855,11 +978,15 @@
 
     targets = [target(i) for i in range(line)]
 
-    def parts_of(t):
-        i, u = t // units, lax.rem(t, units)
+    def target_of(i):
         j = targets[0]
         for k in range(1, line):
             j = jnp.where(i == k, targets[k], j)
+        return j
+
+    def parts_of(t):
+        i, u = t // units, lax.rem(t, units)
+        j = target_of(i)
         slab, column = lax.rem(u, 2), u // 2
         columns = pl.ds(pl.multiple_of(column * step_columns, step_columns), step_columns)
         return j, u, slab, column, columns
@@ -906,7 +1033,6 @@
 
     def begin(t):
         j, u, slab, column, columns = parts_of(t)
-        k = t // 2
         mixed = jnp.logical_and(is_attention, column == per_slab - 1)
         which = jnp.where(jnp.logical_or(slab == 1, mixed), 1, 0)
 
@@ -922,17 +1048,32 @@
             core_copy(t).start()
             r.mine[lax.rem(t, 2)] = nn(r.left[which, ours(j), :], right)
 
-        @pl.when(jnp.logical_and(is_ffn, slab == 1))
-        def _():
-            right = r.right[2, :, columns]
-
-            @pl.when(k >= 4)
-            def _():
-                up_core_copy(k - 4).wait_send()
-
-            r.up_core_tx[lax.rem(k, 4)] = nn(r.left[0, theirs(j), :], right).astype(BF16)
-            up_core_copy(k).start()
-            r.up_mine[...] = nn(r.left[0, ours(j), :], right)
+    def up_parts(k):
+        i, column = k // per_slab, lax.rem(k, per_slab)
+        columns = pl.ds(pl.multiple_of(column * step_columns, step_columns), step_columns)
+        return target_of(i), columns
+
+    def begin_up(k):
+        j, columns = up_parts(k)
+        right = r.right[2, :, columns]
+
+        @pl.when(k >= 4)
+        def _():
+            up_core_copy(k - 4).wait_send()
+
+        r.up_core_tx[lax.rem(k, 4)] = nn(r.left[0, theirs(j), :], right).astype(BF16)
+        up_core_copy(k).start()
+        r.up_mine[lax.rem(k, 2)] = nn(r.left[0, ours(j), :], right)
+
+    def finish_up(k):
+        up_core_copy(k).wait_recv()
+
+        @pl.when(k >= 4)
+        def _():
+            up_copy(k - 4).wait_send()
+
+        r.up_tx[lax.rem(k, 4)] = (r.up_mine[lax.rem(k, 2)] + r.up_rx[k].astype(F32)).astype(BF16)
+        up_copy(k).start()
 
     def finish(t):
         j, u, slab, column, columns = parts_of(t)
@@ -949,17 +1090,6 @@
             up_copy(k).wait_recv()
             total[...] = r.up_rx[k].astype(F32)
 
-        @pl.when(jnp.logical_and(is_ffn, slab == 1))
-        def _():
-            up_core_copy(k).wait_recv()
-
-            @pl.when(k >= 4)
-            def _():
-                up_copy(k - 4).wait_send()
-
-            r.up_tx[lax.rem(k, 4)] = (r.up_mine[...] + r.up_rx[k].astype(F32)).astype(BF16)
-            up_copy(k).start()
-
         way = jnp.where(j < place, 1, 0)
 
         @pl.when(jnp.logical_and(place > 0, j >= place))
@@ -974,11 +1104,13 @@
 
         @pl.when(jnp.logical_and(j == place, slab == 0))
         def _():
-            r.main_out[0, :, columns] = total[...]
+            r.main_v[:, columns] = total[...]
+            slab_put(0, column, columns).start()
 
         @pl.when(jnp.logical_and(j == place, slab == 1))
         def _():
-            r.side_out[0, :, columns] = total[...]
+            r.side_v[:, columns] = total[...]
+            slab_put(1, column, columns).start()
 
         @pl.when(j != place)
         def _():
@@ -999,8 +1131,14 @@
     def _():
         proj_first()
 
+    ups = steps // 2
     pl.semaphore_wait(r.core_ready, 1)
     begin(jnp.int32(0))
+
+    @pl.when(is_ffn)
+    def _():
+        begin_up(jnp.int32(0))
+
     neighbours = jnp.where(place > 0, 1, 0) + jnp.where(place < line - 1, 1, 0)
     pl.semaphore_wait(r.line_ready, neighbours)
 
@@ -1009,8 +1147,16 @@
         def _():
             begin(t)
 
+        @pl.when(jnp.logical_and(is_ffn, t < ups))
+        def _():
+            begin_up(t)
+
         finish(t - 1)
 
+        @pl.when(jnp.logical_and(is_ffn, t <= ups))
+        def _():
+            finish_up(t - 1)
+
         @pl.when(jnp.logical_and(s == last, t == 2))
         def _():
             proj_second()
@@ -1026,11 +1172,22 @@
         @pl.when(t == units + 4)
         def _():
             small_second()
+
+        @pl.when(t == steps - units)
+        def _():
+            come_home()
 
         return carry
 
     lax.fori_loop(1, steps + 1, step, 0)
     small_last()
+    for slab in range(2):
+        for column in range(per_slab):
+            slab_put(
+                slab, column, slice(column * step_columns, (column + 1) * step_columns)
+            ).wait()
+    for one in small_puts:
+        one.wait()
 
     def drain(t, carry):
         line_copy(t, 0, 1, 0, place).wait_send()
@@ -1066,25 +1223,35 @@
     smem = pl.BlockSpec(memory_space=pltpu.SMEM)
     anywhere = pl.BlockSpec(memory_space=pl.ANY)
     inputs = dict(
-        hid=(hid, vmem),
+        hid_hbm=(hid, anywhere),
         lengths=(lengths, smem),
         labels=(labels, smem),
-        chosen=(chosen, vmem),
+        chosen_hbm=(chosen, anywhere),
         main_hbm=(main, anywhere),
         side_hbm=(side, anywhere),
-        gain=(gain, vmem),
-        bias=(bias, vmem),
-        buckets=(buckets, vmem),
-        fgain=(fgain, vmem),
-        proj=(proj, vmem),
-        docs=(docs, vmem),
+        gain_hbm=(gain, anywhere),
+        bias_hbm=(bias, anywhere),
+        buckets_hbm=(buckets, anywhere),
+        fgain_hbm=(fgain, anywhere),
+        proj_hbm=(proj, anywhere),
+        docs_hbm=(docs, anywhere),
     )
     outputs = dict(
         units=shape((z.batch_size, z.query_len, z.vector), BF16),
         loss=shape((8, rows), F32),
         dx=shape((z.batch_size, z.query_len, width), F32),
     )
-    scratch = dict(
+    def like(value):
+        return VMEM(value.shape, value.dtype)
+
+    scratch = {name + "_v": like(value) for name, value in outputs.items()}
+    scratch |= dict(
+        chosen=like(chosen),
+        bias=like(bias),
+        buckets=like(buckets),
+        gain=like(gain),
+        fgain=like(fgain),
+        proj=like(proj),
         main=VMEM((width, ff), BF16),
         side=VMEM((width, ff), BF16),
         lent=VMEM((width, ff), BF16),
@@ -1110,7 +1277,9 @@
         unit_rx=VMEM((rows, z.vector), BF16),
         loss_tx=VMEM((sections, 8, rows), F32),
         loss_rx=VMEM((8, rows), F32),
-        load_sem=dma((2,)),
+        small_sem=dma((6,)),
+        load_sem=dma((3,)),
+        put_sem=dma((7,)),
         state_ss=dma((sections + 1,)),
         state_rs=dma((sections,)),
         grad_ss=dma((sections,)),
@@ -1121,8 +1290,9 @@
         idx_rs=dma((sections,)),
         tab_ss=dma((dp_size,)),
         tab_rs=dma((dp_size,)),
-        lend_ss=dma((4, z.parts)),
-        lend_rs=dma((4, z.parts)),
+        tabf_ss=dma((dp_size,)),
+        lend_ss=dma((4, z.parts, 2)),
+        lend_rs=dma((4, z.parts, 2)),
         fin_ss=dma((sections,)),
         fin_rs=dma,
         unit_ss=dma((sections,)),
@@ -1148,8 +1318,14 @@
         )
         scratch |= {name: VMEM(*kind) for name, kind in (factors | partials).items()}
         scratch |= dict(
+            gain_out_v=VMEM((1, share), F32),
+            table_out_v=VMEM((H, 32), F32),
+            fgain_out_v=VMEM((width,), F32),
+            main_v=VMEM((share, ff), F32),
+            side_v=VMEM((share, ff), F32),
+            slab_sem=dma((2, z.per_slab)),
             mine=VMEM((2,) + piece, F32),
-            up_mine=VMEM(piece, F32),
+            up_mine=VMEM((2,) + piece, F32),
             core_tx=VMEM((4,) + piece, BF16),
             up_core_tx=VMEM((4,) + piece, BF16),
             up_tx=VMEM((4,) + piece, BF16),
@@ -1191,7 +1367,7 @@
         functools.partial(relay_kernel, z, (*inputs, *outputs, *scratch)),
         out_shape=tuple(outputs.values()),
         in_specs=[spec for _, spec in inputs.values()],
-        out_specs=(vmem,) * len(outputs),
+        out_specs=tuple(vmem if name in factors or name in partials else anywhere for name in outputs),
         scratch_shapes=list(scratch.values()),
         compiler_params=pltpu.CompilerParams(
             collective_id=0, has_side_effects=True, vmem_limit_bytes=62 * 2**20

time: 209 us -> 201 us (0.962)
  Pallas kernels: 208 us -> 200 us
    pallas_call x1, Pallas kernels: 205 us -> 196 us  [relay(): pl.pallas_call(functools.partial(relay_kernel, z, (*inputs, *outputs, *sc...]
where the time goes in v4:
time: 201 us; the launch traced here: 200 us
  Pallas kernels  200 us (100%)
    pallas_call x1, Pallas kernels, relay(): pl.pallas_call(functools.partial(relay_kernel, z, (*inputs, *outputs, *sc...  196 us

profile of v4, /device:TPU:16, one launch (start us, length us, event | category | flops | bytes accessed | tf_op | source)
XLA Modules:
  0.0 200.4 jit_solution(814292020331791685)
XLA Ops:
  0.6 196.1 %relay.1 = (bf16[4,32,128]{2,1,0:T(8,128)(2,1)}, f32[8,128]{1,0:T(8,128)}, f32[4,32,768]{2,1,0:T(8,128)}, f32[1,96,3072]{2,1,0:T(8,128)}, f32[1,96,3072]{2,1,0:T...) custom-call(bf16[128,768]{1,0:T(8,128)(2,1)} %bitcast.4, s32[4]{0:T(128)} %refs_1_.1, ...), custom_call_target="tpu_custom_call" | custom-call | tf_op jit(solution)/shard_map/relay/pallas_call | solution.py:1366
  196.8 3.6 %deliver.1 = (bf16[4,32,128]{2,1,0:T(8,128)(2,1)}, f32[4,32,768]{2,1,0:T(8,128)}, f32[1,96,3072]{2,1,0:T(8,128)}, f32[1,96,3072]{2,1,0:T(8,128)}, f32[1,96]{1,0:...) custom-call(bf16[4,32,128]{2,1,0:T(8,128)(2,1)} %get-tuple-element.27.refs_0_, ...), custom_call_target="tpu_custom_call" | custom-call | tf_op jit(solution)/shard_map/deliver/pallas_call | solution.py:1390

commit v5 on v4

--- a/solution.py
+++ b/solution.py
@@ -92,6 +92,8 @@
         self.steps = self.line * self.units
         self.chunk = self.share if self.summed else H * 8
         self.slab_chunks = ff // self.chunk
+        self.windows = self.total // self.chunk
+        self.handed = self.summed and sections == 4 and 3 * self.line - 2 <= 3 * self.windows
         arriving = self.steps + 2 * (self.line - 1) * self.units
         self.pool = max(3 * self.slab_chunks, arriving if self.summed else 0)
 
@@ -709,7 +711,9 @@
                 grad_copy(m).start()
 
             loop(both)
-            r.dproj[...] = tn(r.xout[...].reshape(z.total, width), r.final_right[...])
+            r.dproj[...] = tn(r.xout[...].reshape(z.total, width), r.final_right[...]).astype(
+                r.dproj.dtype
+            )
 
         @pl.when(s != last)
         def _():
@@ -873,7 +877,7 @@
                 (r.gain_out_v, r.gain_out),
                 (r.table_out_v, r.table_out),
                 (r.fgain_out_v, r.fgain_out),
-                (r.proj_sum, r.proj_out),
+                (r.proj_v, r.proj_out),
             )
         )
     ]
@@ -885,9 +889,9 @@
         )
 
     def total_of(ref, count):
-        total = ref[0]
+        total = ref[0].astype(F32)
         for k in range(1, count):
-            total = total + ref[k]
+            total = total + ref[k].astype(F32)
         return total
 
     def to_others(body):
@@ -916,7 +920,7 @@
     def proj_second():
         peers(lambda owner: proj_copy(owner, owner).wait_recv())
         peers(lambda owner: fgain_copy(owner, owner).wait_recv())
-        r.proj_sum[piece_rows(d), :] = total_of(r.proj_rx, dp_size)
+        r.proj_sum[piece_rows(d), :] = total_of(r.proj_rx, dp_size).astype(BF16)
         r.fgain_tx[...] = total_of(r.fgain_rx, dp_size)
         r.fgain_sum[...] = r.fgain_tx[...]
         peers(lambda to: spread_copy(to, d).start())
@@ -953,6 +957,7 @@
             proj_across(last).wait_recv()
 
         r.fgain_out_v[...] = r.fgain_sum[...].reshape(width)
+        r.proj_v[...] = r.proj_sum[...].astype(F32)
         for one in small_puts:
             one.start()
         peers(lambda to: gain_copy(to, d).wait_send())
@@ -1005,6 +1010,60 @@
         return copy(
             r.up_tx.at[lax.rem(k, 4)], r.up_rx.at[k], r.up_ss.at[k], r.up_rs.at[k], before, d
         )
+
+    hand_column = per_slab - 1
+    hand_columns = slice(hand_column * step_columns, ff)
+
+    def window(n):
+        row = pl.ds(pl.multiple_of(lax.rem(n, z.windows) * share, share), share)
+        column = pl.ds(pl.multiple_of(n // z.windows * step_columns, step_columns), step_columns)
+        return r.qkv.at[row, column]
+
+    def hand_copy(k):
+        i = k // per_slab
+        return copy(r.up_tx.at[lax.rem(k, 4)], window(i), r.up_ss.at[k], r.hand_rs.at[i], last, d)
+
+    def hand_line(i, way, j, to):
+        slot = way * (line - 1) + j - 1 + way
+        return copy(
+            line_view(steps - units + i),
+            window(line + slot),
+            r.line_ss.at[steps - units + i],
+            r.hand_rs.at[line + slot],
+            s,
+            to * 2 + core,
+        )
+
+    def hand_home():
+        return copy(
+            r.up_mine.at[0], r.side_v.at[:, hand_columns], r.home_ss, r.home_rs, 0, d
+        )
+
+    def extra(i):
+        j = target_of(i)
+        total = r.up_mine.at[0]
+        hand_copy(i * per_slab).wait_recv()
+        total[...] = window(i)[...].astype(F32)
+        way = jnp.where(j < place, 1, 0)
+
+        @pl.when(jnp.logical_and(place > 0, j >= place))
+        def _():
+            hand_line(i, 0, j, place).wait_recv()
+            total[...] += window(line + j - 1)[...].astype(F32)
+
+        @pl.when(jnp.logical_and(place < line - 1, j <= place))
+        def _():
+            hand_line(i, 1, j, place).wait_recv()
+            total[...] += window(line + line - 1 + j)[...].astype(F32)
+
+        @pl.when(j == place)
+        def _():
+            hand_home().start()
+
+        @pl.when(j != place)
+        def _():
+            line_view(steps - units + i)[...] = total[...].astype(BF16)
+            hand_line(i, way, j, place + 1 - 2 * way).start()
 
     def line_view(t):
         row = pl.ds(pl.multiple_of(lax.rem(t, dp_size) * share, share), share)
@@ -1073,9 +1132,28 @@
             up_copy(k - 4).wait_send()
 
         r.up_tx[lax.rem(k, 4)] = (r.up_mine[lax.rem(k, 2)] + r.up_rx[k].astype(F32)).astype(BF16)
-        up_copy(k).start()
+        if z.handed:
+            handed = jnp.logical_and(s == 1, lax.rem(k, per_slab) == hand_column)
+
+            @pl.when(handed)
+            def _():
+                hand_copy(k).start()
+
+            @pl.when(jnp.logical_not(handed))
+            def _():
+                up_copy(k).start()
+        else:
+            up_copy(k).start()
+
+    def gone(t):
+        return jnp.logical_and(s == 0, lax.rem(t, units) == units - 1) if z.handed else False
 
     def finish(t):
+        @pl.when(jnp.logical_not(gone(t)))
+        def _():
+            finish_here(t)
+
+    def finish_here(t):
         j, u, slab, column, columns = parts_of(t)
         k = t // 2
         total = r.mine.at[lax.rem(t, 2)]
@@ -1157,6 +1235,12 @@
         def _():
             finish_up(t - 1)
 
+        if z.handed:
+
+            @pl.when(jnp.logical_and(s == last, jnp.logical_and(t >= 2 * units, t < 2 * units + line)))
+            def _():
+                extra(t - 2 * units)
+
         @pl.when(jnp.logical_and(s == last, t == 2))
         def _():
             proj_second()
@@ -1181,6 +1265,19 @@
 
     lax.fori_loop(1, steps + 1, step, 0)
     small_last()
+    if z.handed:
+
+        @pl.when(s == 0)
+        def _():
+            hand_home().wait_recv()
+            slab_put(1, hand_column, hand_columns).start()
+
+        @pl.when(s == last)
+        def _():
+            hand_home().wait_send()
+            for i in range(line - 1):
+                hand_line(i, 0, 1, place).wait_send()
+
     for slab in range(2):
         for column in range(per_slab):
             slab_put(
@@ -1190,7 +1287,10 @@
         one.wait()
 
     def drain(t, carry):
-        line_copy(t, 0, 1, 0, place).wait_send()
+        @pl.when(jnp.logical_not(gone(t)))
+        def _():
+            line_copy(t, 0, 1, 0, place).wait_send()
+
         return carry
 
     lax.fori_loop(0, steps - units, drain, 0)
@@ -1305,7 +1405,7 @@
         gain_grad=((1, width), F32),
         fgain_grad=((1, width), F32),
         tab_grad=((16, 32), F32),
-        dproj=((width, z.vector), F32),
+        dproj=((width, z.vector), BF16 if z.summed else F32),
     )
     if z.summed:
         outputs |= dict(
@@ -1337,13 +1437,17 @@
             fgain_rx=VMEM((dp_size, 1, width), F32),
             fgain_tx=VMEM((1, width), F32),
             fgain_sum=VMEM((1, width), F32),
-            proj_sum=VMEM((width, z.vector), F32),
-            proj_rx=VMEM((dp_size, share, z.vector), F32),
+            proj_sum=VMEM((width, z.vector), BF16),
+            proj_v=VMEM((width, z.vector), F32),
+            proj_rx=VMEM((dp_size, share, z.vector), BF16),
             core_ss=dma((steps,)),
             core_rs=dma((steps,)),
             up_core_ss=dma((steps // 2,)),
             up_ss=dma((steps // 2,)),
             up_rs=dma((steps // 2,)),
+            hand_rs=dma((3 * z.line - 2,)),
+            home_ss=dma,
+            home_rs=dma,
             line_ss=dma((steps,)),
             line_rs=dma((2, z.line - 1, units)),
             core_ready=pltpu.SemaphoreType.REGULAR,

time: 201 us -> 192 us (0.955)
  Pallas kernels: 200 us -> 191 us
    pallas_call x1, Pallas kernels: 196 us -> 187 us  [relay(): pl.pallas_call(functools.partial(relay_kernel, z, (*inputs, *outputs, *sc...]
where the time goes in v5:
time: 192 us; the launch traced here: 191 us
  Pallas kernels  191 us (99%)
    pallas_call x1, Pallas kernels, relay(): pl.pallas_call(functools.partial(relay_kernel, z, (*inputs, *outputs, *sc...  187 us

profile of v5, /device:TPU:16, one launch (start us, length us, event | category | flops | bytes accessed | tf_op | source)
XLA Modules:
  0.0 191.4 jit_solution(2716233654981040519)
XLA Ops:
  0.6 187.1 %relay.1 = (bf16[4,32,128]{2,1,0:T(8,128)(2,1)}, f32[8,128]{1,0:T(8,128)}, f32[4,32,768]{2,1,0:T(8,128)}, f32[1,96,3072]{2,1,0:T(8,128)}, f32[1,96,3072]{2,1,0:T...) custom-call(bf16[128,768]{1,0:T(8,128)(2,1)} %bitcast.4, s32[4]{0:T(128)} %refs_1_.1, ...), custom_call_target="tpu_custom_call" | custom-call | tf_op jit(solution)/shard_map/relay/pallas_call | solution.py:1470
  187.7 3.6 %deliver.1 = (bf16[4,32,128]{2,1,0:T(8,128)(2,1)}, f32[4,32,768]{2,1,0:T(8,128)}, f32[1,96,3072]{2,1,0:T(8,128)}, f32[1,96,3072]{2,1,0:T(8,128)}, f32[1,96]{1,0:...) custom-call(bf16[4,32,128]{2,1,0:T(8,128)(2,1)} %get-tuple-element.27.refs_0_, ...), custom_call_target="tpu_custom_call" | custom-call | tf_op jit(solution)/shard_map/deliver/pallas_call | solution.py:1494

commit v6 on v5

--- a/solution.py
+++ b/solution.py
@@ -337,9 +337,14 @@
 
     low_half = lax.broadcasted_iota(jnp.int32, (1, 128), 1) < DH
 
-    def half_of(value, upper):
-        keep = jnp.logical_not(low_half) if upper else low_half
-        return jnp.where(keep, value.astype(F32), 0.0).astype(BF16)
+    def split_heads(value):
+        wide = value.astype(F32)
+        return jnp.concatenate(
+            [jnp.where(low_half, wide, 0.0), jnp.where(low_half, 0.0, wide)], axis=0
+        ).astype(BF16)
+
+    def join_heads(value):
+        return jnp.where(low_half, value[:rows], value[rows:]).astype(BF16)
 
     def attention_setup():
         buckets = r.buckets[...]
@@ -347,7 +352,7 @@
             total = jnp.zeros(buckets.shape, F32)
             for b in range(32):
                 total = jnp.where(buckets == b, r.bias[h : h + 1, b : b + 1], total)
-            r.bias_sc[h] = total
+            r.bias_sc[h // 2, h % 2] = total
 
     def attention_table():
         buckets = r.buckets[...]
@@ -355,7 +360,7 @@
         head_row = lax.broadcasted_iota(jnp.int32, (16, 32), 0)
 
         def head(h, carry):
-            grad = r.dbias[h]
+            grad = r.dbias[h // 2, lax.rem(h, 2)]
             rest = jnp.concatenate(
                 [
                     jnp.sum(jnp.where(buckets == b, grad, 0.0), axis=0, keepdims=True)
@@ -394,7 +399,7 @@
             r.qkv[block(m), start : start + head_width] = nn(
                 normed_low, r.main[:, start : start + head_width]
             ).astype(BF16)
-        live = r.meta_rx[m, 0:1, :] > 0.5
+        live = jnp.broadcast_to(r.meta_rx[m, 0:1, :], (rows, rows)).T > 0.5
         row_query = lax.broadcasted_iota(jnp.int32, (rows, rows), 0) // query_len
         column_query = lax.broadcasted_iota(jnp.int32, (rows, rows), 1) // query_len
         keep = jnp.logical_and(row_query == column_query, live)
@@ -403,19 +408,15 @@
             query = r.qkv[block(m), at : at + 128]
             keys = r.qkv[block(m), head_width + at : head_width + at + 128]
             values = r.qkv[block(m), 2 * head_width + at : 2 * head_width + at + 128]
-            contexts = []
-            for upper in (0, 1):
-                h = 2 * pair + upper
-                raw = nt(half_of(query, upper), keys)
-                biased = raw.reshape(batch_size, query_len, rows) + r.bias_sc[h][None]
-                scores = jnp.where(keep, biased.reshape(rows, rows), MASK_FILL)
-                top = jnp.max(scores, axis=-1, keepdims=True)
-                grown = jnp.exp(scores - top)
-                soft = grown / jnp.sum(grown, axis=-1, keepdims=True)
-                r.probs[m, h] = soft
-                contexts.append(nn(soft.astype(BF16), values))
-            r.right[0, block(m), 3 * head_width + at : 3 * head_width + at + 128] = jnp.where(
-                low_half, contexts[0], contexts[1]
+            raw = nt(split_heads(keys), query)
+            biased = raw.reshape(2, batch_size, query_len, rows) + r.bias_sc[pair][:, None]
+            scores = jnp.where(keep[None], biased.reshape(2, rows, rows), MASK_FILL)
+            top = jnp.max(scores, axis=1, keepdims=True)
+            grown = jnp.exp(scores - top)
+            soft = (grown / jnp.sum(grown, axis=1, keepdims=True)).reshape(2 * rows, rows)
+            r.probs[m, pair] = soft
+            r.right[0, block(m), 3 * head_width + at : 3 * head_width + at + 128] = tn(
+                soft.astype(BF16), split_heads(values)
             ).astype(BF16)
         context = r.right[0, block(m), 3 * head_width :]
         return states + nt(context, r.main[:, 3 * head_width :])
@@ -432,27 +433,24 @@
             keys = r.qkv[block(m), head_width + at : head_width + at + 128]
             values = r.qkv[block(m), 2 * head_width + at : 2 * head_width + at + 128]
             grad_pair = grad_context[:, at : at + 128]
-            found = []
-            for upper in (0, 1):
-                h = 2 * pair + upper
-                soft = r.probs[m, h]
-                grad_soft = nt(half_of(grad_pair, upper), values)
-                moved = soft * grad_soft
-                grad_scores = moved - soft * jnp.sum(moved, axis=-1, keepdims=True)
-                r.dbias[h] += jnp.sum(grad_scores.reshape(batch_size, query_len, rows), axis=0)
-                scores_low = grad_scores.astype(BF16)
-                found.append(
-                    (
-                        nn(scores_low, keys),
-                        tn(scores_low, query),
-                        tn(soft.astype(BF16), grad_pair),
-                    )
-                )
+            soft = r.probs[m, pair]
+            grad_soft = nt(split_heads(values), grad_pair)
+            moved = (soft * grad_soft).reshape(2, rows, rows)
+            grad_scores = moved - soft.reshape(2, rows, rows) * jnp.sum(
+                moved, axis=1, keepdims=True
+            )
+            r.dbias[pair] += jnp.sum(
+                grad_scores.reshape(2, batch_size, query_len, rows), axis=1
+            )
+            scores_low = grad_scores.reshape(2 * rows, rows).astype(BF16)
+            found = (
+                tn(scores_low, split_heads(keys)).astype(BF16),
+                join_heads(nn(scores_low, query)),
+                join_heads(nn(soft.astype(BF16), grad_pair)),
+            )
             for third in range(3):
                 start = third * head_width + at
-                r.right[0, block(m), start : start + 128] = jnp.where(
-                    low_half, found[0][third], found[1][third]
-                ).astype(BF16)
+                r.right[0, block(m), start : start + 128] = found[third]
         grad_normed = nn(r.right[0, block(m), : 3 * head_width], turned(0, 0, 3 * head_width))
         grad_states, grad_gain = rms_back(scaled, inverse, gain, grad_normed)
         r.gain_grad[...] += grad_gain
@@ -1369,9 +1367,9 @@
         pool=VMEM((z.pool, z.chunk, width), BF16),
         final_right=VMEM((z.total, z.vector), BF16),
         qkv=VMEM((z.total, 3 * H * DH), BF16),
-        probs=VMEM((sections, H, rows, rows), F32),
-        bias_sc=VMEM((H, z.query_len, rows), F32),
-        dbias=VMEM((H, z.query_len, rows), F32),
+        probs=VMEM((sections, H // 2, 2 * rows, rows), F32),
+        bias_sc=VMEM((H // 2, 2, z.query_len, rows), F32),
+        dbias=VMEM((H // 2, 2, z.query_len, rows), F32),
         fin_rx=VMEM((rows, width), BF16),
         unit_tx=VMEM((sections, rows, z.vector), BF16),
         unit_rx=VMEM((rows, z.vector), BF16),
@@ -1560,7 +1558,7 @@
         out_proj.shape[1],
         doc_vectors.shape[0],
     )
-    buckets = jnp.asarray(np.tile(bucket_table(query_len), (1, batch_size)))
+    buckets = jnp.asarray(np.tile(bucket_table(query_len).T, (1, batch_size)))
     out = relay(
         z,
         hidden_in.reshape(rows, width),

time: 192 us -> 187 us (0.974)
  Pallas kernels: 191 us -> 184 us
    pallas_call x1, Pallas kernels: 187 us -> 180 us  [relay(): pl.pallas_call(functools.partial(relay_kernel, z, (*inputs, *outputs, *sc...]
where the time goes in v6:
time: 187 us; the launch traced here: 185 us
  Pallas kernels  184 us (98%)
    pallas_call x1, Pallas kernels, relay(): pl.pallas_call(functools.partial(relay_kernel, z, (*inputs, *outputs, *sc...  180 us

profile of v6, /device:TPU:16, one launch (start us, length us, event | category | flops | bytes accessed | tf_op | source)
XLA Modules:
  0.0 184.7 jit_solution(14896662957327596124)
XLA Ops:
  0.6 180.4 %relay.1 = (bf16[4,32,128]{2,1,0:T(8,128)(2,1)}, f32[8,128]{1,0:T(8,128)}, f32[4,32,768]{2,1,0:T(8,128)}, f32[1,96,3072]{2,1,0:T(8,128)}, f32[1,96,3072]{2,1,0:T...) custom-call(bf16[128,768]{1,0:T(8,128)(2,1)} %bitcast.4, s32[4]{0:T(128)} %refs_1_.1, ...), custom_call_target="tpu_custom_call" | custom-call | tf_op jit(solution)/shard_map/relay/pallas_call | solution.py:1468
  181.0 3.6 %deliver.1 = (bf16[4,32,128]{2,1,0:T(8,128)(2,1)}, f32[4,32,768]{2,1,0:T(8,128)}, f32[1,96,3072]{2,1,0:T(8,128)}, f32[1,96,3072]{2,1,0:T(8,128)}, f32[1,96]{1,0:...) custom-call(bf16[4,32,128]{2,1,0:T(8,128)(2,1)} %get-tuple-element.27.refs_0_, ...), custom_call_target="tpu_custom_call" | custom-call | tf_op jit(solution)/shard_map/deliver/pallas_call | solution.py:1492

commit v7 on v6

--- a/solution.py
+++ b/solution.py
@@ -24,6 +24,7 @@
 GELU_A = 0.044715
 FF_STEP = 768
 LEND_STEP = 128
+LEND_CUTS = 2
 
 
 def bucket_table(query_len):
@@ -207,7 +208,7 @@
 
     def lend_copy(part, half):
         columns = lend_columns(place, part)
-        depth = slice(half * (width // 2), (half + 1) * (width // 2))
+        depth = slice(half * (width // LEND_CUTS), (half + 1) * (width // LEND_CUTS))
         return copy(
             r.side_hbm.at[0, depth, columns],
             r.lent.at[depth, columns],
@@ -219,7 +220,7 @@
 
     def lend_forward(kind, quarter, part, half, peer):
         columns = lend_columns(quarter, part)
-        depth = slice(half * (width // 2), (half + 1) * (width // 2))
+        depth = slice(half * (width // LEND_CUTS), (half + 1) * (width // LEND_CUTS))
         return copy(
             r.lent.at[depth, columns],
             r.lent.at[depth, columns],
@@ -229,7 +230,7 @@
             peer,
         )
 
-    pieces = [(part, half) for part in range(parts) for half in range(2)]
+    pieces = [(part, half) for part in range(parts) for half in range(LEND_CUTS)]
 
     def state_copy(m):
         return copy(r.xout.at[m], r.xin.at[m], r.state_ss.at[m], r.state_rs.at[m], after, d)
@@ -295,7 +296,7 @@
     @pl.when(is_attention)
     def _():
         for part in range(parts):
-            for half in range(2):
+            for half in range(LEND_CUTS):
                 lend_copy(part, half).start()
 
     other_sections(lambda to: meta_copy(to, s).start())
@@ -337,11 +338,11 @@
 
     low_half = lax.broadcasted_iota(jnp.int32, (1, 128), 1) < DH
 
+    low_lanes = jnp.where(low_half, 1.0, 0.0).astype(BF16)
+    high_lanes = jnp.where(low_half, 0.0, 1.0).astype(BF16)
+
     def split_heads(value):
-        wide = value.astype(F32)
-        return jnp.concatenate(
-            [jnp.where(low_half, wide, 0.0), jnp.where(low_half, 0.0, wide)], axis=0
-        ).astype(BF16)
+        return jnp.concatenate([value * low_lanes, value * high_lanes], axis=0)
 
     def join_heads(value):
         return jnp.where(low_half, value[:rows], value[rows:]).astype(BF16)
@@ -413,13 +414,14 @@
             scores = jnp.where(keep[None], biased.reshape(2, rows, rows), MASK_FILL)
             top = jnp.max(scores, axis=1, keepdims=True)
             grown = jnp.exp(scores - top)
-            soft = (grown / jnp.sum(grown, axis=1, keepdims=True)).reshape(2 * rows, rows)
+            soft = grown * (1.0 / jnp.sum(grown, axis=1, keepdims=True))
+            soft = soft.reshape(2 * rows, rows)
             r.probs[m, pair] = soft
             r.right[0, block(m), 3 * head_width + at : 3 * head_width + at + 128] = tn(
                 soft.astype(BF16), split_heads(values)
             ).astype(BF16)
         context = r.right[0, block(m), 3 * head_width :]
-        return states + nt(context, r.main[:, 3 * head_width :])
+        return states + nn(context, turned(0, 3 * head_width, ff))
 
     def attention_backward(m):
         states, inverse, scaled = load_state(m)
@@ -607,6 +609,8 @@
     def _():
         attention_setup()
         main_load().wait()
+        for start in range(0, ff, FF_STEP):
+            turn(r.main, 0, start)
 
         def forward(m):
             wait_meta(m)
@@ -620,8 +624,6 @@
             state_copy(m).start()
 
         loop(forward)
-        for start in range(0, ff, FF_STEP):
-            turn(r.main, 0, start)
 
         def backward(m):
             grad_copy(m).wait_recv()
@@ -649,7 +651,7 @@
             lend_forward(2, far_place, *piece, far_peer).wait_recv()
             lend_forward(3, far_place, *piece, core_peer).start()
 
-        lag = 2
+        lag = LEND_CUTS
         for k, piece in enumerate(pieces):
             lend_copy(*piece).wait_recv()
             lend_forward(2, place, *piece, far_peer).start()
@@ -688,6 +690,12 @@
             for start in range(0, ff, FF_STEP):
                 turn(r.lent, 2, start)
 
+        def lend_sent():
+            for piece in pieces:
+                lend_forward(1, place, *piece, core_peer).wait_send()
+                lend_forward(2, place, *piece, far_peer).wait_send()
+                lend_forward(3, far_place, *piece, core_peer).wait_send()
+
         @pl.when(s == last)
         def _():
             docs_load().wait()
@@ -700,6 +708,7 @@
             loop(pick_docs)
             turn_lent()
             loop(wait_meta)
+            lend_sent()
 
             def both(m):
                 wait_state(m)
@@ -722,6 +731,8 @@
 
             loop(forward)
             turn_lent()
+            loop(wait_meta)
+            lend_sent()
 
             def backward(m):
                 grad_copy(m).wait_recv()
@@ -729,12 +740,6 @@
                 grad_copy(m).start()
 
             loop(backward)
-            loop(wait_meta)
-
-        for piece in pieces:
-            lend_forward(1, place, *piece, core_peer).wait_send()
-            lend_forward(2, place, *piece, far_peer).wait_send()
-            lend_forward(3, far_place, *piece, core_peer).wait_send()
 
     def put(k, name):
         return pltpu.make_async_copy(getattr(r, name + "_v"), getattr(r, name), r.put_sem.at[k])
@@ -990,7 +995,7 @@
     def parts_of(t):
         i, u = t // units, lax.rem(t, units)
         j = target_of(i)
-        slab, column = lax.rem(u, 2), u // 2
+        slab, column = 1 - lax.rem(u, 2), u // 2
         columns = pl.ds(pl.multiple_of(column * step_columns, step_columns), step_columns)
         return j, u, slab, column, columns
 
@@ -1144,7 +1149,7 @@
             up_copy(k).start()
 
     def gone(t):
-        return jnp.logical_and(s == 0, lax.rem(t, units) == units - 1) if z.handed else False
+        return jnp.logical_and(s == 0, lax.rem(t, units) == units - 2) if z.handed else False
 
     def finish(t):
         @pl.when(jnp.logical_not(gone(t)))
@@ -1294,7 +1299,7 @@
     lax.fori_loop(0, steps - units, drain, 0)
 
     def drain_core(t, carry):
-        slab = lax.rem(t, 2)
+        slab = 1 - lax.rem(t, 2)
 
         @pl.when(jnp.logical_or(is_ffn, slab == 0))
         def _():
@@ -1389,8 +1394,8 @@
         tab_ss=dma((dp_size,)),
         tab_rs=dma((dp_size,)),
         tabf_ss=dma((dp_size,)),
-        lend_ss=dma((4, z.parts, 2)),
-        lend_rs=dma((4, z.parts, 2)),
+        lend_ss=dma((4, z.parts, LEND_CUTS)),
+        lend_rs=dma((4, z.parts, LEND_CUTS)),
         fin_ss=dma((sections,)),
         fin_rs=dma,
         unit_ss=dma((sections,)),

time: 187 us -> 186 us (level)
  no operation moved by 1% of the time
where the time goes in v7:
time: 186 us; the launch traced here: 185 us
  Pallas kernels  184 us (99%)
    pallas_call x1, Pallas kernels, relay(): pl.pallas_call(functools.partial(relay_kernel, z, (*inputs, *outputs, *sc...  181 us

profile of v7, /device:TPU:16, one launch (start us, length us, event | category | flops | bytes accessed | tf_op | source)
XLA Modules:
  0.0 185.2 jit_solution(15778707105956900830)
XLA Ops:
  0.6 180.9 %relay.1 = (bf16[4,32,128]{2,1,0:T(8,128)(2,1)}, f32[8,128]{1,0:T(8,128)}, f32[4,32,768]{2,1,0:T(8,128)}, f32[1,96,3072]{2,1,0:T(8,128)}, f32[1,96,3072]{2,1,0:T...) custom-call(bf16[128,768]{1,0:T(8,128)(2,1)} %bitcast.4, s32[4]{0:T(128)} %refs_1_.1, ...), custom_call_target="tpu_custom_call" | custom-call | tf_op jit(solution)/shard_map/relay/pallas_call | solution.py:1473
  181.5 3.6 %deliver.1 = (bf16[4,32,128]{2,1,0:T(8,128)(2,1)}, f32[4,32,768]{2,1,0:T(8,128)}, f32[1,96,3072]{2,1,0:T(8,128)}, f32[1,96,3072]{2,1,0:T(8,128)}, f32[1,96]{1,0:...) custom-call(bf16[4,32,128]{2,1,0:T(8,128)(2,1)} %get-tuple-element.27.refs_0_, ...), custom_call_target="tpu_custom_call" | custom-call | tf_op jit(solution)/shard_map/deliver/pallas_call | solution.py:1497

commit v8 on v7

--- a/solution.py
+++ b/solution.py
@@ -772,6 +772,39 @@
 
         for one in homes:
             one.start()
+        sent()
+
+    def sent():
+        other_sections(lambda to: meta_copy(to, s).wait_send())
+
+        @pl.when(s != 0)
+        def _():
+            hid_copy(s).wait_send()
+            loop(lambda m: grad_copy(m).wait_send())
+
+        @pl.when(s == 0)
+        def _():
+            for m in range(1, sections):
+                fin_copy(m, m).wait_send()
+
+        @pl.when(is_attention)
+        def _():
+            for piece in pieces:
+                lend_copy(*piece).wait_send()
+
+        @pl.when(s != last)
+        def _():
+            idx_copy(s).wait_send()
+            loop(lambda m: state_copy(m).wait_send())
+
+        @pl.when(s == last)
+        def _():
+            table_near(d).wait_send()
+            far_owners(lambda to: table_copy(to, d).wait_send())
+            far_owners(lambda owner: table_forward(owner).wait_send())
+            for m in range(sections - 1):
+                unit_copy(m, m).wait_send()
+                loss_copy(m, m).wait_send()
 
     if z.summed:
         sum_gradients(
@@ -782,36 +815,6 @@
 
     for one in homes:
         one.wait()
-    other_sections(lambda to: meta_copy(to, s).wait_send())
-
-    @pl.when(s != 0)
-    def _():
-        hid_copy(s).wait_send()
-        loop(lambda m: grad_copy(m).wait_send())
-
-    @pl.when(s == 0)
-    def _():
-        for m in range(1, sections):
-            fin_copy(m, m).wait_send()
-
-    @pl.when(is_attention)
-    def _():
-        for piece in pieces:
-            lend_copy(*piece).wait_send()
-
-    @pl.when(s != last)
-    def _():
-        idx_copy(s).wait_send()
-        loop(lambda m: state_copy(m).wait_send())
-
-    @pl.when(s == last)
-    def _():
-        table_near(d).wait_send()
-        far_owners(lambda to: table_copy(to, d).wait_send())
-        far_owners(lambda owner: table_forward(owner).wait_send())
-        for m in range(sections - 1):
-            unit_copy(m, m).wait_send()
-            loss_copy(m, m).wait_send()
 
 
 def sum_gradients(
@@ -1264,10 +1267,22 @@
         def _():
             come_home()
 
+        @pl.when(t > steps - units)
+        def _():
+            first = (t - 1 - (steps - units)) * (line - 1)
+            for k in range(line - 1):
+
+                @pl.when(jnp.logical_not(gone(first + k)))
+                def _():
+                    line_copy(first + k, 0, 1, 0, place).wait_send()
+
+        @pl.when(t == steps - 2)
+        def _():
+            small_last()
+
         return carry
 
     lax.fori_loop(1, steps + 1, step, 0)
-    small_last()
     if z.handed:
 
         @pl.when(s == 0)
@@ -1288,15 +1303,6 @@
             ).wait()
     for one in small_puts:
         one.wait()
-
-    def drain(t, carry):
-        @pl.when(jnp.logical_not(gone(t)))
-        def _():
-            line_copy(t, 0, 1, 0, place).wait_send()
-
-        return carry
-
-    lax.fori_loop(0, steps - units, drain, 0)
 
     def drain_core(t, carry):
         slab = 1 - lax.rem(t, 2)

time: 186 us -> 186 us (level)
  no operation moved by 1% of the time
where the time goes in v8:
time: 186 us; the launch traced here: 185 us
  Pallas kernels  184 us (99%)
    pallas_call x1, Pallas kernels, relay(): pl.pallas_call(functools.partial(relay_kernel, z, (*inputs, *outputs, *sc...  180 us

profile of v8, /device:TPU:16, one launch (start us, length us, event | category | flops | bytes accessed | tf_op | source)
XLA Modules:
  0.0 184.8 jit_solution(17051712624817966499)
XLA Ops:
  0.6 180.4 %relay.1 = (bf16[4,32,128]{2,1,0:T(8,128)(2,1)}, f32[8,128]{1,0:T(8,128)}, f32[4,32,768]{2,1,0:T(8,128)}, f32[1,96,3072]{2,1,0:T(8,128)}, f32[1,96,3072]{2,1,0:T...) custom-call(bf16[128,768]{1,0:T(8,128)(2,1)} %bitcast.4, s32[4]{0:T(128)} %refs_1_.1, ...), custom_call_target="tpu_custom_call" | custom-call | tf_op jit(solution)/shard_map/relay/pallas_call | solution.py:1479
  181.1 3.6 %deliver.1 = (bf16[4,32,128]{2,1,0:T(8,128)(2,1)}, f32[4,32,768]{2,1,0:T(8,128)}, f32[1,96,3072]{2,1,0:T(8,128)}, f32[1,96,3072]{2,1,0:T(8,128)}, f32[1,96]{1,0:...) custom-call(bf16[4,32,128]{2,1,0:T(8,128)(2,1)} %get-tuple-element.27.refs_0_, ...), custom_call_target="tpu_custom_call" | custom-call | tf_op jit(solution)/shard_map/deliver/pallas_call | solution.py:1503
